TPU v7x, 512 devices: a whole 4x8x8 slice. The times are simulated.
512 devices in a mesh: dp: 64 (over x, z, core), mp: 8 (over y).
Axes of the slice: x: 4, y: 8, z: 8, core: 2. Of those that a mesh axis runs over, the one named last changes fastest.
Arguments:
- activations: bfloat16 [65536, 12288], P('dp', 'mp'), may hold values from -40 to 40
- output_grads: bfloat16 [65536, 512], P('dp', 'mp'), may hold values from -2.5 to 2.5
- master: float32 [512, 12288], P('mp', 'dp'), may hold values from -0.12 to 0.12
- moment_q: bfloat16 [512, 12288], P('mp', 'dp'), may hold values from -1 to 1
- moment_range: float32 [1], replicated, may hold values from 0.01 to 0.05
- second_moment: float32 [512, 12288], P('mp', 'dp'), may hold values from 0.0001 to 0.03
Outputs:
- master_new: float32 [512, 12288], P('mp', 'dp')
- moment_q_new: bfloat16 [512, 12288], P('mp', 'dp')
- moment_range_new: float32 [1], replicated
- second_new: float32 [512, 12288], P('mp', 'dp')
- weight_q: bfloat16 [512, 12288], P('mp')
- weight_range: float32 [1], replicated
- grad_range: float32 [1], replicated
All inputs are finite; a program needn't handle non-finite values. Where the computation divides by a largest or mean magnitude, that divisor is 1e-20 or more.
Results may differ from a plain program's by a relative error of at most 0.0051.
Values may be sent and summed in bfloat16 or wider, within the bound.
No kernel may reach another device: no remote copies, remote signals or barrier semaphores. Data moves between devices by JAX's collectives and lax.ppermute only.
A program may use at most 64 MiB of HBM per device.

v0:
```python
import jax
import jax.numpy as jnp
from jax import lax
from jax.sharding import PartitionSpec as P

EPSILON = 1e-06
BETA_ONE = 0.9
BETA_TWO = 0.999
LEARN_RATE = 0.001
DECAY_RATE = 0.1
ADAM_EPSILON = 1e-08


def on_device(activations, output_grads, master, moment_q, moment_range, second_moment):
    dp_count = lax.axis_size("dp")
    gathered = lax.all_gather(output_grads, "mp", axis=1, tiled=True)
    partial_value = lax.dot_general(
        gathered, activations, (((0,), (0,)), ((), ())), preferred_element_type=jnp.float32
    )
    grad_range = lax.pmax(jnp.max(jnp.abs(partial_value)), ("dp", "mp")) + EPSILON
    quantized = (partial_value / grad_range).astype(jnp.bfloat16)
    quantized = lax.all_to_all(quantized, "mp", split_axis=0, concat_axis=1, tiled=True)
    summed = lax.psum_scatter(quantized.astype(jnp.float32), "dp", scatter_dimension=1, tiled=True)
    gradient = summed * grad_range / dp_count
    moment = (
        BETA_ONE * (moment_q.astype(jnp.float32) * moment_range[0]) + (1.0 - BETA_ONE) * gradient
    )
    second_new = BETA_TWO * second_moment + (1.0 - BETA_TWO) * gradient * gradient
    master_new = master - LEARN_RATE * (
        moment / (jnp.sqrt(second_new) + ADAM_EPSILON) + DECAY_RATE * master
    )
    moment_largest, weight_largest = lax.pmax(
        (jnp.max(jnp.abs(moment)), jnp.max(jnp.abs(master_new))), ("dp", "mp")
    )
    moment_span = moment_largest + EPSILON
    weight_span = weight_largest + EPSILON
    moment_q_new = (moment / moment_span).astype(jnp.bfloat16)
    weight_local = (master_new / weight_span).astype(jnp.bfloat16)
    weight_q = lax.all_gather(weight_local, "dp", axis=1, tiled=True)
    return (
        master_new,
        moment_q_new,
        jnp.reshape(moment_span, (1,)),
        second_new,
        weight_q,
        jnp.reshape(weight_span, (1,)),
        jnp.reshape(grad_range, (1,)),
    )


def solution(mesh):
    placed = (P("dp", "mp"), P("dp", "mp"), P("mp", "dp"), P("mp", "dp"), P(), P("mp", "dp"))
    return jax.shard_map(
        on_device,
        mesh=mesh,
        in_specs=placed,
        out_specs=(P("mp", "dp"), P("mp", "dp"), P(), P("mp", "dp"), P("mp", None), P(), P()),
        check_vma=False,
    )
```

profile of v0, /device:TPU:1, one launch (start us, length us, event | category | flops | bytes accessed | tf_op | source)
XLA Modules:
  0.0 562.6 jit_solution(2169242761006490564)
XLA Ops:
  7.2 0.0 copy-start
  7.2 0.0 all-gather.4.cloned.1.call-start
  7.2 0.7 all-gather.4.cloned.1.call-update
  7.9 0.0 reduce-scatter.4.cloned.1.call-start
  8.0 43.8 %all-gather.4.cloned.1.call-done = bf16[1024,512]{0,1:T(8,128)(2,1)} async-done(((bf16[1024,64]{0,1:T(8,128)(2,1)}), bf16[1024,512]{0,1:T(8,128)(2,1)}) %all-gather.4.cloned.1.call-update) | async-done | bytes 1048592 | tf_op jit(solution)/shard_map/all_gather | solution.py:16
  51.8 0.0 copy-done
  51.8 5.3 abs_reduce_fusion
  57.0 102.4 %pmax.21 = f32[]{:T(128)} all-reduce(f32[]{:T(128)} %get-tuple-element.13), channel_id=1, replica_groups=mesh['dp'=64,'mp'=8] {'dp','mp'}, use_global_device_ids=true, to_apply=%region_1.0 | all-reduce | flops 1 | bytes 8 | tf_op jit(solution)/shard_map/pmax | solution.py:20
  160.1 2.2 divide_convert_fusion
  162.3 43.4 %all_to_all.13 = bf16[8,64,1536]{2,1,0:T(8,128)(2,1)S(1)} all-to-all(bf16[8,64,1536]{2,1,0:T(8,128)(2,1)S(1)} %bitcast.23), channel_id=1, replica_groups=mesh['dp'=64,'mp'=8] {'mp'}, dimensions={0} | all-to-all | bytes 3145728 | tf_op jit(solution)/shard_map/all_to_all | solution.py:22
  205.7 2.1 convert_bitcast_fusion
  207.8 5.7 %copy.20 = f32[64,8,1536]{0,2,1:T(8,128)} copy(f32[64,8,1536]{2,0,1:T(8,128)} %convert_bitcast_fusion) | data formatting | bytes 6291456
  213.6 0.0 copy-start.2
  213.6 0.0 copy-start.3
  213.6 0.0 copy-start.4
  213.6 0.0 reduce-scatter.4.cloned.1.call-update
  213.6 0.0 all-gather.6.cloned.1.call-start
  214.3 145.0 %reduce-scatter.4.cloned.1.call-done = f32[192,64]{1,0:T(8,128)} async-done(((f32[12288,64]{1,0:T(8,128)}), f32[192,64]{1,0:T(8,128)}) %reduce-scatter.4.cloned.1.call-update) | async-done | bytes 49168
  359.3 1.0 copy.19
  360.3 0.0 copy-done.2
  360.3 0.0 copy-done.3
  360.3 0.0 copy-done.4
  360.3 1.3 abs_reduce_fusion.1
  361.6 0.0 copy-start.1
  361.6 100.7 %all-reduce = (f32[]{:T(128)}, f32[]{:T(128)}) all-reduce(f32[]{:T(128)} %get-tuple-element.12, f32[]{:T(128)} %get-tuple-element.9), channel_id=1, replica_groups=mesh['dp'=64,'mp'=8] {'dp','mp'}, use_global_device_ids=true, to_apply=%region_4.0 | all-reduce | flops 2 | bytes 16 | tf_op jit(solution)/shard_map/pmax | solution.py:32
  462.9 0.6 fusion
  463.6 0.0 all-gather.6.cloned.1.call-update
  464.2 0.6 divide_convert_fusion.2
  464.9 79.3 %all-gather.6.cloned.1.call-done = bf16[64,192,64]{1,2,0:T(8,128)(2,1)} async-done(((bf16[1,192,64]{1,2,0:T(8,128)(2,1)}), bf16[64,192,64]{1,2,0:T(8,128)(2,1)}) %all-gather.6.cloned.1.call-update) | async-done | bytes 1572880 | tf_op jit(solution)/shard_map/all_gather | solution.py:39
  544.2 4.1 copy.17
  548.2 4.5 reshape.33
  552.7 0.0 copy-done.1
Async XLA Ops:
  7.2 44.6 %copy-start = (bf16[1024,1536]{1,0:T(8,128)(2,1)S(1)}, bf16[1024,1536]{1,0:T(8,128)(2,1)}, u32[]{:S(2)}) copy-start(bf16[1024,1536]{1,0:T(8,128)(2,1)} %param.6) | copy-start | bytes 9437188
  7.2 44.6 %all-gather.4.cloned.1.call-start = ((), (), s32[]{:S(2)}) async-start(), calls=%async_computation.2 | async-start | bytes 1179648 | tf_op jit(solution)/shard_map/all_gather | solution.py:16
  7.9 351.4 %reduce-scatter.4.cloned.1.call-start = ((), (), s32[]{:S(2)}) async-start(), calls=%async_computation.4 | async-start | bytes 6389760
  213.6 146.7 %copy-start.2 = (bf16[64,192]{1,0:T(8,128)(2,1)S(1)}, bf16[64,192]{1,0:T(8,128)(2,1)}, u32[]{:S(2)}) copy-start(bf16[64,192]{1,0:T(8,128)(2,1)} %param.9) | copy-start | bytes 73732
  213.6 146.7 %copy-start.3 = (f32[64,192]{1,0:T(8,128)S(1)}, f32[64,192]{1,0:T(8,128)}, u32[]{:S(2)}) copy-start(f32[64,192]{1,0:T(8,128)} %param.8) | copy-start | bytes 147460
  213.6 146.8 %copy-start.4 = (f32[64,192]{1,0:T(8,128)S(1)}, f32[64,192]{1,0:T(8,128)}, u32[]{:S(2)}) copy-start(f32[64,192]{1,0:T(8,128)} %param.11) | copy-start | bytes 147460
  213.6 330.6 %all-gather.6.cloned.1.call-start = ((), (), s32[]{:S(2)}) async-start(), calls=%async_computation.3 | async-start | bytes 2129920 | tf_op jit(solution)/shard_map/all_gather | solution.py:39
  361.6 191.1 %copy-start.1 = (f32[64,192]{1,0:T(8,128)}, f32[64,192]{1,0:T(8,128)S(1)}, u32[]{:S(2)}) copy-start(f32[64,192]{1,0:T(8,128)S(1)} %get-tuple-element.10) | copy-start | bytes 147460
Sparse Core Ops, SparseCore 0:
  10.1 41.6 all-gather.3
  213.7 145.5 reduce-scatter.3
  463.7 80.4 all-gather.5
where the time goes:
time: 563 us
  waiting for transfers between devices  269 us (48%)
  blocking collectives  246 us (44%)
  between operations  19.8 us (4%)
  local copies, waits for them, and re-layouts  15.2 us (3%)
  other arithmetic  6.87 us (1%)
    unnamed x4, waiting for transfers between devices  146 us
    pmax x1, blocking collectives, on_device(): lax.pmax(jnp.max(jnp.abs(partial_value)), ('dp', 'mp')) + EPSILON  102 us
    pmax x1, blocking collectives, on_device(): lax.pmax((jnp.max(jnp.abs(moment)), jnp.max(jnp.abs(master_new))), ('dp',...  101 us
    all_gather x1, waiting for transfers between devices, on_device(): weight_q = lax.all_gather(weight_local, 'dp', axis=1, tiled=True)  79.3 us
    all_gather x1, waiting for transfers between devices, on_device(): gathered = lax.all_gather(output_grads, 'mp', axis=1, tiled=True)  43.8 us
    all_to_all x1, blocking collectives, on_device(): lax.all_to_all(quantized, 'mp', split_axis=0, concat_axis=1, tiled=True)  43.4 us
  transfers between devices with their start and end apart: 3, of which 3 were waited for; matrix products, arithmetic and copies ran while one was open for 0% of the time, Pallas kernels for 0%

commit v1 on v0

v1 whole, which is shorter than its diff:
```python
import functools

import jax
import jax.numpy as jnp
from jax import lax
from jax.experimental import pallas as pl
from jax.experimental.pallas import tpu as pltpu
from jax.sharding import Mesh, PartitionSpec as P

EPSILON = 1e-06
BETA_ONE = 0.9
BETA_TWO = 0.999
LEARN_RATE = 0.001
DECAY_RATE = 0.1
ADAM_EPSILON = 1e-08

F32 = jnp.float32
BF16 = jnp.bfloat16
LANES = 128
MAX_ROWS = 16
DEVICE = ("x", "z", "core", "y")


def pack(block):
    half = block.shape[0] // 2
    tail = block[:, LANES:]
    return jnp.concatenate([block[:, :LANES], jnp.concatenate([tail[:half], tail[half:]], 1)], 0)


def unpack(packed, rows):
    tail = packed[rows:]
    tail = jnp.concatenate([tail[:, : LANES // 2], tail[:, LANES // 2 :]], 0)
    return jnp.concatenate([packed[:rows], tail], 1)


def add_and_cut(parts_ref, out_ref):
    total = parts_ref[0].astype(F32)
    for part in range(1, parts_ref.shape[0]):
        total += parts_ref[part].astype(F32)
    width = total.shape[1] // out_ref.shape[0]
    for piece in range(out_ref.shape[0]):
        out_ref[piece] = pack(total[:, piece * width : (piece + 1) * width]).astype(BF16)


def largest(value):
    return jnp.max(jnp.max(jnp.abs(value), axis=1, keepdims=True), axis=0, keepdims=True)


def adam_step(
    devices, summed_ref, partial_ref, range_ref, master_ref, moment_ref, second_ref,
    master_out, second_out, moment_out, sent_out,
):
    rows = master_ref.shape[0]
    gradient = unpack(summed_ref[...], rows) / devices
    moment = (
        BETA_ONE * (moment_ref[...].astype(F32) * range_ref[0]) + (1.0 - BETA_ONE) * gradient
    )
    second_new = BETA_TWO * second_ref[...] + (1.0 - BETA_TWO) * gradient * gradient
    master = master_ref[...]
    master_new = master - LEARN_RATE * (
        moment / (jnp.sqrt(second_new) + ADAM_EPSILON) + DECAY_RATE * master
    )
    master_out[...] = master_new
    second_out[...] = second_new
    moment_out[...] = moment
    packed = pack(master_new)
    sent_out[: packed.shape[0]] = packed.astype(BF16)
    row = lax.broadcasted_iota(jnp.int32, (MAX_ROWS, LANES), 0)
    spread = jnp.zeros((MAX_ROWS, LANES), F32)
    tops = (jnp.full((1, 1), partial_ref[0], F32), largest(moment), largest(master_new))
    for place, top in enumerate(tops):
        rest = jnp.broadcast_to(top, (MAX_ROWS, LANES))
        for piece in range(3):
            rounded = rest.astype(BF16).astype(F32)
            spread = jnp.where(row == 3 * place + piece, rounded, spread)
            rest = rest - rounded
    sent_out[packed.shape[0] :] = spread.astype(BF16)


def find_tops(own_ref, other_ref, out_ref):
    held = jnp.concatenate([own_ref[...], other_ref[...]], 0).astype(F32)
    best = [None] * 3
    for block in range(held.shape[0]):
        for place in range(3):
            row = 3 * place
            top = held[block, row : row + 1] + held[block, row + 1 : row + 2] + held[block, row + 2 : row + 3]
            best[place] = top if best[place] is None else jnp.maximum(best[place], top)
    out_ref[...] = jnp.concatenate(best + [jnp.zeros((5, LANES), F32)], 0)


def scale_weights(core_ref, spans_ref, own_ref, other_ref, moment_ref, weight_out, moment_out):
    rows = weight_out.shape[0]
    is_first = core_ref[0] == 0
    span = spans_ref[2]

    @pl.when(pl.program_id(0) == 0)
    def _():
        moment_out[...] = (moment_ref[...] / spans_ref[1]).astype(BF16)

    used = rows + rows // 2
    for place in range(own_ref.shape[1]):
        own = own_ref[0, place, :used].astype(F32)
        other = other_ref[0, place, :used].astype(F32)
        first = unpack(jnp.where(is_first, own, other), rows)
        second = unpack(jnp.where(is_first, other, own), rows)
        pair = jnp.concatenate([first, second], 1) / span
        width = pair.shape[1]
        weight_out[:, place * width : (place + 1) * width] = pair.astype(BF16)


def copies_to_all(value, axis):
    copies = jnp.broadcast_to(value[None], (lax.axis_size(axis), *value.shape))
    return lax.all_to_all(copies, axis, 0, 0, tiled=True)


def on_device(activations, output_grads, master, moment_q, moment_range, second_moment):
    xs, zs, cores, ys = (lax.axis_size(name) for name in DEVICE)
    rows, width = master.shape
    packed_rows = rows + rows // 2
    sent_rows = packed_rows + MAX_ROWS
    smem = pl.BlockSpec(memory_space=pltpu.SMEM)
    vmem = pl.BlockSpec(memory_space=pltpu.VMEM)

    gathered = copies_to_all(output_grads.T, "y").reshape(-1, output_grads.shape[0])
    partial_value = jnp.dot(gathered, activations, preferred_element_type=F32)
    partial_top = jnp.max(jnp.abs(partial_value))

    value = partial_value.astype(BF16).reshape(cores, -1, partial_value.shape[1])
    value = lax.all_to_all(value, "core", 0, 0, tiled=True)
    value = jnp.sum(value.astype(F32), axis=0).astype(BF16)
    value = lax.all_to_all(value.reshape(xs, rows, -1), "x", 0, 0, tiled=True)
    value = pl.pallas_call(
        add_and_cut,
        out_shape=jax.ShapeDtypeStruct((zs, packed_rows, LANES), BF16),
        in_specs=[vmem],
        out_specs=vmem,
    )(value)
    value = lax.all_to_all(value, "z", 0, 0, tiled=True)
    value = jnp.sum(value.astype(F32), axis=0)
    route = []
    for x in range(xs):
        for z in range(zs):
            for core in range(cores):
                for y in range(ys):
                    source = ((x * zs + z) * cores + core) * ys + y
                    route.append((source, (y * zs + z) * ys + core * xs + x))
    value = lax.ppermute(value, DEVICE, route)

    block = jax.ShapeDtypeStruct((rows, width), F32)
    master_new, second_new, moment, sent = pl.pallas_call(
        functools.partial(adam_step, xs * zs * cores),
        out_shape=(block, block, block, jax.ShapeDtypeStruct((sent_rows, LANES), BF16)),
        in_specs=[vmem, smem, smem, vmem, vmem, vmem],
        out_specs=(vmem,) * 4,
    )(value, partial_top.reshape(1), moment_range, master, moment_q, second_moment)

    held = copies_to_all(sent, "z")
    held = copies_to_all(held, "x").reshape(xs, zs, sent_rows, LANES)
    other = lax.ppermute(held, "core", [(0, 1), (1, 0)])
    tops = pl.pallas_call(
        find_tops,
        out_shape=jax.ShapeDtypeStruct((8, LANES), F32),
        in_specs=[vmem, vmem],
        out_specs=vmem,
    )(
        held[:, :, packed_rows:].reshape(xs * zs, MAX_ROWS, LANES),
        other[:, :, packed_rows:].reshape(xs * zs, MAX_ROWS, LANES),
    )
    spans = lax.pmax(tops[:3, 0], "y") + EPSILON

    group = (1, zs, sent_rows, LANES)
    weight_q, moment_q_new = pl.pallas_call(
        scale_weights,
        grid=(xs,),
        out_shape=(
            jax.ShapeDtypeStruct((rows, width * xs * zs * cores), BF16),
            jax.ShapeDtypeStruct((rows, width), BF16),
        ),
        in_specs=[
            smem,
            smem,
            pl.BlockSpec(group, lambda i: (i, 0, 0, 0)),
            pl.BlockSpec(group, lambda i: (i, 0, 0, 0)),
            pl.BlockSpec((rows, width), lambda i: (0, 0)),
        ],
        out_specs=(
            pl.BlockSpec((rows, width * zs * cores), lambda i: (0, i)),
            pl.BlockSpec((rows, width), lambda i: (0, 0)),
        ),
    )(lax.axis_index("core").reshape(1), spans, held, other, moment)
    return (
        master_new,
        moment_q_new,
        spans[1:2],
        second_new,
        weight_q,
        spans[2:3],
        spans[0:1],
    )


def solution(mesh):
    inner = Mesh(mesh.devices.reshape(4, 8, 2, 8), DEVICE)
    dp, mp = ("x", "z", "core"), "y"
    placed = (P(dp, mp), P(dp, mp), P(mp, dp), P(mp, dp), P(), P(mp, dp))
    return jax.shard_map(
        on_device,
        mesh=inner,
        in_specs=placed,
        out_specs=(P(mp, dp), P(mp, dp), P(), P(mp, dp), P(mp, None), P(), P()),
        check_vma=False,
    )
```

time: 563 us -> 162 us (0.29)
  waiting for transfers between devices: 269 us -> 1.96 us
  blocking collectives: 246 us -> 122 us
  between operations: 19.8 us -> 1.33 us
  starting transfers between devices: 0.12 us -> 11.7 us
  Pallas kernels: 0 us -> 10.2 us
  local copies, waits for them, and re-layouts: 15.2 us -> 7.22 us
    pmax x2 -> x1, blocking collectives: 203 us -> 11.7 us  [on_device(): spans = lax.pmax(tops[:3, 0], 'y') + EPSILON]
    unnamed x4 -> x0, waiting for transfers between devices: 146 us -> none
    all_gather x2 -> x0, waiting for transfers between devices: 123 us -> none  [the longest x1 79.3 us: on_device(): weight_q = lax.all_gather(weight_local, 'dp', axis=1, tiled=True)]
    all_to_all x1 -> x6, blocking collectives: 43.4 us -> 110 us  [the longest x3 66.2 us: copies_to_all(): return lax.all_to_all(copies, axis, 0, 0, tiled=True)]
    ppermute x0 -> x2, starting transfers between devices: none -> 11.7 us  [the longest x1 6.79 us: on_device(): other = lax.ppermute(held, 'core', [(0, 1), (1, 0)])]
    unnamed x13 -> x6, local copies, waits for them, and re-layouts: 11.2 us -> 0.63 us
    pallas_call x0 -> x4, Pallas kernels: none -> 10.2 us  [the longest x1 4.11 us: on_device(): pl.pallas_call(scale_weights, grid=(xs,), out_shape=(jax.ShapeDtypeStruct...]
  transfers between devices with their start and end apart: 3 -> 2, of which waited for: 3 -> 2; matrix products, arithmetic and copies ran while one was open for 0% -> 1% of each run, Pallas kernels for 0% -> 0%
where the time goes in v1:
time: 162 us; the launch traced here: 159 us
  blocking collectives  122 us (75%)
  starting transfers between devices  11.7 us (7%)
  Pallas kernels  10.2 us (6%)
  local copies, waits for them, and re-layouts  7.22 us (4%)
  other arithmetic  2.8 us (2%)
  matrix products  2.42 us (1%)
  waiting for transfers between devices  1.96 us (1%)
    all_to_all x3, blocking collectives, copies_to_all(): return lax.all_to_all(copies, axis, 0, 0, tiled=True)  66.2 us
    all_to_all x1, blocking collectives, on_device(): value = lax.all_to_all(value, 'z', 0, 0, tiled=True)  18.6 us
    all_to_all x1, blocking collectives, on_device(): value = lax.all_to_all(value.reshape(xs, rows, -1), 'x', 0, 0, tiled=True)  16.1 us
    pmax x1, blocking collectives, on_device(): spans = lax.pmax(tops[:3, 0], 'y') + EPSILON  11.7 us
    all_to_all x1, blocking collectives, on_device(): value = lax.all_to_all(value, 'core', 0, 0, tiled=True)  9.17 us
    ppermute x1, starting transfers between devices, on_device(): other = lax.ppermute(held, 'core', [(0, 1), (1, 0)])  6.79 us
    ppermute x1, starting transfers between devices, on_device(): value = lax.ppermute(value, DEVICE, route)  4.94 us
    pallas_call x1, Pallas kernels, on_device(): pl.pallas_call(scale_weights, grid=(xs,), out_shape=(jax.ShapeDtypeStruct...  4.11 us
  transfers between devices with their start and end apart: 2, of which 2 were waited for; matrix products, arithmetic and copies ran while one was open for 1% of the time, Pallas kernels for 0%

profile of v1, /device:TPU:1, one launch (start us, length us, event | category | flops | bytes accessed | tf_op | source)
XLA Modules:
  0.0 159.4 jit_solution(1882465623876104485)
XLA Ops:
  0.6 0.0 copy-start
  0.6 1.2 broadcast_in_dim.6
  1.8 33.4 %all_to_all.30 = bf16[8,64,1024]{2,1,0:T(8,128)(2,1)S(1)} all-to-all(bf16[8,64,1024]{2,1,0:T(8,128)(2,1)S(1)} %broadcast_in_dim.6), channel_id=1, replica_groups=mesh['x'=4,'z'=8,'core'=2,'y'=8] {'y'}, dimensions={0} | all-to-all | bytes 2097152 | tf_op jit(solution)/shard_map/all_to_all | solution.py:113
  35.2 0.0 copy-done
  35.2 2.4 %abs_reduce_fusion = (f32[]{:T(128)}, bf16[512,1536]{1,0:T(8,128)(2,1)S(1)}) fusion(bf16[512,1024]{1,0:T(8,128)(2,1)S(1)} %bitcast.12, bf16[1024,1536]{1,0:T(8,128)(2,1)S(1)} %copy-done), kind=kOutput, calls=%fused_computation | convolution fusion | flops 1612972032 | bytes 5767172 | tf_op jit(solution)/shard_map/dot_general | solution.py:125
  37.7 9.2 %all_to_all.31 = bf16[2,256,1536]{2,1,0:T(8,128)(2,1)} all-to-all(bf16[2,256,1536]{2,1,0:T(8,128)(2,1)S(1)} %bitcast.11), channel_id=1, replica_groups=mesh['x'=4,'z'=8,'core'=2,'y'=8] {'core'}, dimensions={0} | all-to-all | bytes 3145728 | tf_op jit(solution)/shard_map/all_to_all | solution.py:129
  46.8 2.8 %reduce_sum.21 = bf16[256,1536]{1,0:T(8,128)(2,1)} reduce(bf16[2,256,1536]{2,1,0:T(8,128)(2,1)} %all_to_all.31, bf16[]{:T(256)} %constant.3.clone.1), dimensions={0}, to_apply=%region_0.0 | reduce | flops 393216 | bytes 2359298 | tf_op jit(solution)/shard_map/reduce_sum | solution.py:130
  49.6 16.1 %all_to_all.32.parts_ref = bf16[4,64,1536]{2,1,0:T(8,128)(2,1)} all-to-all(bf16[4,64,1536]{2,1,0:T(8,128)(2,1)} %bitcast.10), channel_id=1, replica_groups=mesh['x'=4,'z'=8,'core'=2,'y'=8] {'x'}, dimensions={0} | all-to-all | bytes 1572864 | tf_op jit(solution)/shard_map/all_to_all | solution.py:131
  65.7 2.0 %shard_map.117 = bf16[8,96,128]{2,1,0:T(8,128)(2,1)} custom-call(bf16[4,64,1536]{2,1,0:T(8,128)(2,1)} %all_to_all.32.parts_ref), custom_call_target="tpu_custom_call" | custom-call | tf_op jit(solution)/shard_map/pallas_call | solution.py:132
  67.7 18.6 %all_to_all.33 = bf16[8,96,128]{2,1,0:T(8,128)(2,1)S(1)} all-to-all(bf16[8,96,128]{2,1,0:T(8,128)(2,1)} %shard_map.117), channel_id=1, replica_groups=mesh['x'=4,'z'=8,'core'=2,'y'=8] {'z'}, dimensions={0} | all-to-all | bytes 393216 | tf_op jit(solution)/shard_map/all_to_all | solution.py:138
  86.4 4.9 %collective-permute-start = (f32[96,128]{1,0:T(8,128)S(1)}, f32[96,128]{1,0:T(8,128)S(1)}, u32[]{:S(2)}, u32[]{:S(2)}) collective-permute-start(f32[96,128]{1,0:T(8,128)S(1)} %convert_reduce_fusion), channel_id=1, source_target_pairs={{0,0},{1,64},{2,128},{3,192},{4,256},{5,320},{6,384},{7,448},{8,4}... | collective-permute-start | bytes 147464 | tf_op jit(solution)/shard_map/ppermute | solution.py:147
  92.0 1.1 collective-permute-done.summed_ref
  93.1 0.0 copy-start.1
  93.1 0.6 copy-done.1
  93.7 2.4 %shard_map.118 = (f32[64,192]{1,0:T(8,128)}, f32[64,192]{1,0:T(8,128)}, f32[64,192]{1,0:T(8,128)}, bf16[112,128]{1,0:T(8,128)(2,1)}) custom-call(f32[96,128]{1,0:T(8,128)} %copy-done.1, f32[1]{0:T(128)} %bitcast.4.partial_ref, f32[1]{0:T(128)S(6)} %copy.13.range_ref, f32[64,192]{1,0:T(8,128)} %master_ref.1, bf16[64,192]{1,0:T(8,128)(2,1)} %moment_ref.1, ...), custom_call_target="tpu_custom_call" | custom-call | tf_op jit(solution)/shard_map/pallas_call | solution.py:150
  96.1 0.8 broadcast_in_dim.7
  96.9 14.7 %all_to_all.34 = bf16[8,112,128]{2,1,0:T(8,128)(2,1)S(1)} all-to-all(bf16[8,112,128]{2,1,0:T(8,128)(2,1)S(1)} %broadcast_in_dim.7), channel_id=1, replica_groups=mesh['x'=4,'z'=8,'core'=2,'y'=8] {'z'}, dimensions={0} | all-to-all | bytes 458752 | tf_op jit(solution)/shard_map/all_to_all | solution.py:113
  111.5 0.1 broadcast_in_dim.8
  111.7 18.2 %all_to_all.35.own_ref = bf16[4,8,112,128]{3,2,1,0:T(8,128)(2,1)} all-to-all(bf16[4,8,112,128]{3,2,1,0:T(8,128)(2,1)S(1)} %broadcast_in_dim.8), channel_id=1, replica_groups=mesh['x'=4,'z'=8,'core'=2,'y'=8] {'x'}, dimensions={0} | all-to-all | bytes 1835008 | tf_op jit(solution)/shard_map/all_to_all | solution.py:113
  129.8 6.8 %collective-permute-start.1 = (bf16[4,8,112,128]{3,2,1,0:T(8,128)(2,1)}, bf16[4,8,112,128]{3,2,1,0:T(8,128)(2,1)}, u32[]{:S(2)}, u32[]{:S(2)}) collective-permute-start(bf16[4,8,112,128]{3,2,1,0:T(8,128)(2,1)} %all_to_all.35.own_ref), channel_id=1, source_target_pairs={{0,8},{8,0},{1,9},{9,1},{2,10},{10,2},{3,11},{11,3},{4,12},{12,4},... | collective-permute-start | bytes 2752520 | tf_op jit(solution)/shard_map/ppermute | solution.py:159
  136.6 1.6 slice.24
  138.2 0.8 collective-permute-done.1.other_ref
  139.0 1.6 slice.25
  140.6 1.7 %shard_map.119 = f32[8,128]{1,0:T(8,128)} custom-call(bf16[32,16,128]{2,1,0:T(8,128)(2,1)} %bitcast.13, bf16[32,16,128]{2,1,0:T(8,128)(2,1)} %bitcast.14), custom_call_target="tpu_custom_call" | custom-call | tf_op jit(solution)/shard_map/pallas_call | solution.py:160
  142.3 0.8 slice_reduce_fusion
  143.1 11.7 %pmax.7 = f32[3]{0:T(128)S(1)} all-reduce(f32[3]{0:T(128)S(1)} %slice_reduce_fusion), channel_id=1, replica_groups=mesh['x'=4,'z'=8,'core'=2,'y'=8] {'y'}, use_global_device_ids=true, to_apply=%region_3.0 | all-reduce | flops 3 | bytes 24 | tf_op jit(solution)/shard_map/pmax | solution.py:169
  154.7 0.0 copy-start.2
  154.7 0.6 fusion
  155.3 0.0 copy-done.2
  155.3 4.1 %shard_map.120 = (bf16[64,12288]{1,0:T(8,128)(2,1)}, bf16[64,192]{1,0:T(8,128)(2,1)}) custom-call(s32[1]{0:T(128)} %bitcast.5.core_ref, f32[3]{0:T(128)} %copy-done.2, bf16[4,8,112,128]{3,2,1,0:T(8,128)(2,1)} %all_to_all.35.own_ref, bf16[4,8,112,128]{3,2,1,0:T(8,128)(2,1)} %collective-permute-done.1.other_ref, f32[64,192]{1,0:T(8,128)} %get-tuple-element.15.moment_ref), custom_call_target="tpu_custom_call" | custom-call | tf_op jit(solution)/shard_map/pallas_call | solution.py:172
  (2 shorter events, 0.0 us)
Async XLA Ops:
  0.6 34.6 %copy-start = (bf16[1024,1536]{1,0:T(8,128)(2,1)S(1)}, bf16[1024,1536]{1,0:T(8,128)(2,1)}, u32[]{:S(2)}) copy-start(bf16[1024,1536]{1,0:T(8,128)(2,1)} %param.6) | copy-start | bytes 9437188
  86.4 6.7 %collective-permute-start = (f32[96,128]{1,0:T(8,128)S(1)}, f32[96,128]{1,0:T(8,128)S(1)}, u32[]{:S(2)}, u32[]{:S(2)}) collective-permute-start(f32[96,128]{1,0:T(8,128)S(1)} %convert_reduce_fusion), channel_id=1, source_target_pairs={{0,0},{1,64},{2,128},{3,192},{4,256},{5,320},{6,384},{7,448},{8,4}... | collective-permute-start | bytes 147464 | tf_op jit(solution)/shard_map/ppermute | solution.py:147
  93.1 0.6 copy-start.1
  129.8 9.2 %collective-permute-start.1 = (bf16[4,8,112,128]{3,2,1,0:T(8,128)(2,1)}, bf16[4,8,112,128]{3,2,1,0:T(8,128)(2,1)}, u32[]{:S(2)}, u32[]{:S(2)}) collective-permute-start(bf16[4,8,112,128]{3,2,1,0:T(8,128)(2,1)} %all_to_all.35.own_ref), channel_id=1, source_target_pairs={{0,8},{8,0},{1,9},{9,1},{2,10},{10,2},{3,11},{11,3},{4,12},{12,4},... | collective-permute-start | bytes 2752520 | tf_op jit(solution)/shard_map/ppermute | solution.py:159
  154.7 0.6 copy-start.2

commit v2 on v0

v2 whole, which is shorter than its diff:
```python
import functools

import jax
import jax.numpy as jnp
from jax import lax
from jax.experimental import pallas as pl
from jax.experimental.pallas import tpu as pltpu
from jax.sharding import Mesh, PartitionSpec as P

EPSILON = 1e-06
BETA_ONE = 0.9
BETA_TWO = 0.999
LEARN_RATE = 0.001
DECAY_RATE = 0.1
ADAM_EPSILON = 1e-08

F32 = jnp.float32
BF16 = jnp.bfloat16
LANES = 128
HALF = LANES // 2
TOP_ROWS = 16
TILE = 512
DEVICE = ("x", "z", "core", "y")
SMEM = pl.BlockSpec(memory_space=pltpu.SMEM)
VMEM = pl.BlockSpec(memory_space=pltpu.VMEM)
PARAMS = pltpu.CompilerParams(vmem_limit_bytes=32 * 1024 * 1024)


def fold(middle, odd):
    rows = middle.shape[0] // 2
    upper, lower = middle[:rows], pltpu.roll(middle[rows:], HALF, 1)
    left = lax.broadcasted_iota(jnp.int32, upper.shape, 1) < HALF
    return jnp.where(left, lower, upper) if odd else jnp.where(left, upper, lower)


def unfold(even_tail, odd_tail):
    left = lax.broadcasted_iota(jnp.int32, even_tail.shape, 1) < HALF
    upper = jnp.where(left, even_tail, odd_tail)
    lower = pltpu.roll(jnp.where(left, odd_tail, even_tail), HALF, 1)
    return jnp.concatenate([upper, lower], 0)


def largest(value):
    return jnp.max(jnp.max(jnp.abs(value), axis=1, keepdims=True), axis=0, keepdims=True)


def multiply_for_other(core_ref, grads_ref, activations_ref, out_ref, top_ref):
    grads = grads_ref[1 - core_ref[0]]
    best = None
    for start in range(0, out_ref.shape[1], TILE):
        value = jnp.dot(grads, activations_ref[:, start : start + TILE], preferred_element_type=F32)
        out_ref[:, start : start + TILE] = value.astype(BF16)
        best = largest(value) if best is None else jnp.maximum(best, largest(value))
    top_ref[...] = jnp.broadcast_to(best, top_ref.shape)


def multiply_and_add(core_ref, grads_ref, activations_ref, other_ref, out_ref, top_ref):
    grads = grads_ref[core_ref[0]]
    best = None
    for start in range(0, out_ref.shape[1], TILE):
        value = jnp.dot(grads, activations_ref[:, start : start + TILE], preferred_element_type=F32)
        out_ref[:, start : start + TILE] = (
            value + other_ref[:, start : start + TILE].astype(F32)
        ).astype(BF16)
        best = largest(value) if best is None else jnp.maximum(best, largest(value))
    top_ref[...] = jnp.broadcast_to(best, top_ref.shape)


def add_and_cut(parts_ref, out_ref):
    rows = parts_ref.shape[1]

    def total(tile):
        where = slice(tile * LANES, (tile + 1) * LANES)
        value = parts_ref[0, :, where].astype(F32)
        for part in range(1, parts_ref.shape[0]):
            value += parts_ref[part, :, where].astype(F32)
        return value

    for pair in range(out_ref.shape[0] // 2):
        middle = total(3 * pair + 1)
        for odd in range(2):
            out_ref[2 * pair + odd, :rows] = total(3 * pair + 2 * odd).astype(BF16)
            out_ref[2 * pair + odd, rows:] = fold(middle, odd).astype(BF16)


def adam_step(
    devices, core_ref, range_ref, summed_ref, first_top_ref, second_top_ref,
    master_ref, moment_ref, second_ref,
    master_out, second_out, moment_out, sent_out, tops_out,
):
    rows = master_ref.shape[0]
    is_even = core_ref[0] == 0
    own, tail = summed_ref[:rows], summed_ref[rows:]
    middle = unfold(tail, tail)
    gradient = jnp.where(
        is_even,
        jnp.concatenate([own, middle[:, :HALF]], 1),
        jnp.concatenate([middle[:, HALF:], own], 1),
    ) / devices
    moment = (
        BETA_ONE * (moment_ref[...].astype(F32) * range_ref[0]) + (1.0 - BETA_ONE) * gradient
    )
    second_new = BETA_TWO * second_ref[...] + (1.0 - BETA_TWO) * gradient * gradient
    master = master_ref[...]
    master_new = master - LEARN_RATE * (
        moment / (jnp.sqrt(second_new) + ADAM_EPSILON) + DECAY_RATE * master
    )
    master_out[...] = master_new
    second_out[...] = second_new
    moment_out[...] = moment
    sent_out[:rows] = jnp.where(is_even, master_new[:, :LANES], master_new[:, HALF:]).astype(BF16)
    middle = jnp.concatenate([master_new[:, LANES:], master_new[:, :HALF]], 1)
    sent_out[rows:] = jnp.where(is_even, fold(middle, False), fold(middle, True)).astype(BF16)
    row = lax.broadcasted_iota(jnp.int32, (8, LANES), 0)
    partial_top = jnp.maximum(first_top_ref[...], second_top_ref[...])
    tops = jnp.where(row == 0, partial_top, jnp.where(row == 1, largest(moment), largest(master_new)))
    for copy in range(tops_out.shape[0]):
        tops_out[copy] = tops


def join_tops(tops_ref, weights_ref, out_ref):
    rows = weights_ref.shape[0]
    top = tops_ref[0]
    for place in range(1, tops_ref.shape[0]):
        top = jnp.maximum(top, tops_ref[place])
    high = top.astype(BF16).astype(F32)
    middle = (top - high).astype(BF16).astype(F32)
    low = top - high - middle
    row = lax.broadcasted_iota(jnp.int32, top.shape, 0)
    spread = jnp.concatenate([jnp.where(row < 4, high, pltpu.roll(low, 4, 0)), middle], 0)
    for copy in range(out_ref.shape[0]):
        out_ref[copy, :rows] = weights_ref[...]
        out_ref[copy, rows:] = spread.astype(BF16)


def scale_weights(
    core_ref, own_ref, other_ref, moment_ref,
    weight_out, moment_out, moment_span_out, weight_span_out, grad_span_out, span_ref,
):
    rows = weight_out.shape[0]
    packed = rows + rows // 2
    step = pl.program_id(0)
    is_even = core_ref[0] == 0

    @pl.when(step == 0)
    def _():
        best = jnp.zeros((8, LANES), F32)
        for held in (own_ref, other_ref):
            for x in range(held.shape[0]):
                for z in range(held.shape[1]):
                    spread = held[x, z, packed:].astype(F32)
                    high, middle = spread[:8], spread[8:]
                    best = jnp.maximum(best, high + middle + pltpu.roll(high, 4, 0))
        spans = best + EPSILON
        span_ref[...] = spans
        moment_out[...] = (moment_ref[...] / largest(spans[1:2])).astype(BF16)
        grad_span_out[0] = jnp.max(spans[0:1])
        moment_span_out[0] = jnp.max(spans[1:2])
        weight_span_out[0] = jnp.max(spans[2:3])

    span = span_ref[2:3]
    for place in range(own_ref.shape[1]):
        own = own_ref[step, place, :packed].astype(F32) / span
        other = other_ref[step, place, :packed].astype(F32) / span
        even, odd = jnp.where(is_even, own, other), jnp.where(is_even, other, own)
        start = 3 * LANES * place
        weight_out[:, start : start + LANES] = even[:rows].astype(BF16)
        weight_out[:, start + LANES : start + 2 * LANES] = unfold(even[rows:], odd[rows:]).astype(BF16)
        weight_out[:, start + 2 * LANES : start + 3 * LANES] = odd[:rows].astype(BF16)


def copies_to_all(value, axis):
    copies = jnp.broadcast_to(value[None], (lax.axis_size(axis), *value.shape))
    return lax.all_to_all(copies, axis, 0, 0, tiled=True)


def on_device(activations, output_grads, master, moment_q, moment_range, second_moment):
    xs, zs, cores, ys = (lax.axis_size(name) for name in DEVICE)
    rows, width = master.shape
    packed = rows + rows // 2
    sent_rows = packed + TOP_ROWS
    core = lax.axis_index("core").reshape(1)
    swap = [(0, 1), (1, 0)]

    grads = copies_to_all(output_grads.T, "y").reshape(cores, -1, output_grads.shape[0])
    product = (
        jax.ShapeDtypeStruct((grads.shape[1], activations.shape[1]), BF16),
        jax.ShapeDtypeStruct((8, LANES), F32),
    )
    value, first_top = pl.pallas_call(
        multiply_for_other,
        out_shape=product,
        in_specs=[SMEM, VMEM, VMEM],
        out_specs=(VMEM, VMEM),
        compiler_params=PARAMS,
    )(core, grads, activations)

    value = lax.ppermute(value, "core", swap)
    value, second_top = pl.pallas_call(
        multiply_and_add,
        out_shape=product,
        in_specs=[SMEM, VMEM, VMEM, VMEM],
        out_specs=(VMEM, VMEM),
        compiler_params=PARAMS,
    )(core, grads, activations, value)
    value = lax.all_to_all(value.reshape(xs, rows, -1), "x", 0, 0, tiled=True)
    value = pl.pallas_call(
        add_and_cut,
        out_shape=jax.ShapeDtypeStruct((zs, packed, LANES), BF16),
        in_specs=[VMEM],
        out_specs=VMEM,
    )(value)
    value = lax.all_to_all(value, "z", 0, 0, tiled=True)
    value = jnp.sum(value.astype(F32), axis=0)
    route = []
    for x in range(xs):
        for z in range(zs):
            for half in range(cores):
                for y in range(ys):
                    source = ((x * zs + z) * cores + half) * ys + y
                    route.append((source, (y * zs + z) * ys + half * xs + x))
    value = lax.ppermute(value, DEVICE, route)

    block = jax.ShapeDtypeStruct((rows, width), F32)
    master_new, second_new, moment, weights, tops = pl.pallas_call(
        functools.partial(adam_step, xs * zs * cores),
        out_shape=(
            block,
            block,
            block,
            jax.ShapeDtypeStruct((packed, LANES), BF16),
            jax.ShapeDtypeStruct((ys, 8, LANES), F32),
        ),
        in_specs=[SMEM, SMEM] + [VMEM] * 6,
        out_specs=(VMEM,) * 5,
    )(core, moment_range, value, first_top, second_top, master, moment_q, second_moment)

    tops = lax.all_to_all(tops, "y", 0, 0, tiled=True)
    held = pl.pallas_call(
        join_tops,
        out_shape=jax.ShapeDtypeStruct((zs, sent_rows, LANES), BF16),
        in_specs=[VMEM, VMEM],
        out_specs=VMEM,
    )(tops, weights)
    held = lax.all_to_all(held, "z", 0, 0, tiled=True)
    held = copies_to_all(held, "x").reshape(xs, zs, sent_rows, LANES)
    other = lax.ppermute(held, "core", swap)

    one = jax.ShapeDtypeStruct((1,), F32)
    weight_q, moment_q_new, moment_span, weight_span, grad_span = pl.pallas_call(
        scale_weights,
        grid=(xs,),
        out_shape=(
            jax.ShapeDtypeStruct((rows, width * xs * zs * cores), BF16),
            jax.ShapeDtypeStruct((rows, width), BF16),
            one,
            one,
            one,
        ),
        in_specs=[SMEM, VMEM, VMEM, VMEM],
        out_specs=(
            pl.BlockSpec((rows, width * zs * cores), lambda i: (0, i)),
            VMEM,
            SMEM,
            SMEM,
            SMEM,
        ),
        scratch_shapes=[pltpu.VMEM((8, LANES), F32)],
        compiler_params=PARAMS,
    )(core, held, other, moment)
    return master_new, moment_q_new, moment_span, second_new, weight_q, weight_span, grad_span


def solution(mesh):
    inner = Mesh(mesh.devices.reshape(4, 8, 2, 8), DEVICE)
    dp, mp = ("x", "z", "core"), "y"
    placed = (P(dp, mp), P(dp, mp), P(mp, dp), P(mp, dp), P(), P(mp, dp))
    return jax.shard_map(
        on_device,
        mesh=inner,
        in_specs=placed,
        out_specs=(P(mp, dp), P(mp, dp), P(), P(mp, dp), P(mp, None), P(), P()),
        check_vma=False,
    )
```

time: 563 us -> 153 us (0.27)
  waiting for transfers between devices: 269 us -> 32.2 us
  blocking collectives: 246 us -> 76.9 us
  starting transfers between devices: 0.12 us -> 25.8 us
  between operations: 19.8 us -> 1.36 us
  Pallas kernels: 0 us -> 11.9 us
  local copies, waits for them, and re-layouts: 15.2 us -> 4.07 us
  other arithmetic: 6.87 us -> 0.03 us
    pmax x2 -> x0, blocking collectives: 203 us -> none  [the longest x1 102 us: on_device(): lax.pmax(jnp.max(jnp.abs(partial_value)), ('dp', 'mp')) + EPSILON]
    unnamed x4 -> x0, waiting for transfers between devices: 146 us -> none
    all_gather x2 -> x0, waiting for transfers between devices: 123 us -> none  [the longest x1 79.3 us: on_device(): weight_q = lax.all_gather(weight_local, 'dp', axis=1, tiled=True)]
    all_to_all x1 -> x5, blocking collectives: 43.4 us -> 76.9 us  [the longest x1 18.7 us: on_device(): value = lax.all_to_all(value, 'z', 0, 0, tiled=True)]
    all_to_all x0 -> x1, waiting for transfers between devices: none -> 26.7 us  [copies_to_all(): return lax.all_to_all(copies, axis, 0, 0, tiled=True)]
    ppermute x0 -> x3, starting transfers between devices: none -> 18.2 us  [the longest x1 7.88 us: on_device(): other = lax.ppermute(held, 'core', swap)]
    pallas_call x0 -> x6, Pallas kernels: none -> 11.9 us  [the longest x1 2.28 us: on_device(): pl.pallas_call(multiply_and_add, out_shape=product, in_specs=[SMEM, VMEM,...]
    unnamed x13 -> x10, local copies, waits for them, and re-layouts: 11.2 us -> 1.8 us
  transfers between devices with their start and end apart: 3 -> 4, of which waited for: 3 -> 4; matrix products, arithmetic and copies ran while one was open for 0% -> 0% of each run, Pallas kernels for 0% -> 0%
where the time goes in v2:
time: 153 us; the launch traced here: 152 us
  blocking collectives  76.9 us (50%)
  waiting for transfers between devices  32.2 us (21%)
  starting transfers between devices  25.8 us (17%)
  Pallas kernels  11.9 us (8%)
  local copies, waits for them, and re-layouts  4.07 us (3%)
    all_to_all x1, waiting for transfers between devices, copies_to_all(): return lax.all_to_all(copies, axis, 0, 0, tiled=True)  26.7 us
    all_to_all x1, blocking collectives, on_device(): value = lax.all_to_all(value, 'z', 0, 0, tiled=True)  18.7 us
    all_to_all x1, blocking collectives, on_device(): held = lax.all_to_all(held, 'z', 0, 0, tiled=True)  15.6 us
    all_to_all x1, blocking collectives, on_device(): value = lax.all_to_all(value.reshape(xs, rows, -1), 'x', 0, 0, tiled=True)  15.3 us
    all_to_all x1, blocking collectives, copies_to_all(): return lax.all_to_all(copies, axis, 0, 0, tiled=True)  15.2 us
    all_to_all x1, blocking collectives, on_device(): tops = lax.all_to_all(tops, 'y', 0, 0, tiled=True)  12.1 us
    ppermute x1, starting transfers between devices, on_device(): other = lax.ppermute(held, 'core', swap)  7.88 us
    all_to_all x1, starting transfers between devices, copies_to_all(): return lax.all_to_all(copies, axis, 0, 0, tiled=True)  7.65 us
  transfers between devices with their start and end apart: 4, of which 4 were waited for; matrix products, arithmetic and copies ran while one was open for 0% of the time, Pallas kernels for 0%

profile of v2, /device:TPU:1, one launch (start us, length us, event | category | flops | bytes accessed | tf_op | source)
XLA Modules:
  0.0 152.2 jit_solution(16782357409016279867)
XLA Ops:
  0.6 0.0 copy-start
  0.6 2.2 %broadcast_in_dim.4 = bf16[8,64,1024]{2,1,0:T(8,128)(2,1)} broadcast(bf16[64,1024]{1,0:T(8,128)(2,1)} %bitcast.5), dimensions={1,2} | broadcast | bytes 1179648 | tf_op jit(solution)/shard_map/broadcast_in_dim | solution.py:173
  2.8 7.7 %all-to-all-start = ((bf16[8,64,1024]{2,1,0:T(8,128)(2,1)}), bf16[8,64,1024]{2,1,0:T(8,128)(2,1)}, u32[]{:S(2)}, u32[]{:S(2)}) async-start(bf16[8,64,1024]{2,1,0:T(8,128)(2,1)} %broadcast_in_dim.4), calls=%async_computation | async-start | bytes 2097152 | tf_op jit(solution)/shard_map/all_to_all | solution.py:174
  10.4 26.7 %all-to-all-done = bf16[8,64,1024]{2,1,0:T(8,128)(2,1)} async-done(((bf16[8,64,1024]{2,1,0:T(8,128)(2,1)}), bf16[8,64,1024]{2,1,0:T(8,128)(2,1)}, u32[]{:S(2)}, u32[]{:S(2)}) %all-to-all-start) | async-done | bytes 1048608 | tf_op jit(solution)/shard_map/all_to_all | solution.py:174
  37.2 0.0 copy-done
  37.2 2.3 %shard_map.117 = (bf16[256,1536]{1,0:T(8,128)(2,1)S(1)}, f32[8,128]{1,0:T(8,128)S(1)}) custom-call(s32[1]{0:T(128)} %bitcast.core_ref, bf16[2,256,1024]{2,1,0:T(8,128)(2,1)} %bitcast.2.grads_ref, bf16[1024,1536]{1,0:T(8,128)(2,1)S(1)} %copy-done), custom_call_target="tpu_custom_call" | custom-call | tf_op jit(solution)/shard_map/pallas_call | solution.py:190
  39.5 0.0 copy-start.2
  39.5 0.6 copy-done.2
  40.1 5.0 %collective-permute-start = (bf16[256,1536]{1,0:T(8,128)(2,1)S(1)}, bf16[256,1536]{1,0:T(8,128)(2,1)S(1)}, u32[]{:S(2)}, u32[]{:S(2)}) collective-permute-start(bf16[256,1536]{1,0:T(8,128)(2,1)S(1)} %get-tuple-element.21), channel_id=1, source_target_pairs={{0,8},{8,0},{1,9},{9,1},{2,10},{10,2},{3,11},{11,3},{4,12},{12,4},... | collective-permute-start | bytes 2359304 | tf_op jit(solution)/shard_map/ppermute | solution.py:198
  45.1 1.9 %collective-permute-done.other_ref = bf16[256,1536]{1,0:T(8,128)(2,1)S(1)} collective-permute-done((bf16[256,1536]{1,0:T(8,128)(2,1)S(1)}, bf16[256,1536]{1,0:T(8,128)(2,1)S(1)}, u32[]{:S(2)}, u32[]{:S(2)}) %collective-permute-start) | collective-permute-done | bytes 786464 | tf_op jit(solution)/shard_map/ppermute | solution.py:198
  47.0 2.3 %shard_map.118 = (bf16[256,1536]{1,0:T(8,128)(2,1)S(1)}, f32[8,128]{1,0:T(8,128)S(1)}) custom-call(s32[1]{0:T(128)} %bitcast.core_ref, bf16[2,256,1024]{2,1,0:T(8,128)(2,1)} %bitcast.2.grads_ref, bf16[1024,1536]{1,0:T(8,128)(2,1)S(1)} %copy-done, bf16[256,1536]{1,0:T(8,128)(2,1)S(1)} %collective-permute-done.other_ref), custom_call_target="tpu_custom_call" | custom-call | tf_op jit(solution)/shard_map/pallas_call | solution.py:199
  49.3 0.0 copy-start.3
  49.3 0.6 copy-done.3
  49.9 15.3 %all_to_all.30.parts_ref = bf16[4,64,1536]{2,1,0:T(8,128)(2,1)} all-to-all(bf16[4,64,1536]{2,1,0:T(8,128)(2,1)S(1)} %bitcast.4), channel_id=1, replica_groups=mesh['x'=4,'z'=8,'core'=2,'y'=8] {'x'}, dimensions={0} | all-to-all | bytes 1572864 | tf_op jit(solution)/shard_map/all_to_all | solution.py:206
  65.1 1.9 %shard_map.119 = bf16[8,96,128]{2,1,0:T(8,128)(2,1)} custom-call(bf16[4,64,1536]{2,1,0:T(8,128)(2,1)} %all_to_all.30.parts_ref), custom_call_target="tpu_custom_call" | custom-call | tf_op jit(solution)/shard_map/pallas_call | solution.py:207
  67.1 18.7 %all_to_all.31 = bf16[8,96,128]{2,1,0:T(8,128)(2,1)S(1)} all-to-all(bf16[8,96,128]{2,1,0:T(8,128)(2,1)} %shard_map.119), channel_id=1, replica_groups=mesh['x'=4,'z'=8,'core'=2,'y'=8] {'z'}, dimensions={0} | all-to-all | bytes 393216 | tf_op jit(solution)/shard_map/all_to_all | solution.py:213
  85.8 5.3 %collective-permute-start.1 = (f32[96,128]{1,0:T(8,128)S(1)}, f32[96,128]{1,0:T(8,128)S(1)}, u32[]{:S(2)}, u32[]{:S(2)}) collective-permute-start(f32[96,128]{1,0:T(8,128)S(1)} %convert_reduce_fusion), channel_id=1, source_target_pairs={{0,0},{1,64},{2,128},{3,192},{4,256},{5,320},{6,384},{7,448},{8,4}... | collective-permute-start | bytes 147464 | tf_op jit(solution)/shard_map/ppermute | solution.py:222
  91.7 1.5 collective-permute-done.1.summed_ref
  93.2 0.0 copy-start.4
  93.2 0.6 copy-done.4
  93.8 1.9 %shard_map.120 = (f32[64,192]{1,0:T(8,128)}, f32[64,192]{1,0:T(8,128)}, f32[64,192]{1,0:T(8,128)}, bf16[96,128]{1,0:T(8,128)(2,1)}, f32[8,8,128]{2,1,0:T(8,128)}) custom-call(s32[1]{0:T(128)} %bitcast.core_ref, f32[1]{0:T(128)S(6)} %copy.13.range_ref, f32[96,128]{1,0:T(8,128)} %copy-done.4, f32[8,128]{1,0:T(8,128)} %copy-done.2, f32[8,128]{1,0:T(8,128)} %copy-done.3, ...), custom_call_target="tpu_custom_call" | custom-call | tf_op jit(solution)/shard_map/pallas_call | solution.py:225
  95.7 0.0 copy-start.1
  95.7 12.1 %all_to_all.32.tops_ref = f32[8,8,128]{2,1,0:T(8,128)} all-to-all(f32[8,8,128]{2,1,0:T(8,128)} %get-tuple-element.26), channel_id=1, replica_groups=mesh['x'=4,'z'=8,'core'=2,'y'=8] {'y'}, dimensions={0} | all-to-all | bytes 65536 | tf_op jit(solution)/shard_map/all_to_all | solution.py:238
  107.8 1.5 shard_map.121
  109.3 15.6 %all_to_all.33 = bf16[8,112,128]{2,1,0:T(8,128)(2,1)S(1)} all-to-all(bf16[8,112,128]{2,1,0:T(8,128)(2,1)} %shard_map.121), channel_id=1, replica_groups=mesh['x'=4,'z'=8,'core'=2,'y'=8] {'z'}, dimensions={0} | all-to-all | bytes 458752 | tf_op jit(solution)/shard_map/all_to_all | solution.py:245
  124.9 0.1 broadcast_in_dim.5
  125.0 15.2 %all_to_all.34.own_ref = bf16[4,8,112,128]{3,2,1,0:T(8,128)(2,1)S(1)} all-to-all(bf16[4,8,112,128]{3,2,1,0:T(8,128)(2,1)S(1)} %broadcast_in_dim.5), channel_id=1, replica_groups=mesh['x'=4,'z'=8,'core'=2,'y'=8] {'x'}, dimensions={0} | all-to-all | bytes 1835008 | tf_op jit(solution)/shard_map/all_to_all | solution.py:174
  140.2 7.9 %collective-permute-start.2 = (bf16[4,8,112,128]{3,2,1,0:T(8,128)(2,1)S(1)}, bf16[4,8,112,128]{3,2,1,0:T(8,128)(2,1)S(1)}, u32[]{:S(2)}, u32[]{:S(2)}) collective-permute-start(bf16[4,8,112,128]{3,2,1,0:T(8,128)(2,1)S(1)} %all_to_all.34.own_ref), channel_id=1, source_target_pairs={{0,8},{8,0},{1,9},{9,1},{2,10},{10,2},{3,11},{11,3},{4,12},{12,4},... | collective-permute-start | bytes 2752520 | tf_op jit(solution)/shard_map/ppermute | solution.py:247
  148.1 2.1 %collective-permute-done.2.other_ref = bf16[4,8,112,128]{3,2,1,0:T(8,128)(2,1)S(1)} collective-permute-done((bf16[4,8,112,128]{3,2,1,0:T(8,128)(2,1)S(1)}, bf16[4,8,112,128]{3,2,1,0:T(8,128)(2,1)S(1)}, u32[]{:S(2)}, u32[]{:S(2)}) %collective-permute-start.2) | collective-permute-done | bytes 917536 | tf_op jit(solution)/shard_map/ppermute | solution.py:247
  150.1 0.0 copy-done.1
  150.1 2.1 %shard_map.122 = (bf16[64,12288]{1,0:T(8,128)(2,1)}, bf16[64,192]{1,0:T(8,128)(2,1)}, f32[1]{0:T(128)}, f32[1]{0:T(128)}, f32[1]{0:T(128)}) custom-call(s32[1]{0:T(128)} %bitcast.core_ref, bf16[4,8,112,128]{3,2,1,0:T(8,128)(2,1)S(1)} %all_to_all.34.own_ref, bf16[4,8,112,128]{3,2,1,0:T(8,128)(2,1)S(1)} %collective-permute-done.2.other_ref, ...), custom_call_target="tpu_custom_call" | custom-call | tf_op jit(solution)/shard_map/pallas_call | solution.py:250
  (1 shorter events, 0.0 us)
Async XLA Ops:
  0.6 36.5 %copy-start = (bf16[1024,1536]{1,0:T(8,128)(2,1)S(1)}, bf16[1024,1536]{1,0:T(8,128)(2,1)}, u32[]{:S(2)}) copy-start(bf16[1024,1536]{1,0:T(8,128)(2,1)} %activations_ref.3) | copy-start | bytes 9437188
  2.8 34.4 %all-to-all-start = ((bf16[8,64,1024]{2,1,0:T(8,128)(2,1)}), bf16[8,64,1024]{2,1,0:T(8,128)(2,1)}, u32[]{:S(2)}, u32[]{:S(2)}) async-start(bf16[8,64,1024]{2,1,0:T(8,128)(2,1)} %broadcast_in_dim.4), calls=%async_computation | async-start | bytes 2097152 | tf_op jit(solution)/shard_map/all_to_all | solution.py:174
  39.5 0.6 copy-start.2
  40.1 6.9 %collective-permute-start = (bf16[256,1536]{1,0:T(8,128)(2,1)S(1)}, bf16[256,1536]{1,0:T(8,128)(2,1)S(1)}, u32[]{:S(2)}, u32[]{:S(2)}) collective-permute-start(bf16[256,1536]{1,0:T(8,128)(2,1)S(1)} %get-tuple-element.21), channel_id=1, source_target_pairs={{0,8},{8,0},{1,9},{9,1},{2,10},{10,2},{3,11},{11,3},{4,12},{12,4},... | collective-permute-start | bytes 2359304 | tf_op jit(solution)/shard_map/ppermute | solution.py:198
  49.3 0.6 copy-start.3
  85.8 7.4 %collective-permute-start.1 = (f32[96,128]{1,0:T(8,128)S(1)}, f32[96,128]{1,0:T(8,128)S(1)}, u32[]{:S(2)}, u32[]{:S(2)}) collective-permute-start(f32[96,128]{1,0:T(8,128)S(1)} %convert_reduce_fusion), channel_id=1, source_target_pairs={{0,0},{1,64},{2,128},{3,192},{4,256},{5,320},{6,384},{7,448},{8,4}... | collective-permute-start | bytes 147464 | tf_op jit(solution)/shard_map/ppermute | solution.py:222
  93.2 0.6 copy-start.4
  95.7 54.5 %copy-start.1 = (f32[64,192]{1,0:T(8,128)S(1)}, f32[64,192]{1,0:T(8,128)}, u32[]{:S(2)}) copy-start(f32[64,192]{1,0:T(8,128)} %get-tuple-element.28.moment_ref) | copy-start | bytes 147460
  140.2 10.0 %collective-permute-start.2 = (bf16[4,8,112,128]{3,2,1,0:T(8,128)(2,1)S(1)}, bf16[4,8,112,128]{3,2,1,0:T(8,128)(2,1)S(1)}, u32[]{:S(2)}, u32[]{:S(2)}) collective-permute-start(bf16[4,8,112,128]{3,2,1,0:T(8,128)(2,1)S(1)} %all_to_all.34.own_ref), channel_id=1, source_target_pairs={{0,8},{8,0},{1,9},{9,1},{2,10},{10,2},{3,11},{11,3},{4,12},{12,4},... | collective-permute-start | bytes 2752520 | tf_op jit(solution)/shard_map/ppermute | solution.py:247

commit v3 on v2

--- a/solution.py
+++ b/solution.py
@@ -23,7 +23,7 @@
 DEVICE = ("x", "z", "core", "y")
 SMEM = pl.BlockSpec(memory_space=pltpu.SMEM)
 VMEM = pl.BlockSpec(memory_space=pltpu.VMEM)
-PARAMS = pltpu.CompilerParams(vmem_limit_bytes=32 * 1024 * 1024)
+PARAMS = pltpu.CompilerParams(vmem_limit_bytes=12 * 1024 * 1024)
 
 
 def fold(middle, odd):
@@ -44,26 +44,34 @@
     return jnp.max(jnp.max(jnp.abs(value), axis=1, keepdims=True), axis=0, keepdims=True)
 
 
+def magnitude(value, best):
+    top = jnp.max(jnp.abs(value).reshape(-1, 8, value.shape[1]), axis=0)
+    for start in range(0, value.shape[1], LANES):
+        part = top[:, start : start + LANES]
+        best = part if best is None else jnp.maximum(best, part)
+    return best
+
+
 def multiply_for_other(core_ref, grads_ref, activations_ref, out_ref, top_ref):
     grads = grads_ref[1 - core_ref[0]]
     best = None
     for start in range(0, out_ref.shape[1], TILE):
-        value = jnp.dot(grads, activations_ref[:, start : start + TILE], preferred_element_type=F32)
-        out_ref[:, start : start + TILE] = value.astype(BF16)
-        best = largest(value) if best is None else jnp.maximum(best, largest(value))
-    top_ref[...] = jnp.broadcast_to(best, top_ref.shape)
-
-
-def multiply_and_add(core_ref, grads_ref, activations_ref, other_ref, out_ref, top_ref):
+        where = slice(start, start + TILE)
+        value = jnp.dot(grads, activations_ref[:, where], preferred_element_type=F32)
+        out_ref[:, where] = value.astype(BF16)
+        best = magnitude(value, best)
+    top_ref[...] = best
+
+
+def multiply_and_add(core_ref, grads_ref, activations_ref, other_ref, first_ref, out_ref, top_ref):
     grads = grads_ref[core_ref[0]]
-    best = None
+    best = first_ref[...]
     for start in range(0, out_ref.shape[1], TILE):
-        value = jnp.dot(grads, activations_ref[:, start : start + TILE], preferred_element_type=F32)
-        out_ref[:, start : start + TILE] = (
-            value + other_ref[:, start : start + TILE].astype(F32)
-        ).astype(BF16)
-        best = largest(value) if best is None else jnp.maximum(best, largest(value))
-    top_ref[...] = jnp.broadcast_to(best, top_ref.shape)
+        where = slice(start, start + TILE)
+        value = jnp.dot(grads, activations_ref[:, where], preferred_element_type=F32)
+        out_ref[:, where] = (value + other_ref[:, where].astype(F32)).astype(BF16)
+        best = magnitude(value, best)
+    top_ref[...] = best
 
 
 def add_and_cut(parts_ref, out_ref):
@@ -84,9 +92,8 @@
 
 
 def adam_step(
-    devices, core_ref, range_ref, summed_ref, first_top_ref, second_top_ref,
-    master_ref, moment_ref, second_ref,
-    master_out, second_out, moment_out, sent_out, tops_out,
+    devices, core_ref, range_ref, summed_ref, top_ref, master_ref, moment_ref, second_ref,
+    master_out, second_out, moment_out, sent_out,
 ):
     rows = master_ref.shape[0]
     is_even = core_ref[0] == 0
@@ -108,33 +115,36 @@
     master_out[...] = master_new
     second_out[...] = second_new
     moment_out[...] = moment
-    sent_out[:rows] = jnp.where(is_even, master_new[:, :LANES], master_new[:, HALF:]).astype(BF16)
+    own = jnp.where(is_even, master_new[:, :LANES], master_new[:, HALF:]).astype(BF16)
     middle = jnp.concatenate([master_new[:, LANES:], master_new[:, :HALF]], 1)
-    sent_out[rows:] = jnp.where(is_even, fold(middle, False), fold(middle, True)).astype(BF16)
+    tail = jnp.where(is_even, fold(middle, False), fold(middle, True)).astype(BF16)
     row = lax.broadcasted_iota(jnp.int32, (8, LANES), 0)
-    partial_top = jnp.maximum(first_top_ref[...], second_top_ref[...])
-    tops = jnp.where(row == 0, partial_top, jnp.where(row == 1, largest(moment), largest(master_new)))
-    for copy in range(tops_out.shape[0]):
-        tops_out[copy] = tops
-
-
-def join_tops(tops_ref, weights_ref, out_ref):
-    rows = weights_ref.shape[0]
-    top = tops_ref[0]
-    for place in range(1, tops_ref.shape[0]):
-        top = jnp.maximum(top, tops_ref[place])
+    tops = (largest(top_ref[...]), largest(moment), largest(master_new))
+    top = jnp.where(row == 0, tops[0], jnp.where(row == 1, tops[1], tops[2]))
     high = top.astype(BF16).astype(F32)
     middle = (top - high).astype(BF16).astype(F32)
     low = top - high - middle
-    row = lax.broadcasted_iota(jnp.int32, top.shape, 0)
     spread = jnp.concatenate([jnp.where(row < 4, high, pltpu.roll(low, 4, 0)), middle], 0)
+    for copy in range(sent_out.shape[0]):
+        sent_out[copy, :rows] = own
+        sent_out[copy, rows : rows + rows // 2] = tail
+        sent_out[copy, rows + rows // 2 :] = spread.astype(BF16)
+
+
+def join_tops(held_ref, out_ref):
+    packed = held_ref.shape[2] - TOP_ROWS
+    best = jnp.zeros((8, LANES), F32)
+    for x in range(held_ref.shape[0]):
+        for z in range(held_ref.shape[1]):
+            spread = held_ref[x, z, packed:].astype(F32)
+            high, middle = spread[:8], spread[8:]
+            best = jnp.maximum(best, high + middle + pltpu.roll(high, 4, 0))
     for copy in range(out_ref.shape[0]):
-        out_ref[copy, :rows] = weights_ref[...]
-        out_ref[copy, rows:] = spread.astype(BF16)
+        out_ref[copy] = best
 
 
 def scale_weights(
-    core_ref, own_ref, other_ref, moment_ref,
+    core_ref, tops_ref, own_ref, other_ref, moment_ref,
     weight_out, moment_out, moment_span_out, weight_span_out, grad_span_out, span_ref,
 ):
     rows = weight_out.shape[0]
@@ -144,13 +154,9 @@
 
     @pl.when(step == 0)
     def _():
-        best = jnp.zeros((8, LANES), F32)
-        for held in (own_ref, other_ref):
-            for x in range(held.shape[0]):
-                for z in range(held.shape[1]):
-                    spread = held[x, z, packed:].astype(F32)
-                    high, middle = spread[:8], spread[8:]
-                    best = jnp.maximum(best, high + middle + pltpu.roll(high, 4, 0))
+        best = tops_ref[0]
+        for place in range(1, tops_ref.shape[0]):
+            best = jnp.maximum(best, tops_ref[place])
         spans = best + EPSILON
         span_ref[...] = spans
         moment_out[...] = (moment_ref[...] / largest(spans[1:2])).astype(BF16)
@@ -187,7 +193,7 @@
         jax.ShapeDtypeStruct((grads.shape[1], activations.shape[1]), BF16),
         jax.ShapeDtypeStruct((8, LANES), F32),
     )
-    value, first_top = pl.pallas_call(
+    value, top = pl.pallas_call(
         multiply_for_other,
         out_shape=product,
         in_specs=[SMEM, VMEM, VMEM],
@@ -196,13 +202,13 @@
     )(core, grads, activations)
 
     value = lax.ppermute(value, "core", swap)
-    value, second_top = pl.pallas_call(
+    value, top = pl.pallas_call(
         multiply_and_add,
         out_shape=product,
-        in_specs=[SMEM, VMEM, VMEM, VMEM],
+        in_specs=[SMEM] + [VMEM] * 4,
         out_specs=(VMEM, VMEM),
         compiler_params=PARAMS,
-    )(core, grads, activations, value)
+    )(core, grads, activations, value, top)
     value = lax.all_to_all(value.reshape(xs, rows, -1), "x", 0, 0, tiled=True)
     value = pl.pallas_call(
         add_and_cut,
@@ -222,29 +228,23 @@
     value = lax.ppermute(value, DEVICE, route)
 
     block = jax.ShapeDtypeStruct((rows, width), F32)
-    master_new, second_new, moment, weights, tops = pl.pallas_call(
+    master_new, second_new, moment, held = pl.pallas_call(
         functools.partial(adam_step, xs * zs * cores),
-        out_shape=(
-            block,
-            block,
-            block,
-            jax.ShapeDtypeStruct((packed, LANES), BF16),
-            jax.ShapeDtypeStruct((ys, 8, LANES), F32),
-        ),
-        in_specs=[SMEM, SMEM] + [VMEM] * 6,
-        out_specs=(VMEM,) * 5,
-    )(core, moment_range, value, first_top, second_top, master, moment_q, second_moment)
-
-    tops = lax.all_to_all(tops, "y", 0, 0, tiled=True)
-    held = pl.pallas_call(
-        join_tops,
-        out_shape=jax.ShapeDtypeStruct((zs, sent_rows, LANES), BF16),
-        in_specs=[VMEM, VMEM],
-        out_specs=VMEM,
-    )(tops, weights)
+        out_shape=(block, block, block, jax.ShapeDtypeStruct((zs, sent_rows, LANES), BF16)),
+        in_specs=[SMEM, SMEM] + [VMEM] * 5,
+        out_specs=(VMEM,) * 4,
+    )(core, moment_range, value, top, master, moment_q, second_moment)
+
     held = lax.all_to_all(held, "z", 0, 0, tiled=True)
     held = copies_to_all(held, "x").reshape(xs, zs, sent_rows, LANES)
     other = lax.ppermute(held, "core", swap)
+    tops = pl.pallas_call(
+        join_tops,
+        out_shape=jax.ShapeDtypeStruct((cores * ys, 8, LANES), F32),
+        in_specs=[VMEM],
+        out_specs=VMEM,
+    )(held)
+    tops = lax.all_to_all(tops, ("core", "y"), 0, 0, tiled=True)
 
     one = jax.ShapeDtypeStruct((1,), F32)
     weight_q, moment_q_new, moment_span, weight_span, grad_span = pl.pallas_call(
@@ -257,7 +257,7 @@
             one,
             one,
         ),
-        in_specs=[SMEM, VMEM, VMEM, VMEM],
+        in_specs=[SMEM, VMEM, VMEM, VMEM, VMEM],
         out_specs=(
             pl.BlockSpec((rows, width * zs * cores), lambda i: (0, i)),
             VMEM,
@@ -266,8 +266,8 @@
             SMEM,
         ),
         scratch_shapes=[pltpu.VMEM((8, LANES), F32)],
-        compiler_params=PARAMS,
-    )(core, held, other, moment)
+        compiler_params=pltpu.CompilerParams(vmem_limit_bytes=8 * 1024 * 1024),
+    )(core, tops, held, other, moment)
     return master_new, moment_q_new, moment_span, second_new, weight_q, weight_span, grad_span
 
 

time: 153 us -> 151 us (0.987)
  waiting for transfers between devices: 32.2 us -> 30.1 us
    ppermute x1, waiting for transfers between devices: 2.08 us -> 0.01 us  [on_device(): other = lax.ppermute(held, 'core', swap)]
    all_to_all x1, blocking collectives: 12.1 us -> 10.5 us  [on_device(): tops = lax.all_to_all(tops, ('core', 'y'), 0, 0, tiled=True)]
  transfers between devices with their start and end apart: 4 -> 4, of which waited for: 4 -> 3; matrix products, arithmetic and copies ran while one was open for 0% -> 0% of each run, Pallas kernels for 0% -> 1%
where the time goes in v3:
time: 151 us; the launch traced here: 150 us
  blocking collectives  77.4 us (51%)
  waiting for transfers between devices  30.1 us (20%)
  starting transfers between devices  24.5 us (16%)
  Pallas kernels  12.2 us (8%)
  local copies, waits for them, and re-layouts  4.65 us (3%)
    all_to_all x1, waiting for transfers between devices, copies_to_all(): return lax.all_to_all(copies, axis, 0, 0, tiled=True)  26.7 us
    all_to_all x1, blocking collectives, on_device(): value = lax.all_to_all(value, 'z', 0, 0, tiled=True)  18.7 us
    all_to_all x1, blocking collectives, copies_to_all(): return lax.all_to_all(copies, axis, 0, 0, tiled=True)  16.6 us
    all_to_all x1, blocking collectives, on_device(): held = lax.all_to_all(held, 'z', 0, 0, tiled=True)  16.3 us
    all_to_all x1, blocking collectives, on_device(): value = lax.all_to_all(value.reshape(xs, rows, -1), 'x', 0, 0, tiled=True)  15.3 us
    all_to_all x1, blocking collectives, on_device(): tops = lax.all_to_all(tops, ('core', 'y'), 0, 0, tiled=True)  10.5 us
    all_to_all x1, starting transfers between devices, copies_to_all(): return lax.all_to_all(copies, axis, 0, 0, tiled=True)  7.65 us
    ppermute x1, starting transfers between devices, on_device(): other = lax.ppermute(held, 'core', swap)  6.59 us
  transfers between devices with their start and end apart: 4, of which 3 were waited for; matrix products, arithmetic and copies ran while one was open for 0% of the time, Pallas kernels for 1%

profile of v3, /device:TPU:1, one launch (start us, length us, event | category | flops | bytes accessed | tf_op | source)
XLA Modules:
  0.0 150.2 jit_solution(11328005347659482989)
XLA Ops:
  0.6 0.0 copy-start
  0.6 2.2 %broadcast_in_dim.4 = bf16[8,64,1024]{2,1,0:T(8,128)(2,1)} broadcast(bf16[64,1024]{1,0:T(8,128)(2,1)} %bitcast.5), dimensions={1,2} | broadcast | bytes 1179648 | tf_op jit(solution)/shard_map/broadcast_in_dim | solution.py:179
  2.8 7.7 %all-to-all-start = ((bf16[8,64,1024]{2,1,0:T(8,128)(2,1)}), bf16[8,64,1024]{2,1,0:T(8,128)(2,1)}, u32[]{:S(2)}, u32[]{:S(2)}) async-start(bf16[8,64,1024]{2,1,0:T(8,128)(2,1)} %broadcast_in_dim.4), calls=%async_computation | async-start | bytes 2097152 | tf_op jit(solution)/shard_map/all_to_all | solution.py:180
  10.4 26.7 %all-to-all-done = bf16[8,64,1024]{2,1,0:T(8,128)(2,1)} async-done(((bf16[8,64,1024]{2,1,0:T(8,128)(2,1)}), bf16[8,64,1024]{2,1,0:T(8,128)(2,1)}, u32[]{:S(2)}, u32[]{:S(2)}) %all-to-all-start) | async-done | bytes 1048608 | tf_op jit(solution)/shard_map/all_to_all | solution.py:180
  37.2 0.0 copy-done
  37.2 2.2 %shard_map.117 = (bf16[256,1536]{1,0:T(8,128)(2,1)S(1)}, f32[8,128]{1,0:T(8,128)S(1)}) custom-call(s32[1]{0:T(128)} %bitcast.core_ref, bf16[2,256,1024]{2,1,0:T(8,128)(2,1)} %bitcast.2.grads_ref, bf16[1024,1536]{1,0:T(8,128)(2,1)S(1)} %copy-done), custom_call_target="tpu_custom_call" | custom-call | tf_op jit(solution)/shard_map/pallas_call | solution.py:196
  39.4 5.0 %collective-permute-start = (bf16[256,1536]{1,0:T(8,128)(2,1)S(1)}, bf16[256,1536]{1,0:T(8,128)(2,1)S(1)}, u32[]{:S(2)}, u32[]{:S(2)}) collective-permute-start(bf16[256,1536]{1,0:T(8,128)(2,1)S(1)} %get-tuple-element.20), channel_id=1, source_target_pairs={{0,8},{8,0},{1,9},{9,1},{2,10},{10,2},{3,11},{11,3},{4,12},{12,4},... | collective-permute-start | bytes 2359304 | tf_op jit(solution)/shard_map/ppermute | solution.py:204
  44.4 1.9 %collective-permute-done.other_ref = bf16[256,1536]{1,0:T(8,128)(2,1)S(1)} collective-permute-done((bf16[256,1536]{1,0:T(8,128)(2,1)S(1)}, bf16[256,1536]{1,0:T(8,128)(2,1)S(1)}, u32[]{:S(2)}, u32[]{:S(2)}) %collective-permute-start) | collective-permute-done | bytes 786464 | tf_op jit(solution)/shard_map/ppermute | solution.py:204
  46.3 2.2 %shard_map.118 = (bf16[256,1536]{1,0:T(8,128)(2,1)S(1)}, f32[8,128]{1,0:T(8,128)S(1)}) custom-call(s32[1]{0:T(128)} %bitcast.core_ref, bf16[2,256,1024]{2,1,0:T(8,128)(2,1)} %bitcast.2.grads_ref, bf16[1024,1536]{1,0:T(8,128)(2,1)S(1)} %copy-done, bf16[256,1536]{1,0:T(8,128)(2,1)S(1)} %collective-permute-done.other_ref, f32[8,128]{1,0:T(8,128)S(1)} %get-tuple-element.21.first_ref), custom_call_target="tpu_custom_call" | custom-call | tf_op jit(solution)/shard_map/pallas_call | solution.py:205
  48.5 0.0 copy-start.4
  48.6 0.6 copy-done.4
  49.1 15.3 %all_to_all.30.parts_ref = bf16[4,64,1536]{2,1,0:T(8,128)(2,1)} all-to-all(bf16[4,64,1536]{2,1,0:T(8,128)(2,1)S(1)} %bitcast.4), channel_id=1, replica_groups=mesh['x'=4,'z'=8,'core'=2,'y'=8] {'x'}, dimensions={0} | all-to-all | bytes 1572864 | tf_op jit(solution)/shard_map/all_to_all | solution.py:212
  64.4 1.9 %shard_map.119 = bf16[8,96,128]{2,1,0:T(8,128)(2,1)} custom-call(bf16[4,64,1536]{2,1,0:T(8,128)(2,1)} %all_to_all.30.parts_ref), custom_call_target="tpu_custom_call" | custom-call | tf_op jit(solution)/shard_map/pallas_call | solution.py:213
  66.3 18.7 %all_to_all.31 = bf16[8,96,128]{2,1,0:T(8,128)(2,1)S(1)} all-to-all(bf16[8,96,128]{2,1,0:T(8,128)(2,1)} %shard_map.119), channel_id=1, replica_groups=mesh['x'=4,'z'=8,'core'=2,'y'=8] {'z'}, dimensions={0} | all-to-all | bytes 393216 | tf_op jit(solution)/shard_map/all_to_all | solution.py:219
  85.1 5.3 %collective-permute-start.1 = (f32[96,128]{1,0:T(8,128)S(1)}, f32[96,128]{1,0:T(8,128)S(1)}, u32[]{:S(2)}, u32[]{:S(2)}) collective-permute-start(f32[96,128]{1,0:T(8,128)S(1)} %convert_reduce_fusion), channel_id=1, source_target_pairs={{0,0},{1,64},{2,128},{3,192},{4,256},{5,320},{6,384},{7,448},{8,4}... | collective-permute-start | bytes 147464 | tf_op jit(solution)/shard_map/ppermute | solution.py:228
  91.0 1.5 collective-permute-done.1.summed_ref
  92.5 0.0 copy-start.5
  92.5 0.6 copy-done.5
  93.1 2.0 %shard_map.120 = (f32[64,192]{1,0:T(8,128)}, f32[64,192]{1,0:T(8,128)}, f32[64,192]{1,0:T(8,128)}, bf16[8,112,128]{2,1,0:T(8,128)(2,1)}) custom-call(s32[1]{0:T(128)} %bitcast.core_ref, f32[1]{0:T(128)S(6)} %copy.13.range_ref, f32[96,128]{1,0:T(8,128)} %copy-done.5, f32[8,128]{1,0:T(8,128)} %copy-done.4, f32[64,192]{1,0:T(8,128)} %master_ref.1, ...), custom_call_target="tpu_custom_call" | custom-call | tf_op jit(solution)/shard_map/pallas_call | solution.py:231
  95.0 0.0 copy-start.3
  95.1 16.3 %all_to_all.32 = bf16[8,112,128]{2,1,0:T(8,128)(2,1)S(1)} all-to-all(bf16[8,112,128]{2,1,0:T(8,128)(2,1)} %get-tuple-element.25), channel_id=1, replica_groups=mesh['x'=4,'z'=8,'core'=2,'y'=8] {'z'}, dimensions={0} | all-to-all | bytes 458752 | tf_op jit(solution)/shard_map/all_to_all | solution.py:238
  111.3 0.1 broadcast_in_dim.5
  111.4 16.6 %all_to_all.33.held_ref.own_ref = bf16[4,8,112,128]{3,2,1,0:T(8,128)(2,1)S(1)} all-to-all(bf16[4,8,112,128]{3,2,1,0:T(8,128)(2,1)S(1)} %broadcast_in_dim.5), channel_id=1, replica_groups=mesh['x'=4,'z'=8,'core'=2,'y'=8] {'x'}, dimensions={0} | all-to-all | bytes 1835008 | tf_op jit(solution)/shard_map/all_to_all | solution.py:180
  128.1 0.0 copy-start.1
  128.1 6.6 %collective-permute-start.2 = (bf16[4,8,112,128]{3,2,1,0:T(8,128)(2,1)S(1)}, bf16[4,8,112,128]{3,2,1,0:T(8,128)(2,1)S(1)}, u32[]{:S(2)}, u32[]{:S(2)}) collective-permute-start(bf16[4,8,112,128]{3,2,1,0:T(8,128)(2,1)S(1)} %all_to_all.33.held_ref.own_ref), channel_id=1, source_target_pairs={{0,8},{8,0},{1,9},{9,1},{2,10},{10,2},{3,11},{11,3},{4,12},{12,4},... | collective-permute-start | bytes 2752520 | tf_op jit(solution)/shard_map/ppermute | solution.py:240
  134.7 0.0 copy-done.1
  134.7 1.8 %shard_map.121 = f32[16,8,128]{2,1,0:T(8,128)} custom-call(bf16[4,8,112,128]{3,2,1,0:T(8,128)(2,1)} %copy-done.1), custom_call_target="tpu_custom_call" | custom-call | tf_op jit(solution)/shard_map/pallas_call | solution.py:241
  136.5 10.5 %all_to_all.34.tops_ref = f32[16,8,128]{2,1,0:T(8,128)S(1)} all-to-all(f32[16,8,128]{2,1,0:T(8,128)} %shard_map.121), channel_id=1, replica_groups=mesh['x'=4,'z'=8,'core'=2,'y'=8] {'core','y'}, dimensions={0} | all-to-all | bytes 131072 | tf_op jit(solution)/shard_map/all_to_all | solution.py:247
  147.0 0.0 collective-permute-done.2.other_ref
  147.0 0.0 copy-done.3
  147.0 0.0 copy-start.2
  147.0 1.2 copy-done.2
  148.2 2.0 %shard_map.122 = (bf16[64,12288]{1,0:T(8,128)(2,1)}, bf16[64,192]{1,0:T(8,128)(2,1)}, f32[1]{0:T(128)}, f32[1]{0:T(128)}, f32[1]{0:T(128)}) custom-call(s32[1]{0:T(128)} %bitcast.core_ref, f32[16,8,128]{2,1,0:T(8,128)S(1)} %all_to_all.34.tops_ref, bf16[4,8,112,128]{3,2,1,0:T(8,128)(2,1)S(1)} %copy-done.2, ...), custom_call_target="tpu_custom_call" | custom-call | tf_op jit(solution)/shard_map/pallas_call | solution.py:250
  (1 shorter events, 0.0 us)
Async XLA Ops:
  0.6 36.5 %copy-start = (bf16[1024,1536]{1,0:T(8,128)(2,1)S(1)}, bf16[1024,1536]{1,0:T(8,128)(2,1)}, u32[]{:S(2)}) copy-start(bf16[1024,1536]{1,0:T(8,128)(2,1)} %activations_ref.3) | copy-start | bytes 9437188
  2.8 34.4 %all-to-all-start = ((bf16[8,64,1024]{2,1,0:T(8,128)(2,1)}), bf16[8,64,1024]{2,1,0:T(8,128)(2,1)}, u32[]{:S(2)}, u32[]{:S(2)}) async-start(bf16[8,64,1024]{2,1,0:T(8,128)(2,1)} %broadcast_in_dim.4), calls=%async_computation | async-start | bytes 2097152 | tf_op jit(solution)/shard_map/all_to_all | solution.py:180
  39.4 6.9 %collective-permute-start = (bf16[256,1536]{1,0:T(8,128)(2,1)S(1)}, bf16[256,1536]{1,0:T(8,128)(2,1)S(1)}, u32[]{:S(2)}, u32[]{:S(2)}) collective-permute-start(bf16[256,1536]{1,0:T(8,128)(2,1)S(1)} %get-tuple-element.20), channel_id=1, source_target_pairs={{0,8},{8,0},{1,9},{9,1},{2,10},{10,2},{3,11},{11,3},{4,12},{12,4},... | collective-permute-start | bytes 2359304 | tf_op jit(solution)/shard_map/ppermute | solution.py:204
  48.5 0.6 copy-start.4
  85.1 7.4 %collective-permute-start.1 = (f32[96,128]{1,0:T(8,128)S(1)}, f32[96,128]{1,0:T(8,128)S(1)}, u32[]{:S(2)}, u32[]{:S(2)}) collective-permute-start(f32[96,128]{1,0:T(8,128)S(1)} %convert_reduce_fusion), channel_id=1, source_target_pairs={{0,0},{1,64},{2,128},{3,192},{4,256},{5,320},{6,384},{7,448},{8,4}... | collective-permute-start | bytes 147464 | tf_op jit(solution)/shard_map/ppermute | solution.py:228
  92.5 0.6 copy-start.5
  95.0 52.0 %copy-start.3 = (f32[64,192]{1,0:T(8,128)S(1)}, f32[64,192]{1,0:T(8,128)}, u32[]{:S(2)}) copy-start(f32[64,192]{1,0:T(8,128)} %get-tuple-element.26.moment_ref) | copy-start | bytes 147460
  128.1 6.6 %copy-start.1 = (bf16[4,8,112,128]{3,2,1,0:T(8,128)(2,1)}, bf16[4,8,112,128]{3,2,1,0:T(8,128)(2,1)S(1)}, u32[]{:S(2)}) copy-start(bf16[4,8,112,128]{3,2,1,0:T(8,128)(2,1)S(1)} %all_to_all.33.held_ref.own_ref) | copy-start | bytes 2752516
  128.1 19.0 %collective-permute-start.2 = (bf16[4,8,112,128]{3,2,1,0:T(8,128)(2,1)S(1)}, bf16[4,8,112,128]{3,2,1,0:T(8,128)(2,1)S(1)}, u32[]{:S(2)}, u32[]{:S(2)}) collective-permute-start(bf16[4,8,112,128]{3,2,1,0:T(8,128)(2,1)S(1)} %all_to_all.33.held_ref.own_ref), channel_id=1, source_target_pairs={{0,8},{8,0},{1,9},{9,1},{2,10},{10,2},{3,11},{11,3},{4,12},{12,4},... | collective-permute-start | bytes 2752520 | tf_op jit(solution)/shard_map/ppermute | solution.py:240
  147.0 1.2 copy-start.2

commit v4 on v3

--- a/solution.py
+++ b/solution.py
@@ -23,7 +23,11 @@
 DEVICE = ("x", "z", "core", "y")
 SMEM = pl.BlockSpec(memory_space=pltpu.SMEM)
 VMEM = pl.BlockSpec(memory_space=pltpu.VMEM)
-PARAMS = pltpu.CompilerParams(vmem_limit_bytes=12 * 1024 * 1024)
+MIB = 1024 * 1024
+
+
+def grant(size):
+    return pltpu.CompilerParams(vmem_limit_bytes=size * MIB)
 
 
 def fold(middle, odd):
@@ -50,6 +54,25 @@
         part = top[:, start : start + LANES]
         best = part if best is None else jnp.maximum(best, part)
     return best
+
+
+def split(top):
+    high = top.astype(BF16).astype(F32)
+    middle = (top - high).astype(BF16).astype(F32)
+    low = top - high - middle
+    row = lax.broadcasted_iota(jnp.int32, top.shape, 0)
+    high = jnp.where(row < 4, high, pltpu.roll(low, 4, 0))
+    return jnp.concatenate([high, middle], 0).astype(BF16)
+
+
+def joined(spread):
+    spread = spread.astype(F32)
+    return spread[:8] + spread[8:] + pltpu.roll(spread[:8], 4, 0)
+
+
+def copy_grads(grads_ref, out_ref):
+    for copy in range(out_ref.shape[0]):
+        out_ref[copy] = grads_ref[...]
 
 
 def multiply_for_other(core_ref, grads_ref, activations_ref, out_ref, top_ref):
@@ -120,25 +143,28 @@
     tail = jnp.where(is_even, fold(middle, False), fold(middle, True)).astype(BF16)
     row = lax.broadcasted_iota(jnp.int32, (8, LANES), 0)
     tops = (largest(top_ref[...]), largest(moment), largest(master_new))
-    top = jnp.where(row == 0, tops[0], jnp.where(row == 1, tops[1], tops[2]))
-    high = top.astype(BF16).astype(F32)
-    middle = (top - high).astype(BF16).astype(F32)
-    low = top - high - middle
-    spread = jnp.concatenate([jnp.where(row < 4, high, pltpu.roll(low, 4, 0)), middle], 0)
+    spread = split(jnp.where(row == 0, tops[0], jnp.where(row == 1, tops[1], tops[2])))
     for copy in range(sent_out.shape[0]):
         sent_out[copy, :rows] = own
         sent_out[copy, rows : rows + rows // 2] = tail
-        sent_out[copy, rows + rows // 2 :] = spread.astype(BF16)
+        sent_out[copy, rows + rows // 2 :] = spread
+
+
+def join_blocks(held_ref, out_ref):
+    packed = held_ref.shape[1] - TOP_ROWS
+    best = None
+    for z in range(held_ref.shape[0]):
+        out_ref[z * packed : (z + 1) * packed] = held_ref[z, :packed]
+        top = joined(held_ref[z, packed:])
+        best = top if best is None else jnp.maximum(best, top)
+    out_ref[held_ref.shape[0] * packed :] = split(best)
 
 
 def join_tops(held_ref, out_ref):
-    packed = held_ref.shape[2] - TOP_ROWS
-    best = jnp.zeros((8, LANES), F32)
-    for x in range(held_ref.shape[0]):
-        for z in range(held_ref.shape[1]):
-            spread = held_ref[x, z, packed:].astype(F32)
-            high, middle = spread[:8], spread[8:]
-            best = jnp.maximum(best, high + middle + pltpu.roll(high, 4, 0))
+    packed = held_ref.shape[1] - TOP_ROWS
+    best = joined(held_ref[0, packed:])
+    for x in range(1, held_ref.shape[0]):
+        best = jnp.maximum(best, joined(held_ref[x, packed:]))
     for copy in range(out_ref.shape[0]):
         out_ref[copy] = best
 
@@ -165,19 +191,15 @@
         weight_span_out[0] = jnp.max(spans[2:3])
 
     span = span_ref[2:3]
-    for place in range(own_ref.shape[1]):
-        own = own_ref[step, place, :packed].astype(F32) / span
-        other = other_ref[step, place, :packed].astype(F32) / span
+    for place in range((own_ref.shape[1] - TOP_ROWS) // packed):
+        where = slice(place * packed, (place + 1) * packed)
+        own = own_ref[step, where].astype(F32) / span
+        other = other_ref[step, where].astype(F32) / span
         even, odd = jnp.where(is_even, own, other), jnp.where(is_even, other, own)
         start = 3 * LANES * place
         weight_out[:, start : start + LANES] = even[:rows].astype(BF16)
         weight_out[:, start + LANES : start + 2 * LANES] = unfold(even[rows:], odd[rows:]).astype(BF16)
         weight_out[:, start + 2 * LANES : start + 3 * LANES] = odd[:rows].astype(BF16)
-
-
-def copies_to_all(value, axis):
-    copies = jnp.broadcast_to(value[None], (lax.axis_size(axis), *value.shape))
-    return lax.all_to_all(copies, axis, 0, 0, tiled=True)
 
 
 def on_device(activations, output_grads, master, moment_q, moment_range, second_moment):
@@ -186,9 +208,18 @@
     packed = rows + rows // 2
     sent_rows = packed + TOP_ROWS
     core = lax.axis_index("core").reshape(1)
+    output_grads, core = lax.optimization_barrier((output_grads, core))
     swap = [(0, 1), (1, 0)]
 
-    grads = copies_to_all(output_grads.T, "y").reshape(cores, -1, output_grads.shape[0])
+    tokens, columns = output_grads.shape
+    grads = pl.pallas_call(
+        copy_grads,
+        out_shape=jax.ShapeDtypeStruct((ys, columns, tokens), BF16),
+        in_specs=[VMEM],
+        out_specs=VMEM,
+        compiler_params=grant(4),
+    )(output_grads.T)
+    grads = lax.all_to_all(grads, "y", 0, 0, tiled=True).reshape(cores, -1, tokens)
     product = (
         jax.ShapeDtypeStruct((grads.shape[1], activations.shape[1]), BF16),
         jax.ShapeDtypeStruct((8, LANES), F32),
@@ -198,7 +229,7 @@
         out_shape=product,
         in_specs=[SMEM, VMEM, VMEM],
         out_specs=(VMEM, VMEM),
-        compiler_params=PARAMS,
+        compiler_params=grant(12),
     )(core, grads, activations)
 
     value = lax.ppermute(value, "core", swap)
@@ -207,7 +238,7 @@
         out_shape=product,
         in_specs=[SMEM] + [VMEM] * 4,
         out_specs=(VMEM, VMEM),
-        compiler_params=PARAMS,
+        compiler_params=grant(12),
     )(core, grads, activations, value, top)
     value = lax.all_to_all(value.reshape(xs, rows, -1), "x", 0, 0, tiled=True)
     value = pl.pallas_call(
@@ -215,6 +246,7 @@
         out_shape=jax.ShapeDtypeStruct((zs, packed, LANES), BF16),
         in_specs=[VMEM],
         out_specs=VMEM,
+        compiler_params=grant(4),
     )(value)
     value = lax.all_to_all(value, "z", 0, 0, tiled=True)
     value = jnp.sum(value.astype(F32), axis=0)
@@ -233,16 +265,25 @@
         out_shape=(block, block, block, jax.ShapeDtypeStruct((zs, sent_rows, LANES), BF16)),
         in_specs=[SMEM, SMEM] + [VMEM] * 5,
         out_specs=(VMEM,) * 4,
+        compiler_params=grant(4),
     )(core, moment_range, value, top, master, moment_q, second_moment)
 
     held = lax.all_to_all(held, "z", 0, 0, tiled=True)
-    held = copies_to_all(held, "x").reshape(xs, zs, sent_rows, LANES)
+    held = pl.pallas_call(
+        join_blocks,
+        out_shape=jax.ShapeDtypeStruct((zs * packed + TOP_ROWS, LANES), BF16),
+        in_specs=[VMEM],
+        out_specs=VMEM,
+        compiler_params=grant(4),
+    )(held)
+    held = lax.all_gather(held, "x")
     other = lax.ppermute(held, "core", swap)
     tops = pl.pallas_call(
         join_tops,
         out_shape=jax.ShapeDtypeStruct((cores * ys, 8, LANES), F32),
         in_specs=[VMEM],
         out_specs=VMEM,
+        compiler_params=grant(4),
     )(held)
     tops = lax.all_to_all(tops, ("core", "y"), 0, 0, tiled=True)
 
@@ -266,7 +307,7 @@
             SMEM,
         ),
         scratch_shapes=[pltpu.VMEM((8, LANES), F32)],
-        compiler_params=pltpu.CompilerParams(vmem_limit_bytes=8 * 1024 * 1024),
+        compiler_params=grant(8),
     )(core, tops, held, other, moment)
     return master_new, moment_q_new, moment_span, second_new, weight_q, weight_span, grad_span
 

time: 151 us -> 137 us (0.907)
  blocking collectives: 77.4 us -> 107 us
  waiting for transfers between devices: 30.1 us -> 3.35 us
  Pallas kernels: 12.2 us -> 5.11 us
  starting transfers between devices: 24.5 us -> 19.2 us
  local copies, waits for them, and re-layouts: 4.65 us -> 1.06 us
    all_to_all x1 -> x0, waiting for transfers between devices: 26.7 us -> none  [copies_to_all(): return lax.all_to_all(copies, axis, 0, 0, tiled=True)]
    all_to_all x1, blocking collectives: 16.6 us -> 33.4 us  [on_device(): lax.all_to_all(grads, 'y', 0, 0, tiled=True).reshape(cores, -1, tokens)]
    all_gather x0 -> x1, blocking collectives: none -> 13.6 us  [on_device(): held = lax.all_gather(held, 'x')]
    all_to_all x1 -> x0, starting transfers between devices: 7.65 us -> none  [copies_to_all(): return lax.all_to_all(copies, axis, 0, 0, tiled=True)]
    broadcast_in_dim x2 -> x0, local copies, waits for them, and re-layouts: 2.27 us -> none  [copies_to_all(): copies = jnp.broadcast_to(value[None], (lax.axis_size(axis), *value.shape))]
    pallas_call x1, Pallas kernels: 1.84 us -> 0.01 us  [on_device(): pl.pallas_call(join_tops, out_shape=jax.ShapeDtypeStruct((cores * ys, 8,...]
    pallas_call x1, Pallas kernels: 1.92 us -> 0.11 us  [on_device(): pl.pallas_call(add_and_cut, out_shape=jax.ShapeDtypeStruct((zs, packed, L...]
    ppermute x1, starting transfers between devices: 6.59 us -> 8.29 us  [on_device(): other = lax.ppermute(held, 'core', swap)]
  transfers between devices with their start and end apart: 4 -> 3, of which waited for: 3 -> 2; matrix products, arithmetic and copies ran while one was open for 0% -> 0% of each run, Pallas kernels for 1% -> 0%
where the time goes in v4:
time: 137 us
  blocking collectives  107 us (78%)
  starting transfers between devices  19.2 us (14%)
  Pallas kernels  5.11 us (4%)
  waiting for transfers between devices  3.35 us (2%)
    all_to_all x1, blocking collectives, on_device(): lax.all_to_all(grads, 'y', 0, 0, tiled=True).reshape(cores, -1, tokens)  33.4 us
    all_to_all x1, blocking collectives, on_device(): value = lax.all_to_all(value, 'z', 0, 0, tiled=True)  18.5 us
    all_to_all x1, blocking collectives, on_device(): held = lax.all_to_all(held, 'z', 0, 0, tiled=True)  16 us
    all_to_all x1, blocking collectives, on_device(): value = lax.all_to_all(value.reshape(xs, rows, -1), 'x', 0, 0, tiled=True)  15.3 us
    all_gather x1, blocking collectives, on_device(): held = lax.all_gather(held, 'x')  13.6 us
    all_to_all x1, blocking collectives, on_device(): tops = lax.all_to_all(tops, ('core', 'y'), 0, 0, tiled=True)  10.3 us
    ppermute x1, starting transfers between devices, on_device(): other = lax.ppermute(held, 'core', swap)  8.29 us
    ppermute x1, starting transfers between devices, on_device(): value = lax.ppermute(value, 'core', swap)  5.62 us
  transfers between devices with their start and end apart: 3, of which 2 were waited for; matrix products, arithmetic and copies ran while one was open for 0% of the time, Pallas kernels for 0%

profile of v4, /device:TPU:1, one launch (start us, length us, event | category | flops | bytes accessed | tf_op | source)
XLA Modules:
  0.0 137.1 jit_solution(8213685814921598943)
XLA Ops:
  0.6 0.0 copy-start
  0.6 0.0 copy-start.1
  0.7 1.0 copy-done.1
  1.7 0.1 shard_map.117
  1.8 33.4 %all_to_all.25 = bf16[8,64,1024]{2,1,0:T(8,128)(2,1)S(1)} all-to-all(bf16[8,64,1024]{2,1,0:T(8,128)(2,1)S(1)} %shard_map.117), channel_id=1, replica_groups=mesh['x'=4,'z'=8,'core'=2,'y'=8] {'y'}, dimensions={0} | all-to-all | bytes 2097152 | tf_op jit(solution)/shard_map/all_to_all | solution.py:222
  35.2 0.0 copy-done
  35.2 1.0 shard_map.118
  36.2 5.6 %collective-permute-start = (bf16[256,1536]{1,0:T(8,128)(2,1)S(1)}, bf16[256,1536]{1,0:T(8,128)(2,1)S(1)}, u32[]{:S(2)}, u32[]{:S(2)}) collective-permute-start(bf16[256,1536]{1,0:T(8,128)(2,1)S(1)} %get-tuple-element.24), channel_id=1, source_target_pairs={{0,8},{8,0},{1,9},{9,1},{2,10},{10,2},{3,11},{11,3},{4,12},{12,4},... | collective-permute-start | bytes 2359304 | tf_op jit(solution)/shard_map/ppermute | solution.py:235
  41.8 1.9 %collective-permute-done.other_ref = bf16[256,1536]{1,0:T(8,128)(2,1)S(1)} collective-permute-done((bf16[256,1536]{1,0:T(8,128)(2,1)S(1)}, bf16[256,1536]{1,0:T(8,128)(2,1)S(1)}, u32[]{:S(2)}, u32[]{:S(2)}) %collective-permute-start) | collective-permute-done | bytes 786464 | tf_op jit(solution)/shard_map/ppermute | solution.py:235
  43.7 0.0 copy-start.2
  43.7 0.0 copy-start.3
  43.7 0.0 copy-start.4
  43.7 1.0 shard_map.119
  44.7 15.3 %all_to_all.26.parts_ref = bf16[4,64,1536]{2,1,0:T(8,128)(2,1)S(1)} all-to-all(bf16[4,64,1536]{2,1,0:T(8,128)(2,1)S(1)} %bitcast.10), channel_id=1, replica_groups=mesh['x'=4,'z'=8,'core'=2,'y'=8] {'x'}, dimensions={0} | all-to-all | bytes 1572864 | tf_op jit(solution)/shard_map/all_to_all | solution.py:243
  60.0 0.1 shard_map.120
  60.1 18.5 %all_to_all.27 = bf16[8,96,128]{2,1,0:T(8,128)(2,1)S(1)} all-to-all(bf16[8,96,128]{2,1,0:T(8,128)(2,1)S(1)} %shard_map.120), channel_id=1, replica_groups=mesh['x'=4,'z'=8,'core'=2,'y'=8] {'z'}, dimensions={0} | all-to-all | bytes 393216 | tf_op jit(solution)/shard_map/all_to_all | solution.py:251
  78.7 5.3 %collective-permute-start.1 = (f32[96,128]{1,0:T(8,128)S(1)}, f32[96,128]{1,0:T(8,128)S(1)}, u32[]{:S(2)}, u32[]{:S(2)}) collective-permute-start(f32[96,128]{1,0:T(8,128)S(1)} %convert_reduce_fusion), channel_id=1, source_target_pairs={{0,0},{1,64},{2,128},{3,192},{4,256},{5,320},{6,384},{7,448},{8,4}... | collective-permute-start | bytes 147464 | tf_op jit(solution)/shard_map/ppermute | solution.py:260
  84.6 1.5 %collective-permute-done.1.summed_ref = f32[96,128]{1,0:T(8,128)S(1)} collective-permute-done((f32[96,128]{1,0:T(8,128)S(1)}, f32[96,128]{1,0:T(8,128)S(1)}, u32[]{:S(2)}, u32[]{:S(2)}) %collective-permute-start.1) | collective-permute-done | bytes 49184 | tf_op jit(solution)/shard_map/ppermute | solution.py:260
  86.0 0.0 copy-done.2
  86.0 0.0 copy-done.3
  86.0 0.0 copy-done.4
  86.0 0.8 shard_map.121
  86.9 16.0 %all_to_all.28.held_ref = bf16[8,112,128]{2,1,0:T(8,128)(2,1)S(1)} all-to-all(bf16[8,112,128]{2,1,0:T(8,128)(2,1)S(1)} %get-tuple-element.29), channel_id=1, replica_groups=mesh['x'=4,'z'=8,'core'=2,'y'=8] {'z'}, dimensions={0} | all-to-all | bytes 458752 | tf_op jit(solution)/shard_map/all_to_all | solution.py:271
  102.9 13.6 %all-gather = bf16[3136,128]{1,0:T(8,128)(2,1)S(1)} all-gather(bf16[784,128]{1,0:T(8,128)(2,1)S(1)} %shard_map.122), channel_id=2, replica_groups=mesh['x'=4,'z'=8,'core'=2,'y'=8] {'x'}, dimensions={0}, use_global_device_ids=true | all-gather | bytes 1003520 | tf_op jit(solution)/shard_map/all_gather | solution.py:279
  116.5 8.3 %collective-permute-start.2 = (bf16[4,784,128]{2,1,0:T(8,128)(2,1)S(1)}, bf16[4,784,128]{2,1,0:T(8,128)(2,1)S(1)}, u32[]{:S(2)}, u32[]{:S(2)}) collective-permute-start(bf16[4,784,128]{2,1,0:T(8,128)(2,1)S(1)} %bitcast.7), channel_id=1, source_target_pairs={{0,8},{8,0},{1,9},{9,1},{2,10},{10,2},{3,11},{11,3},{4,12},{12,4},... | collective-permute-start | bytes 2408456 | tf_op jit(solution)/shard_map/ppermute | solution.py:280
  124.8 10.3 %all_to_all.29.tops_ref = f32[16,8,128]{2,1,0:T(8,128)S(1)} all-to-all(f32[16,8,128]{2,1,0:T(8,128)S(1)} %shard_map.123), channel_id=1, replica_groups=mesh['x'=4,'z'=8,'core'=2,'y'=8] {'core','y'}, dimensions={0} | all-to-all | bytes 131072 | tf_op jit(solution)/shard_map/all_to_all | solution.py:288
  135.1 0.0 collective-permute-done.2.other_ref
  135.1 2.0 %shard_map.124 = (bf16[64,12288]{1,0:T(8,128)(2,1)}, bf16[64,192]{1,0:T(8,128)(2,1)}, f32[1]{0:T(128)}, f32[1]{0:T(128)}, f32[1]{0:T(128)}) custom-call(s32[1]{0:T(128)} %bitcast.core_ref, f32[16,8,128]{2,1,0:T(8,128)S(1)} %all_to_all.29.tops_ref, bf16[4,784,128]{2,1,0:T(8,128)(2,1)S(1)} %bitcast.9, ...), custom_call_target="tpu_custom_call" | custom-call | tf_op jit(solution)/shard_map/pallas_call | solution.py:291
  (3 shorter events, 0.1 us)
Async XLA Ops:
  0.6 34.6 %copy-start = (bf16[1024,1536]{1,0:T(8,128)(2,1)S(1)}, bf16[1024,1536]{1,0:T(8,128)(2,1)}, u32[]{:S(2)}) copy-start(bf16[1024,1536]{1,0:T(8,128)(2,1)} %activations_ref.3) | copy-start | bytes 9437188
  0.6 1.1 copy-start.1
  36.2 7.5 %collective-permute-start = (bf16[256,1536]{1,0:T(8,128)(2,1)S(1)}, bf16[256,1536]{1,0:T(8,128)(2,1)S(1)}, u32[]{:S(2)}, u32[]{:S(2)}) collective-permute-start(bf16[256,1536]{1,0:T(8,128)(2,1)S(1)} %get-tuple-element.24), channel_id=1, source_target_pairs={{0,8},{8,0},{1,9},{9,1},{2,10},{10,2},{3,11},{11,3},{4,12},{12,4},... | collective-permute-start | bytes 2359304 | tf_op jit(solution)/shard_map/ppermute | solution.py:235
  43.7 42.3 %copy-start.2 = (f32[64,192]{1,0:T(8,128)S(1)}, f32[64,192]{1,0:T(8,128)}, u32[]{:S(2)}) copy-start(f32[64,192]{1,0:T(8,128)} %master_ref.1) | copy-start | bytes 147460
  43.7 42.3 %copy-start.3 = (f32[64,192]{1,0:T(8,128)S(1)}, f32[64,192]{1,0:T(8,128)}, u32[]{:S(2)}) copy-start(f32[64,192]{1,0:T(8,128)} %second_ref.1) | copy-start | bytes 147460
  43.7 42.3 %copy-start.4 = (bf16[64,192]{1,0:T(8,128)(2,1)S(1)}, bf16[64,192]{1,0:T(8,128)(2,1)}, u32[]{:S(2)}) copy-start(bf16[64,192]{1,0:T(8,128)(2,1)} %moment_ref.1) | copy-start | bytes 73732
  78.7 7.4 %collective-permute-start.1 = (f32[96,128]{1,0:T(8,128)S(1)}, f32[96,128]{1,0:T(8,128)S(1)}, u32[]{:S(2)}, u32[]{:S(2)}) collective-permute-start(f32[96,128]{1,0:T(8,128)S(1)} %convert_reduce_fusion), channel_id=1, source_target_pairs={{0,0},{1,64},{2,128},{3,192},{4,256},{5,320},{6,384},{7,448},{8,4}... | collective-permute-start | bytes 147464 | tf_op jit(solution)/shard_map/ppermute | solution.py:260
  116.5 18.6 %collective-permute-start.2 = (bf16[4,784,128]{2,1,0:T(8,128)(2,1)S(1)}, bf16[4,784,128]{2,1,0:T(8,128)(2,1)S(1)}, u32[]{:S(2)}, u32[]{:S(2)}) collective-permute-start(bf16[4,784,128]{2,1,0:T(8,128)(2,1)S(1)} %bitcast.7), channel_id=1, source_target_pairs={{0,8},{8,0},{1,9},{9,1},{2,10},{10,2},{3,11},{11,3},{4,12},{12,4},... | collective-permute-start | bytes 2408456 | tf_op jit(solution)/shard_map/ppermute | solution.py:280

commit v5 on v4

--- a/solution.py
+++ b/solution.py
@@ -75,8 +75,36 @@
         out_ref[copy] = grads_ref[...]
 
 
-def multiply_for_other(core_ref, grads_ref, activations_ref, out_ref, top_ref):
-    grads = grads_ref[1 - core_ref[0]]
+ABOVE = ((4, -1, 0, -2), (-3, 2, 1, 3))
+
+
+def columns_of(core, x, y):
+    place = (x - y // 2) % 4
+    if isinstance(y, int):
+        return (y + ABOVE[core][place]) % 8
+    above = 0
+    for half in range(2):
+        for step in range(4):
+            above = jnp.where((core == half) & (place == step), ABOVE[half][step], above)
+    return (y + above + 8) % 8
+
+
+def slot_of(feature, y):
+    near = feature // 2 if feature % 2 == 0 else 7 - feature // 2
+    return (near + 4 * (y % 2)) % 8
+
+
+def core_and_y(place_ref):
+    return place_ref[0] // 8, place_ref[0] % 8
+
+
+def grads_for(core, y, grads_ref):
+    return jnp.concatenate([grads_ref[columns_of(core, x, y)] for x in range(4)], 0)
+
+
+def multiply_for_other(place_ref, grads_ref, activations_ref, out_ref, top_ref):
+    core, y = core_and_y(place_ref)
+    grads = grads_for(1 - core, y, grads_ref)
     best = None
     for start in range(0, out_ref.shape[1], TILE):
         where = slice(start, start + TILE)
@@ -86,8 +114,8 @@
     top_ref[...] = best
 
 
-def multiply_and_add(core_ref, grads_ref, activations_ref, other_ref, first_ref, out_ref, top_ref):
-    grads = grads_ref[core_ref[0]]
+def multiply_and_add(place_ref, grads_ref, activations_ref, other_ref, first_ref, out_ref, top_ref):
+    grads = grads_for(*core_and_y(place_ref), grads_ref)
     best = first_ref[...]
     for start in range(0, out_ref.shape[1], TILE):
         where = slice(start, start + TILE)
@@ -97,7 +125,8 @@
     top_ref[...] = best
 
 
-def add_and_cut(parts_ref, out_ref):
+def add_and_cut(place_ref, parts_ref, out_ref):
+    y = core_and_y(place_ref)[1]
     rows = parts_ref.shape[1]
 
     def total(tile):
@@ -110,16 +139,17 @@
     for pair in range(out_ref.shape[0] // 2):
         middle = total(3 * pair + 1)
         for odd in range(2):
-            out_ref[2 * pair + odd, :rows] = total(3 * pair + 2 * odd).astype(BF16)
-            out_ref[2 * pair + odd, rows:] = fold(middle, odd).astype(BF16)
+            slot = slot_of(2 * pair + odd, y)
+            out_ref[slot, :rows] = total(3 * pair + 2 * odd).astype(BF16)
+            out_ref[slot, rows:] = fold(middle, odd).astype(BF16)
 
 
 def adam_step(
-    devices, core_ref, range_ref, summed_ref, top_ref, master_ref, moment_ref, second_ref,
+    devices, place_ref, range_ref, summed_ref, top_ref, master_ref, moment_ref, second_ref,
     master_out, second_out, moment_out, sent_out,
 ):
     rows = master_ref.shape[0]
-    is_even = core_ref[0] == 0
+    is_even = core_and_y(place_ref)[0] == 0
     own, tail = summed_ref[:rows], summed_ref[rows:]
     middle = unfold(tail, tail)
     gradient = jnp.where(
@@ -170,13 +200,13 @@
 
 
 def scale_weights(
-    core_ref, tops_ref, own_ref, other_ref, moment_ref,
+    place_ref, tops_ref, own_ref, other_ref, moment_ref,
     weight_out, moment_out, moment_span_out, weight_span_out, grad_span_out, span_ref,
 ):
     rows = weight_out.shape[0]
     packed = rows + rows // 2
     step = pl.program_id(0)
-    is_even = core_ref[0] == 0
+    is_even = core_and_y(place_ref)[0] == 0
 
     @pl.when(step == 0)
     def _():
@@ -190,11 +220,11 @@
         moment_span_out[0] = jnp.max(spans[1:2])
         weight_span_out[0] = jnp.max(spans[2:3])
 
-    span = span_ref[2:3]
+    scale = 1.0 / span_ref[2:3]
     for place in range((own_ref.shape[1] - TOP_ROWS) // packed):
         where = slice(place * packed, (place + 1) * packed)
-        own = own_ref[step, where].astype(F32) / span
-        other = other_ref[step, where].astype(F32) / span
+        own = own_ref[step, where].astype(F32) * scale
+        other = other_ref[step, where].astype(F32) * scale
         even, odd = jnp.where(is_even, own, other), jnp.where(is_even, other, own)
         start = 3 * LANES * place
         weight_out[:, start : start + LANES] = even[:rows].astype(BF16)
@@ -207,8 +237,8 @@
     rows, width = master.shape
     packed = rows + rows // 2
     sent_rows = packed + TOP_ROWS
-    core = lax.axis_index("core").reshape(1)
-    output_grads, core = lax.optimization_barrier((output_grads, core))
+    place = lax.axis_index(("core", "y")).reshape(1)
+    output_grads, place = lax.optimization_barrier((output_grads, place))
     swap = [(0, 1), (1, 0)]
 
     tokens, columns = output_grads.shape
@@ -219,9 +249,9 @@
         out_specs=VMEM,
         compiler_params=grant(4),
     )(output_grads.T)
-    grads = lax.all_to_all(grads, "y", 0, 0, tiled=True).reshape(cores, -1, tokens)
+    grads = lax.all_to_all(grads, "y", 0, 0, tiled=True)
     product = (
-        jax.ShapeDtypeStruct((grads.shape[1], activations.shape[1]), BF16),
+        jax.ShapeDtypeStruct((xs * columns, activations.shape[1]), BF16),
         jax.ShapeDtypeStruct((8, LANES), F32),
     )
     value, top = pl.pallas_call(
@@ -230,7 +260,7 @@
         in_specs=[SMEM, VMEM, VMEM],
         out_specs=(VMEM, VMEM),
         compiler_params=grant(12),
-    )(core, grads, activations)
+    )(place, grads, activations)
 
     value = lax.ppermute(value, "core", swap)
     value, top = pl.pallas_call(
@@ -239,24 +269,24 @@
         in_specs=[SMEM] + [VMEM] * 4,
         out_specs=(VMEM, VMEM),
         compiler_params=grant(12),
-    )(core, grads, activations, value, top)
+    )(place, grads, activations, value, top)
     value = lax.all_to_all(value.reshape(xs, rows, -1), "x", 0, 0, tiled=True)
     value = pl.pallas_call(
         add_and_cut,
         out_shape=jax.ShapeDtypeStruct((zs, packed, LANES), BF16),
-        in_specs=[VMEM],
+        in_specs=[SMEM, VMEM],
         out_specs=VMEM,
         compiler_params=grant(4),
-    )(value)
+    )(place, value)
     value = lax.all_to_all(value, "z", 0, 0, tiled=True)
     value = jnp.sum(value.astype(F32), axis=0)
     route = []
     for x in range(xs):
-        for z in range(zs):
-            for half in range(cores):
-                for y in range(ys):
-                    source = ((x * zs + z) * cores + half) * ys + y
-                    route.append((source, (y * zs + z) * ys + half * xs + x))
+        for half in range(cores):
+            for y in range(ys):
+                for feature in range(zs):
+                    source = ((x * zs + slot_of(feature, y)) * cores + half) * ys + y
+                    route.append((source, (y * zs + feature) * ys + columns_of(half, x, y)))
     value = lax.ppermute(value, DEVICE, route)
 
     block = jax.ShapeDtypeStruct((rows, width), F32)
@@ -266,7 +296,7 @@
         in_specs=[SMEM, SMEM] + [VMEM] * 5,
         out_specs=(VMEM,) * 4,
         compiler_params=grant(4),
-    )(core, moment_range, value, top, master, moment_q, second_moment)
+    )(place, moment_range, value, top, master, moment_q, second_moment)
 
     held = lax.all_to_all(held, "z", 0, 0, tiled=True)
     held = pl.pallas_call(
@@ -308,7 +338,7 @@
         ),
         scratch_shapes=[pltpu.VMEM((8, LANES), F32)],
         compiler_params=grant(8),
-    )(core, tops, held, other, moment)
+    )(place, tops, held, other, moment)
     return master_new, moment_q_new, moment_span, second_new, weight_q, weight_span, grad_span
 
 

time: 137 us -> 135 us (0.985)
  starting transfers between devices: 19.2 us -> 14.7 us
  waiting for transfers between devices: 3.35 us -> 5 us
    ppermute x1, starting transfers between devices: 8.29 us -> 3.82 us  [on_device(): other = lax.ppermute(held, 'core', swap)]
    ppermute x1, waiting for transfers between devices: 1.46 us -> 3.1 us  [on_device(): value = lax.ppermute(value, DEVICE, route)]
    all_to_all x1, blocking collectives: 10.3 us -> 11.7 us  [on_device(): tops = lax.all_to_all(tops, ('core', 'y'), 0, 0, tiled=True)]
where the time goes in v5:
time: 135 us
  blocking collectives  107 us (79%)
  starting transfers between devices  14.7 us (11%)
  Pallas kernels  5.11 us (4%)
  waiting for transfers between devices  5 us (4%)
  between operations  1.36 us (1%)
    all_to_all x1, blocking collectives, on_device(): grads = lax.all_to_all(grads, 'y', 0, 0, tiled=True)  33.4 us
    all_to_all x1, blocking collectives, on_device(): value = lax.all_to_all(value, 'z', 0, 0, tiled=True)  18.5 us
    all_to_all x1, blocking collectives, on_device(): held = lax.all_to_all(held, 'z', 0, 0, tiled=True)  16.2 us
    all_to_all x1, blocking collectives, on_device(): value = lax.all_to_all(value.reshape(xs, rows, -1), 'x', 0, 0, tiled=True)  15.2 us
    all_gather x1, blocking collectives, on_device(): held = lax.all_gather(held, 'x')  12.3 us
    all_to_all x1, blocking collectives, on_device(): tops = lax.all_to_all(tops, ('core', 'y'), 0, 0, tiled=True)  11.7 us
    ppermute x1, starting transfers between devices, on_device(): value = lax.ppermute(value, 'core', swap)  5.63 us
    ppermute x1, starting transfers between devices, on_device(): value = lax.ppermute(value, DEVICE, route)  5.27 us
  transfers between devices with their start and end apart: 3, of which 2 were waited for; matrix products, arithmetic and copies ran while one was open for 0% of the time, Pallas kernels for 0%

profile of v5, /device:TPU:1, one launch (start us, length us, event | category | flops | bytes accessed | tf_op | source)
XLA Modules:
  0.0 134.7 jit_solution(16654150486185138674)
XLA Ops:
  0.6 0.0 copy-start
  0.6 0.0 copy-start.1
  0.7 1.0 copy-done.1
  1.7 0.1 shard_map.117
  1.8 33.4 %all_to_all.25.grads_ref = bf16[8,64,1024]{2,1,0:T(8,128)(2,1)S(1)} all-to-all(bf16[8,64,1024]{2,1,0:T(8,128)(2,1)S(1)} %shard_map.117), channel_id=1, replica_groups=mesh['x'=4,'z'=8,'core'=2,'y'=8] {'y'}, dimensions={0} | all-to-all | bytes 2097152 | tf_op jit(solution)/shard_map/all_to_all | solution.py:252
  35.2 0.0 copy-done
  35.2 1.0 shard_map.118
  36.2 5.6 %collective-permute-start = (bf16[256,1536]{1,0:T(8,128)(2,1)S(1)}, bf16[256,1536]{1,0:T(8,128)(2,1)S(1)}, u32[]{:S(2)}, u32[]{:S(2)}) collective-permute-start(bf16[256,1536]{1,0:T(8,128)(2,1)S(1)} %get-tuple-element.24), channel_id=1, source_target_pairs={{0,8},{8,0},{1,9},{9,1},{2,10},{10,2},{3,11},{11,3},{4,12},{12,4},... | collective-permute-start | bytes 2359304 | tf_op jit(solution)/shard_map/ppermute | solution.py:265
  41.9 1.9 %collective-permute-done.other_ref = bf16[256,1536]{1,0:T(8,128)(2,1)S(1)} collective-permute-done((bf16[256,1536]{1,0:T(8,128)(2,1)S(1)}, bf16[256,1536]{1,0:T(8,128)(2,1)S(1)}, u32[]{:S(2)}, u32[]{:S(2)}) %collective-permute-start) | collective-permute-done | bytes 786464 | tf_op jit(solution)/shard_map/ppermute | solution.py:265
  43.7 0.0 copy-start.2
  43.7 0.0 copy-start.3
  43.7 0.0 copy-start.4
  43.8 1.0 shard_map.119
  44.8 15.2 %all_to_all.26.parts_ref = bf16[4,64,1536]{2,1,0:T(8,128)(2,1)S(1)} all-to-all(bf16[4,64,1536]{2,1,0:T(8,128)(2,1)S(1)} %bitcast.7), channel_id=1, replica_groups=mesh['x'=4,'z'=8,'core'=2,'y'=8] {'x'}, dimensions={0} | all-to-all | bytes 1572864 | tf_op jit(solution)/shard_map/all_to_all | solution.py:273
  60.0 0.1 shard_map.120
  60.1 18.5 %all_to_all.27 = bf16[8,96,128]{2,1,0:T(8,128)(2,1)S(1)} all-to-all(bf16[8,96,128]{2,1,0:T(8,128)(2,1)S(1)} %shard_map.120), channel_id=1, replica_groups=mesh['x'=4,'z'=8,'core'=2,'y'=8] {'z'}, dimensions={0} | all-to-all | bytes 393216 | tf_op jit(solution)/shard_map/all_to_all | solution.py:281
  78.7 5.3 %collective-permute-start.1 = (f32[96,128]{1,0:T(8,128)S(1)}, f32[96,128]{1,0:T(8,128)S(1)}, u32[]{:S(2)}, u32[]{:S(2)}) collective-permute-start(f32[96,128]{1,0:T(8,128)S(1)} %convert_reduce_fusion), channel_id=1, source_target_pairs={{0,4},{112,12},{16,20},{96,28},{32,36},{80,44},{48,52},{64,60},{65... | collective-permute-start | bytes 147464 | tf_op jit(solution)/shard_map/ppermute | solution.py:290
  84.6 3.1 %collective-permute-done.1.summed_ref = f32[96,128]{1,0:T(8,128)S(1)} collective-permute-done((f32[96,128]{1,0:T(8,128)S(1)}, f32[96,128]{1,0:T(8,128)S(1)}, u32[]{:S(2)}, u32[]{:S(2)}) %collective-permute-start.1) | collective-permute-done | bytes 49184 | tf_op jit(solution)/shard_map/ppermute | solution.py:290
  87.7 0.0 copy-done.2
  87.7 0.0 copy-done.3
  87.7 0.0 copy-done.4
  87.7 0.8 shard_map.121
  88.5 16.2 %all_to_all.28.held_ref = bf16[8,112,128]{2,1,0:T(8,128)(2,1)S(1)} all-to-all(bf16[8,112,128]{2,1,0:T(8,128)(2,1)S(1)} %get-tuple-element.29), channel_id=1, replica_groups=mesh['x'=4,'z'=8,'core'=2,'y'=8] {'z'}, dimensions={0} | all-to-all | bytes 458752 | tf_op jit(solution)/shard_map/all_to_all | solution.py:301
  104.8 12.3 %all-gather = bf16[3136,128]{1,0:T(8,128)(2,1)S(1)} all-gather(bf16[784,128]{1,0:T(8,128)(2,1)S(1)} %shard_map.122), channel_id=2, replica_groups=mesh['x'=4,'z'=8,'core'=2,'y'=8] {'x'}, dimensions={0}, use_global_device_ids=true | all-gather | bytes 1003520 | tf_op jit(solution)/shard_map/all_gather | solution.py:309
  117.1 3.8 %collective-permute-start.2 = (bf16[4,784,128]{2,1,0:T(8,128)(2,1)S(1)}, bf16[4,784,128]{2,1,0:T(8,128)(2,1)S(1)}, u32[]{:S(2)}, u32[]{:S(2)}) collective-permute-start(bf16[4,784,128]{2,1,0:T(8,128)(2,1)S(1)} %bitcast.4), channel_id=1, source_target_pairs={{0,8},{8,0},{1,9},{9,1},{2,10},{10,2},{3,11},{11,3},{4,12},{12,4},... | collective-permute-start | bytes 2408456 | tf_op jit(solution)/shard_map/ppermute | solution.py:310
  121.0 11.7 %all_to_all.29.tops_ref = f32[16,8,128]{2,1,0:T(8,128)S(1)} all-to-all(f32[16,8,128]{2,1,0:T(8,128)S(1)} %shard_map.123), channel_id=1, replica_groups=mesh['x'=4,'z'=8,'core'=2,'y'=8] {'core','y'}, dimensions={0} | all-to-all | bytes 131072 | tf_op jit(solution)/shard_map/all_to_all | solution.py:318
  132.6 0.0 collective-permute-done.2.other_ref
  132.6 2.0 %shard_map.124 = (bf16[64,12288]{1,0:T(8,128)(2,1)}, bf16[64,192]{1,0:T(8,128)(2,1)}, f32[1]{0:T(128)}, f32[1]{0:T(128)}, f32[1]{0:T(128)}) custom-call(s32[1]{0:T(128)} %bitcast.place_ref, f32[16,8,128]{2,1,0:T(8,128)S(1)} %all_to_all.29.tops_ref, bf16[4,784,128]{2,1,0:T(8,128)(2,1)S(1)} %bitcast.6, ...), custom_call_target="tpu_custom_call" | custom-call | tf_op jit(solution)/shard_map/pallas_call | solution.py:321
  (3 shorter events, 0.1 us)
Async XLA Ops:
  0.6 34.6 %copy-start = (bf16[1024,1536]{1,0:T(8,128)(2,1)S(1)}, bf16[1024,1536]{1,0:T(8,128)(2,1)}, u32[]{:S(2)}) copy-start(bf16[1024,1536]{1,0:T(8,128)(2,1)} %activations_ref.3) | copy-start | bytes 9437188
  0.6 1.1 copy-start.1
  36.2 7.5 %collective-permute-start = (bf16[256,1536]{1,0:T(8,128)(2,1)S(1)}, bf16[256,1536]{1,0:T(8,128)(2,1)S(1)}, u32[]{:S(2)}, u32[]{:S(2)}) collective-permute-start(bf16[256,1536]{1,0:T(8,128)(2,1)S(1)} %get-tuple-element.24), channel_id=1, source_target_pairs={{0,8},{8,0},{1,9},{9,1},{2,10},{10,2},{3,11},{11,3},{4,12},{12,4},... | collective-permute-start | bytes 2359304 | tf_op jit(solution)/shard_map/ppermute | solution.py:265
  43.7 43.9 %copy-start.2 = (f32[64,192]{1,0:T(8,128)S(1)}, f32[64,192]{1,0:T(8,128)}, u32[]{:S(2)}) copy-start(f32[64,192]{1,0:T(8,128)} %master_ref.1) | copy-start | bytes 147460
  43.7 43.9 %copy-start.3 = (f32[64,192]{1,0:T(8,128)S(1)}, f32[64,192]{1,0:T(8,128)}, u32[]{:S(2)}) copy-start(f32[64,192]{1,0:T(8,128)} %second_ref.1) | copy-start | bytes 147460
  43.7 44.0 %copy-start.4 = (bf16[64,192]{1,0:T(8,128)(2,1)S(1)}, bf16[64,192]{1,0:T(8,128)(2,1)}, u32[]{:S(2)}) copy-start(bf16[64,192]{1,0:T(8,128)(2,1)} %moment_ref.1) | copy-start | bytes 73732
  78.7 9.0 %collective-permute-start.1 = (f32[96,128]{1,0:T(8,128)S(1)}, f32[96,128]{1,0:T(8,128)S(1)}, u32[]{:S(2)}, u32[]{:S(2)}) collective-permute-start(f32[96,128]{1,0:T(8,128)S(1)} %convert_reduce_fusion), channel_id=1, source_target_pairs={{0,4},{112,12},{16,20},{96,28},{32,36},{80,44},{48,52},{64,60},{65... | collective-permute-start | bytes 147464 | tf_op jit(solution)/shard_map/ppermute | solution.py:290
  117.1 15.5 %collective-permute-start.2 = (bf16[4,784,128]{2,1,0:T(8,128)(2,1)S(1)}, bf16[4,784,128]{2,1,0:T(8,128)(2,1)S(1)}, u32[]{:S(2)}, u32[]{:S(2)}) collective-permute-start(bf16[4,784,128]{2,1,0:T(8,128)(2,1)S(1)} %bitcast.4), channel_id=1, source_target_pairs={{0,8},{8,0},{1,9},{9,1},{2,10},{10,2},{3,11},{11,3},{4,12},{12,4},... | collective-permute-start | bytes 2408456 | tf_op jit(solution)/shard_map/ppermute | solution.py:310

commit v6 on v5

--- a/solution.py
+++ b/solution.py
@@ -23,6 +23,7 @@
 DEVICE = ("x", "z", "core", "y")
 SMEM = pl.BlockSpec(memory_space=pltpu.SMEM)
 VMEM = pl.BlockSpec(memory_space=pltpu.VMEM)
+HBM = pl.BlockSpec(memory_space=pltpu.HBM)
 MIB = 1024 * 1024
 
 
@@ -70,9 +71,15 @@
     return spread[:8] + spread[8:] + pltpu.roll(spread[:8], 4, 0)
 
 
-def copy_grads(grads_ref, out_ref):
-    for copy in range(out_ref.shape[0]):
-        out_ref[copy] = grads_ref[...]
+def copy_grads(grads_ref, out_ref, arrived):
+    copies = [
+        pltpu.make_async_copy(grads_ref, out_ref.at[copy], arrived.at[copy])
+        for copy in range(out_ref.shape[0])
+    ]
+    for copy in copies:
+        copy.start()
+    for copy in copies:
+        copy.wait()
 
 
 ABOVE = ((4, -1, 0, -2), (-3, 2, 1, 3))
@@ -144,8 +151,46 @@
             out_ref[slot, rows:] = fold(middle, odd).astype(BF16)
 
 
+def step_of(gradient, moment, second_moment, master):
+    moment = BETA_ONE * moment + (1.0 - BETA_ONE) * gradient
+    second_new = BETA_TWO * second_moment + (1.0 - BETA_TWO) * gradient * gradient
+    master_new = master - LEARN_RATE * (
+        moment / (jnp.sqrt(second_new) + ADAM_EPSILON) + DECAY_RATE * master
+    )
+    return moment, second_new, master_new
+
+
+def pack(value, is_even):
+    own = jnp.where(is_even, value[:, :LANES], value[:, HALF:])
+    middle = jnp.concatenate([value[:, LANES:], value[:, :HALF]], 1)
+    return own, jnp.where(is_even, fold(middle, False), fold(middle, True))
+
+
+def pack_state(place_ref, range_ref, moment_ref, second_ref, master_ref, out_ref):
+    is_even = core_and_y(place_ref)[0] == 0
+    rows = master_ref.shape[0]
+    moment = moment_ref[...].astype(F32) * range_ref[0]
+    for place, state in enumerate((moment, second_ref[...], master_ref[...])):
+        own, tail = pack(state, is_even)
+        out_ref[place, :rows] = own
+        out_ref[place, rows:] = tail
+
+
+def add_and_find_tops(devices, parts_ref, state_ref, top_ref, sum_out, tops_out):
+    total = parts_ref[0].astype(F32)
+    for part in range(1, parts_ref.shape[0]):
+        total += parts_ref[part].astype(F32)
+    sum_out[...] = total
+    moment, _, master_new = step_of(total / devices, state_ref[0], state_ref[1], state_ref[2])
+    row = lax.broadcasted_iota(jnp.int32, (8, LANES), 0)
+    tops = (largest(top_ref[...]), largest(moment), largest(master_new))
+    tops = jnp.where(row == 0, tops[0], jnp.where(row == 1, tops[1], tops[2]))
+    for copy in range(tops_out.shape[0]):
+        tops_out[copy] = tops
+
+
 def adam_step(
-    devices, place_ref, range_ref, summed_ref, top_ref, master_ref, moment_ref, second_ref,
+    devices, place_ref, range_ref, summed_ref, tops_ref, moment_ref, second_ref, master_ref,
     master_out, second_out, moment_out, sent_out,
 ):
     rows = master_ref.shape[0]
@@ -157,26 +202,18 @@
         jnp.concatenate([own, middle[:, :HALF]], 1),
         jnp.concatenate([middle[:, HALF:], own], 1),
     ) / devices
-    moment = (
-        BETA_ONE * (moment_ref[...].astype(F32) * range_ref[0]) + (1.0 - BETA_ONE) * gradient
-    )
-    second_new = BETA_TWO * second_ref[...] + (1.0 - BETA_TWO) * gradient * gradient
-    master = master_ref[...]
-    master_new = master - LEARN_RATE * (
-        moment / (jnp.sqrt(second_new) + ADAM_EPSILON) + DECAY_RATE * master
+    moment_out[...], second_out[...], master_new = step_of(
+        gradient, moment_ref[...].astype(F32) * range_ref[0], second_ref[...], master_ref[...]
     )
     master_out[...] = master_new
-    second_out[...] = second_new
-    moment_out[...] = moment
-    own = jnp.where(is_even, master_new[:, :LANES], master_new[:, HALF:]).astype(BF16)
-    middle = jnp.concatenate([master_new[:, LANES:], master_new[:, :HALF]], 1)
-    tail = jnp.where(is_even, fold(middle, False), fold(middle, True)).astype(BF16)
-    row = lax.broadcasted_iota(jnp.int32, (8, LANES), 0)
-    tops = (largest(top_ref[...]), largest(moment), largest(master_new))
-    spread = split(jnp.where(row == 0, tops[0], jnp.where(row == 1, tops[1], tops[2])))
+    own, tail = pack(master_new, is_even)
+    top = tops_ref[0]
+    for place in range(1, tops_ref.shape[0]):
+        top = jnp.maximum(top, tops_ref[place])
+    spread = split(top)
     for copy in range(sent_out.shape[0]):
-        sent_out[copy, :rows] = own
-        sent_out[copy, rows : rows + rows // 2] = tail
+        sent_out[copy, :rows] = own.astype(BF16)
+        sent_out[copy, rows : rows + rows // 2] = tail.astype(BF16)
         sent_out[copy, rows + rows // 2 :] = spread
 
 
@@ -190,17 +227,8 @@
     out_ref[held_ref.shape[0] * packed :] = split(best)
 
 
-def join_tops(held_ref, out_ref):
-    packed = held_ref.shape[1] - TOP_ROWS
-    best = joined(held_ref[0, packed:])
-    for x in range(1, held_ref.shape[0]):
-        best = jnp.maximum(best, joined(held_ref[x, packed:]))
-    for copy in range(out_ref.shape[0]):
-        out_ref[copy] = best
-
-
 def scale_weights(
-    place_ref, tops_ref, own_ref, other_ref, moment_ref,
+    place_ref, own_ref, other_ref, moment_ref,
     weight_out, moment_out, moment_span_out, weight_span_out, grad_span_out, span_ref,
 ):
     rows = weight_out.shape[0]
@@ -210,9 +238,10 @@
 
     @pl.when(step == 0)
     def _():
-        best = tops_ref[0]
-        for place in range(1, tops_ref.shape[0]):
-            best = jnp.maximum(best, tops_ref[place])
+        best = jnp.zeros((8, LANES), F32)
+        for held_ref in (own_ref, other_ref):
+            for x in range(held_ref.shape[0]):
+                best = jnp.maximum(best, joined(held_ref[x, held_ref.shape[1] - TOP_ROWS :]))
         spans = best + EPSILON
         span_ref[...] = spans
         moment_out[...] = (moment_ref[...] / largest(spans[1:2])).astype(BF16)
@@ -241,15 +270,33 @@
     output_grads, place = lax.optimization_barrier((output_grads, place))
     swap = [(0, 1), (1, 0)]
 
+    route = []
+    for x in range(xs):
+        for half in range(cores):
+            for y in range(ys):
+                for feature in range(zs):
+                    source = ((x * zs + slot_of(feature, y)) * cores + half) * ys + y
+                    route.append((source, (y * zs + feature) * ys + columns_of(half, x, y)))
+    state = pl.pallas_call(
+        pack_state,
+        out_shape=jax.ShapeDtypeStruct((3, packed, LANES), F32),
+        in_specs=[SMEM, SMEM] + [VMEM] * 3,
+        out_specs=VMEM,
+        compiler_params=grant(4),
+    )(place, moment_range, moment_q, second_moment, master)
+    state = lax.ppermute(state, DEVICE, [(owner, source) for source, owner in route])
+
     tokens, columns = output_grads.shape
     grads = pl.pallas_call(
         copy_grads,
         out_shape=jax.ShapeDtypeStruct((ys, columns, tokens), BF16),
-        in_specs=[VMEM],
-        out_specs=VMEM,
-        compiler_params=grant(4),
+        in_specs=[HBM],
+        out_specs=HBM,
+        scratch_shapes=[pltpu.SemaphoreType.DMA((ys,))],
+        compiler_params=grant(60),
     )(output_grads.T)
     grads = lax.all_to_all(grads, "y", 0, 0, tiled=True)
+    grads, state = lax.optimization_barrier((grads, state))
     product = (
         jax.ShapeDtypeStruct((xs * columns, activations.shape[1]), BF16),
         jax.ShapeDtypeStruct((8, LANES), F32),
@@ -279,16 +326,19 @@
         compiler_params=grant(4),
     )(place, value)
     value = lax.all_to_all(value, "z", 0, 0, tiled=True)
-    value = jnp.sum(value.astype(F32), axis=0)
-    route = []
-    for x in range(xs):
-        for half in range(cores):
-            for y in range(ys):
-                for feature in range(zs):
-                    source = ((x * zs + slot_of(feature, y)) * cores + half) * ys + y
-                    route.append((source, (y * zs + feature) * ys + columns_of(half, x, y)))
+    value, tops = pl.pallas_call(
+        functools.partial(add_and_find_tops, xs * zs * cores),
+        out_shape=(
+            jax.ShapeDtypeStruct((packed, LANES), F32),
+            jax.ShapeDtypeStruct((ys, 8, LANES), F32),
+        ),
+        in_specs=[VMEM] * 3,
+        out_specs=(VMEM, VMEM),
+        compiler_params=grant(4),
+    )(value, state, top)
+
     value = lax.ppermute(value, DEVICE, route)
-
+    tops = lax.all_to_all(tops, "y", 0, 0, tiled=True)
     block = jax.ShapeDtypeStruct((rows, width), F32)
     master_new, second_new, moment, held = pl.pallas_call(
         functools.partial(adam_step, xs * zs * cores),
@@ -296,7 +346,7 @@
         in_specs=[SMEM, SMEM] + [VMEM] * 5,
         out_specs=(VMEM,) * 4,
         compiler_params=grant(4),
-    )(place, moment_range, value, top, master, moment_q, second_moment)
+    )(place, moment_range, value, tops, moment_q, second_moment, master)
 
     held = lax.all_to_all(held, "z", 0, 0, tiled=True)
     held = pl.pallas_call(
@@ -308,15 +358,6 @@
     )(held)
     held = lax.all_gather(held, "x")
     other = lax.ppermute(held, "core", swap)
-    tops = pl.pallas_call(
-        join_tops,
-        out_shape=jax.ShapeDtypeStruct((cores * ys, 8, LANES), F32),
-        in_specs=[VMEM],
-        out_specs=VMEM,
-        compiler_params=grant(4),
-    )(held)
-    tops = lax.all_to_all(tops, ("core", "y"), 0, 0, tiled=True)
-
     one = jax.ShapeDtypeStruct((1,), F32)
     weight_q, moment_q_new, moment_span, weight_span, grad_span = pl.pallas_call(
         scale_weights,
@@ -328,7 +369,7 @@
             one,
             one,
         ),
-        in_specs=[SMEM, VMEM, VMEM, VMEM, VMEM],
+        in_specs=[SMEM, VMEM, VMEM, VMEM],
         out_specs=(
             pl.BlockSpec((rows, width * zs * cores), lambda i: (0, i)),
             VMEM,
@@ -338,7 +379,7 @@
         ),
         scratch_shapes=[pltpu.VMEM((8, LANES), F32)],
         compiler_params=grant(8),
-    )(place, tops, held, other, moment)
+    )(place, held, other, moment)
     return master_new, moment_q_new, moment_span, second_new, weight_q, weight_span, grad_span
 
 

time: 135 us -> 181 us (1.34)
  blocking collectives: 107 us -> 58 us
  Pallas kernels: 5.11 us -> 41.4 us
  starting transfers between devices: 14.7 us -> 47.1 us
  waiting for transfers between devices: 5 us -> 31.1 us
    all_to_all x2 -> x0, blocking collectives: 45.1 us -> none  [the longest x1 33.4 us: on_device(): grads = lax.all_to_all(grads, 'y', 0, 0, tiled=True)]
    pallas_call x1, Pallas kernels: 0.07 us -> 32.9 us  [on_device(): pl.pallas_call(copy_grads, out_shape=jax.ShapeDtypeStruct((ys, columns, t...]
    ppermute x0 -> x1, waiting for transfers between devices: none -> 25.8 us  [on_device(): lax.ppermute(state, DEVICE, [(owner, source) for source, owner in route])]
    all_to_all x0 -> x2, starting transfers between devices: none -> 17.4 us  [the longest x1 9.7 us: on_device(): tops = lax.all_to_all(tops, 'y', 0, 0, tiled=True)]
    ppermute x0 -> x1, starting transfers between devices: none -> 14 us  [on_device(): lax.ppermute(state, DEVICE, [(owner, source) for source, owner in route])]
    ppermute x1, starting transfers between devices: 5.27 us -> 9.77 us  [on_device(): value = lax.ppermute(value, DEVICE, route)]
    ppermute x1, starting transfers between devices: 5.63 us -> 1.92 us  [on_device(): value = lax.ppermute(value, 'core', swap)]
    all_to_all x1, blocking collectives: 16.2 us -> 13.8 us  [on_device(): held = lax.all_to_all(held, 'z', 0, 0, tiled=True)]
  transfers between devices with their start and end apart: 3 -> 6, of which waited for: 2 -> 4; matrix products, arithmetic and copies ran while one was open for 0% -> 0% of each run, Pallas kernels for 0% -> 0%
where the time goes in v6:
time: 181 us; the launch traced here: 179 us
  blocking collectives  58 us (32%)
  starting transfers between devices  47.1 us (26%)
  Pallas kernels  41.4 us (23%)
  waiting for transfers between devices  31.1 us (17%)
    pallas_call x1, Pallas kernels, on_device(): pl.pallas_call(copy_grads, out_shape=jax.ShapeDtypeStruct((ys, columns, t...  32.9 us
    ppermute x1, waiting for transfers between devices, on_device(): lax.ppermute(state, DEVICE, [(owner, source) for source, owner in route])  25.8 us
    all_to_all x1, blocking collectives, on_device(): value = lax.all_to_all(value, 'z', 0, 0, tiled=True)  16.6 us
    all_to_all x1, blocking collectives, on_device(): value = lax.all_to_all(value.reshape(xs, rows, -1), 'x', 0, 0, tiled=True)  14.4 us
    ppermute x1, starting transfers between devices, on_device(): lax.ppermute(state, DEVICE, [(owner, source) for source, owner in route])  14 us
    all_to_all x1, blocking collectives, on_device(): held = lax.all_to_all(held, 'z', 0, 0, tiled=True)  13.8 us
    all_gather x1, blocking collectives, on_device(): held = lax.all_gather(held, 'x')  13.1 us
    ppermute x1, starting transfers between devices, on_device(): value = lax.ppermute(value, DEVICE, route)  9.77 us
  transfers between devices with their start and end apart: 6, of which 4 were waited for; matrix products, arithmetic and copies ran while one was open for 0% of the time, Pallas kernels for 0%

profile of v6, /device:TPU:1, one launch (start us, length us, event | category | flops | bytes accessed | tf_op | source)
XLA Modules:
  0.0 178.9 jit_solution(9037840833880882616)
XLA Ops:
  0.6 0.0 copy-start.1
  0.6 0.0 copy-start.3
  0.7 0.0 copy-start.2
  0.7 0.0 copy-start
  0.7 32.9 %shard_map.117 = bf16[8,64,1024]{2,1,0:T(8,128)(2,1)} custom-call(bf16[64,1024]{1,0:T(8,128)(2,1)} %bitcast.7), custom_call_target="tpu_custom_call" | custom-call | tf_op jit(solution)/shard_map/pallas_call | solution.py:290
  33.6 7.7 %all-to-all-start = ((bf16[8,64,1024]{2,1,0:T(8,128)(2,1)}), bf16[8,64,1024]{2,1,0:T(8,128)(2,1)}, u32[]{:S(2)}, u32[]{:S(2)}) async-start(bf16[8,64,1024]{2,1,0:T(8,128)(2,1)} %shard_map.117), calls=%async_computation | async-start | bytes 2097152 | tf_op jit(solution)/shard_map/all_to_all | solution.py:298
  41.9 0.0 copy-done.1
  42.0 0.0 copy-done.3
  42.0 0.0 copy-done.2
  42.0 0.2 shard_map.118
  42.1 14.0 %collective-permute-start = (f32[3,96,128]{2,1,0:T(8,128)S(1)}, f32[3,96,128]{2,1,0:T(8,128)S(1)}, u32[]{:S(2)}, u32[]{:S(2)}) collective-permute-start(f32[3,96,128]{2,1,0:T(8,128)S(1)} %shard_map.118), channel_id=1, source_target_pairs={{4,0},{12,112},{20,16},{28,96},{36,32},{44,80},{52,48},{60,64},{69... | collective-permute-start | bytes 442376 | tf_op jit(solution)/shard_map/ppermute | solution.py:287
  56.1 25.8 %collective-permute-done.state_ref = f32[3,96,128]{2,1,0:T(8,128)S(1)} collective-permute-done((f32[3,96,128]{2,1,0:T(8,128)S(1)}, f32[3,96,128]{2,1,0:T(8,128)S(1)}, u32[]{:S(2)}, u32[]{:S(2)}) %collective-permute-start) | collective-permute-done | bytes 147488 | tf_op jit(solution)/shard_map/ppermute | solution.py:287
  81.9 0.0 all-to-all-done.grads_ref
  81.9 0.0 copy-done
  81.9 2.2 %shard_map.119 = (bf16[256,1536]{1,0:T(8,128)(2,1)S(1)}, f32[8,128]{1,0:T(8,128)S(1)}) custom-call(s32[1]{0:T(128)} %bitcast.place_ref, bf16[8,64,1024]{2,1,0:T(8,128)(2,1)} %all-to-all-done.grads_ref, bf16[1024,1536]{1,0:T(8,128)(2,1)S(1)} %copy-done), custom_call_target="tpu_custom_call" | custom-call | tf_op jit(solution)/shard_map/pallas_call | solution.py:304
  84.1 1.9 %collective-permute-start.1 = (bf16[256,1536]{1,0:T(8,128)(2,1)S(1)}, bf16[256,1536]{1,0:T(8,128)(2,1)S(1)}, u32[]{:S(2)}, u32[]{:S(2)}) collective-permute-start(bf16[256,1536]{1,0:T(8,128)(2,1)S(1)} %get-tuple-element.29), channel_id=1, source_target_pairs={{0,8},{8,0},{1,9},{9,1},{2,10},{10,2},{3,11},{11,3},{4,12},{12,4},... | collective-permute-start | bytes 2359304 | tf_op jit(solution)/shard_map/ppermute | solution.py:312
  86.0 2.3 %collective-permute-done.1.other_ref = bf16[256,1536]{1,0:T(8,128)(2,1)S(1)} collective-permute-done((bf16[256,1536]{1,0:T(8,128)(2,1)S(1)}, bf16[256,1536]{1,0:T(8,128)(2,1)S(1)}, u32[]{:S(2)}, u32[]{:S(2)}) %collective-permute-start.1) | collective-permute-done | bytes 786464 | tf_op jit(solution)/shard_map/ppermute | solution.py:312
  88.3 2.2 %shard_map.120 = (bf16[256,1536]{1,0:T(8,128)(2,1)S(1)}, f32[8,128]{1,0:T(8,128)S(1)}) custom-call(s32[1]{0:T(128)} %bitcast.place_ref, bf16[8,64,1024]{2,1,0:T(8,128)(2,1)} %all-to-all-done.grads_ref, bf16[1024,1536]{1,0:T(8,128)(2,1)S(1)} %copy-done, bf16[256,1536]{1,0:T(8,128)(2,1)S(1)} %collective-permute-done.1.other_ref, ...), custom_call_target="tpu_custom_call" | custom-call | tf_op jit(solution)/shard_map/pallas_call | solution.py:313
  90.5 14.4 %all_to_all.25.parts_ref = bf16[4,64,1536]{2,1,0:T(8,128)(2,1)S(1)} all-to-all(bf16[4,64,1536]{2,1,0:T(8,128)(2,1)S(1)} %bitcast.6), channel_id=1, replica_groups=mesh['x'=4,'z'=8,'core'=2,'y'=8] {'x'}, dimensions={0} | all-to-all | bytes 1572864 | tf_op jit(solution)/shard_map/all_to_all | solution.py:320
  104.9 0.1 shard_map.121
  105.0 16.6 %all_to_all.26.parts_ref = bf16[8,96,128]{2,1,0:T(8,128)(2,1)S(1)} all-to-all(bf16[8,96,128]{2,1,0:T(8,128)(2,1)S(1)} %shard_map.121), channel_id=1, replica_groups=mesh['x'=4,'z'=8,'core'=2,'y'=8] {'z'}, dimensions={0} | all-to-all | bytes 393216 | tf_op jit(solution)/shard_map/all_to_all | solution.py:328
  121.7 0.8 shard_map.122
  122.4 9.7 %all-to-all-start.3 = ((f32[8,8,128]{2,1,0:T(8,128)}), f32[8,8,128]{2,1,0:T(8,128)S(1)}, u32[]{:S(2)}, u32[]{:S(2)}) async-start(f32[8,8,128]{2,1,0:T(8,128)} %get-tuple-element.35), calls=%async_computation.3 | async-start | bytes 65536 | tf_op jit(solution)/shard_map/all_to_all | solution.py:341
  132.1 9.8 %collective-permute-start.2 = (f32[96,128]{1,0:T(8,128)S(1)}, f32[96,128]{1,0:T(8,128)S(1)}, u32[]{:S(2)}, u32[]{:S(2)}) collective-permute-start(f32[96,128]{1,0:T(8,128)S(1)} %get-tuple-element.34), channel_id=1, source_target_pairs={{0,4},{112,12},{16,20},{96,28},{32,36},{80,44},{48,52},{64,60},{65... | collective-permute-start | bytes 147464 | tf_op jit(solution)/shard_map/ppermute | solution.py:340
  141.9 1.2 collective-permute-done.2.summed_ref
  143.1 0.0 all-to-all-done.3.tops_ref
  143.1 0.9 shard_map.123
  144.0 13.8 %all_to_all.27.held_ref = bf16[8,112,128]{2,1,0:T(8,128)(2,1)S(1)} all-to-all(bf16[8,112,128]{2,1,0:T(8,128)(2,1)S(1)} %get-tuple-element.37), channel_id=1, replica_groups=mesh['x'=4,'z'=8,'core'=2,'y'=8] {'z'}, dimensions={0} | all-to-all | bytes 458752 | tf_op jit(solution)/shard_map/all_to_all | solution.py:351
  157.8 13.1 %all-gather = bf16[3136,128]{1,0:T(8,128)(2,1)S(1)} all-gather(bf16[784,128]{1,0:T(8,128)(2,1)S(1)} %shard_map.124), channel_id=2, replica_groups=mesh['x'=4,'z'=8,'core'=2,'y'=8] {'x'}, dimensions={0}, use_global_device_ids=true | all-gather | bytes 1003520 | tf_op jit(solution)/shard_map/all_gather | solution.py:359
  170.9 4.1 %collective-permute-start.3 = (bf16[4,784,128]{2,1,0:T(8,128)(2,1)S(1)}, bf16[4,784,128]{2,1,0:T(8,128)(2,1)S(1)}, u32[]{:S(2)}, u32[]{:S(2)}) collective-permute-start(bf16[4,784,128]{2,1,0:T(8,128)(2,1)S(1)} %bitcast.4), channel_id=1, source_target_pairs={{0,8},{8,0},{1,9},{9,1},{2,10},{10,2},{3,11},{11,3},{4,12},{12,4},... | collective-permute-start | bytes 2408456 | tf_op jit(solution)/shard_map/ppermute | solution.py:360
  175.0 1.9 %collective-permute-done.3.other_ref = bf16[4,784,128]{2,1,0:T(8,128)(2,1)S(1)} collective-permute-done((bf16[4,784,128]{2,1,0:T(8,128)(2,1)S(1)}, bf16[4,784,128]{2,1,0:T(8,128)(2,1)S(1)}, u32[]{:S(2)}, u32[]{:S(2)}) %collective-permute-start.3) | collective-permute-done | bytes 802848 | tf_op jit(solution)/shard_map/ppermute | solution.py:360
  176.9 2.0 %shard_map.125 = (bf16[64,12288]{1,0:T(8,128)(2,1)}, bf16[64,192]{1,0:T(8,128)(2,1)}, f32[1]{0:T(128)}, f32[1]{0:T(128)}, f32[1]{0:T(128)}) custom-call(s32[1]{0:T(128)} %bitcast.place_ref, bf16[4,784,128]{2,1,0:T(8,128)(2,1)S(1)} %bitcast.5, bf16[4,784,128]{2,1,0:T(8,128)(2,1)S(1)} %collective-permute-done.3.other_ref, ...), custom_call_target="tpu_custom_call" | custom-call | tf_op jit(solution)/shard_map/pallas_call | solution.py:362
  (1 shorter events, 0.0 us)
Async XLA Ops:
  0.6 41.3 %copy-start.1 = (f32[64,192]{1,0:T(8,128)S(1)}, f32[64,192]{1,0:T(8,128)}, u32[]{:S(2)}) copy-start(f32[64,192]{1,0:T(8,128)} %second_ref.3) | copy-start | bytes 147460
  0.6 41.3 %copy-start.3 = (bf16[64,192]{1,0:T(8,128)(2,1)S(1)}, bf16[64,192]{1,0:T(8,128)(2,1)}, u32[]{:S(2)}) copy-start(bf16[64,192]{1,0:T(8,128)(2,1)} %moment_ref.3) | copy-start | bytes 73732
  0.7 41.3 %copy-start.2 = (f32[64,192]{1,0:T(8,128)S(1)}, f32[64,192]{1,0:T(8,128)}, u32[]{:S(2)}) copy-start(f32[64,192]{1,0:T(8,128)} %master_ref.3) | copy-start | bytes 147460
  0.7 81.2 %copy-start = (bf16[1024,1536]{1,0:T(8,128)(2,1)S(1)}, bf16[1024,1536]{1,0:T(8,128)(2,1)}, u32[]{:S(2)}) copy-start(bf16[1024,1536]{1,0:T(8,128)(2,1)} %activations_ref.3) | copy-start | bytes 9437188
  33.6 48.3 %all-to-all-start = ((bf16[8,64,1024]{2,1,0:T(8,128)(2,1)}), bf16[8,64,1024]{2,1,0:T(8,128)(2,1)}, u32[]{:S(2)}, u32[]{:S(2)}) async-start(bf16[8,64,1024]{2,1,0:T(8,128)(2,1)} %shard_map.117), calls=%async_computation | async-start | bytes 2097152 | tf_op jit(solution)/shard_map/all_to_all | solution.py:298
  42.1 39.7 %collective-permute-start = (f32[3,96,128]{2,1,0:T(8,128)S(1)}, f32[3,96,128]{2,1,0:T(8,128)S(1)}, u32[]{:S(2)}, u32[]{:S(2)}) collective-permute-start(f32[3,96,128]{2,1,0:T(8,128)S(1)} %shard_map.118), channel_id=1, source_target_pairs={{4,0},{12,112},{20,16},{28,96},{36,32},{44,80},{52,48},{60,64},{69... | collective-permute-start | bytes 442376 | tf_op jit(solution)/shard_map/ppermute | solution.py:287
  84.1 4.2 %collective-permute-start.1 = (bf16[256,1536]{1,0:T(8,128)(2,1)S(1)}, bf16[256,1536]{1,0:T(8,128)(2,1)S(1)}, u32[]{:S(2)}, u32[]{:S(2)}) collective-permute-start(bf16[256,1536]{1,0:T(8,128)(2,1)S(1)} %get-tuple-element.29), channel_id=1, source_target_pairs={{0,8},{8,0},{1,9},{9,1},{2,10},{10,2},{3,11},{11,3},{4,12},{12,4},... | collective-permute-start | bytes 2359304 | tf_op jit(solution)/shard_map/ppermute | solution.py:312
  122.4 20.6 %all-to-all-start.3 = ((f32[8,8,128]{2,1,0:T(8,128)}), f32[8,8,128]{2,1,0:T(8,128)S(1)}, u32[]{:S(2)}, u32[]{:S(2)}) async-start(f32[8,8,128]{2,1,0:T(8,128)} %get-tuple-element.35), calls=%async_computation.3 | async-start | bytes 65536 | tf_op jit(solution)/shard_map/all_to_all | solution.py:341
  132.1 10.9 %collective-permute-start.2 = (f32[96,128]{1,0:T(8,128)S(1)}, f32[96,128]{1,0:T(8,128)S(1)}, u32[]{:S(2)}, u32[]{:S(2)}) collective-permute-start(f32[96,128]{1,0:T(8,128)S(1)} %get-tuple-element.34), channel_id=1, source_target_pairs={{0,4},{112,12},{16,20},{96,28},{32,36},{80,44},{48,52},{64,60},{65... | collective-permute-start | bytes 147464 | tf_op jit(solution)/shard_map/ppermute | solution.py:340
  170.9 6.0 %collective-permute-start.3 = (bf16[4,784,128]{2,1,0:T(8,128)(2,1)S(1)}, bf16[4,784,128]{2,1,0:T(8,128)(2,1)S(1)}, u32[]{:S(2)}, u32[]{:S(2)}) collective-permute-start(bf16[4,784,128]{2,1,0:T(8,128)(2,1)S(1)} %bitcast.4), channel_id=1, source_target_pairs={{0,8},{8,0},{1,9},{9,1},{2,10},{10,2},{3,11},{11,3},{4,12},{12,4},... | collective-permute-start | bytes 2408456 | tf_op jit(solution)/shard_map/ppermute | solution.py:360

commit v7 on v5

--- a/solution.py
+++ b/solution.py
@@ -70,23 +70,16 @@
     return spread[:8] + spread[8:] + pltpu.roll(spread[:8], 4, 0)
 
 
-def copy_grads(grads_ref, out_ref):
-    for copy in range(out_ref.shape[0]):
-        out_ref[copy] = grads_ref[...]
-
-
-ABOVE = ((4, -1, 0, -2), (-3, 2, 1, 3))
-
-
-def columns_of(core, x, y):
-    place = (x - y // 2) % 4
-    if isinstance(y, int):
-        return (y + ABOVE[core][place]) % 8
-    above = 0
-    for half in range(2):
-        for step in range(4):
-            above = jnp.where((core == half) & (place == step), ABOVE[half][step], above)
-    return (y + above + 8) % 8
+ABOVE = (((4, 0), (-1, 3)), ((2, -2), (-3, 1)))
+
+
+def block_of(core, odd, which, y):
+    place = (core + odd) % 2 + 2 * which
+    if isinstance(core, int):
+        above = ABOVE[core][odd][which]
+    else:
+        above = jnp.where(core == 0, ABOVE[0][odd][which], ABOVE[1][odd][which])
+    return (place + y // 2) % 4, (y + above + 8) % 8
 
 
 def slot_of(feature, y):
@@ -98,31 +91,45 @@
     return place_ref[0] // 8, place_ref[0] % 8
 
 
-def grads_for(core, y, grads_ref):
-    return jnp.concatenate([grads_ref[columns_of(core, x, y)] for x in range(4)], 0)
-
-
-def multiply_for_other(place_ref, grads_ref, activations_ref, out_ref, top_ref):
-    core, y = core_and_y(place_ref)
-    grads = grads_for(1 - core, y, grads_ref)
-    best = None
-    for start in range(0, out_ref.shape[1], TILE):
+def multiply(grads, activations_ref, best, *outs):
+    grads = jnp.concatenate(grads, 0)
+    rows = outs[0].shape[1]
+    for start in range(0, activations_ref.shape[1], TILE):
         where = slice(start, start + TILE)
         value = jnp.dot(grads, activations_ref[:, where], preferred_element_type=F32)
-        out_ref[:, where] = value.astype(BF16)
+        first = 0
+        for out_ref in outs:
+            for block in range(out_ref.shape[0]):
+                out_ref[block, :, where] = value[first : first + rows].astype(out_ref.dtype)
+                first += rows
         best = magnitude(value, best)
-    top_ref[...] = best
-
-
-def multiply_and_add(place_ref, grads_ref, activations_ref, other_ref, first_ref, out_ref, top_ref):
-    grads = grads_for(*core_and_y(place_ref), grads_ref)
-    best = first_ref[...]
-    for start in range(0, out_ref.shape[1], TILE):
-        where = slice(start, start + TILE)
-        value = jnp.dot(grads, activations_ref[:, where], preferred_element_type=F32)
-        out_ref[:, where] = (value + other_ref[:, where].astype(F32)).astype(BF16)
-        best = magnitude(value, best)
-    top_ref[...] = best
+    return best
+
+
+def multiply_even(place_ref, grads_ref, activations_ref, other_out, own_out, top_out):
+    core, y = core_and_y(place_ref)
+    grads = []
+    for adder in (1 - core, core):
+        for which in range(2):
+            grads.append(grads_ref[block_of(adder, 0, which, y)[1] // 2])
+    top_out[...] = multiply(grads, activations_ref, None, other_out, own_out)
+
+
+def multiply_odd(of_other, place_ref, low_ref, high_ref, activations_ref, top_ref, out_ref, top_out):
+    core, y = core_and_y(place_ref)
+    grads = []
+    for which in range(2):
+        block = block_of(1 - core if of_other else core, 1, which, y)[1] // 2
+        grads.append(jnp.where(block < 2, low_ref[block % 2], high_ref[block % 2]))
+    top_out[...] = multiply(grads, activations_ref, top_ref[...], out_ref)
+
+
+def add_cores(place_ref, own_even_ref, own_odd_ref, other_even_ref, other_odd_ref, out_ref):
+    core, y = core_and_y(place_ref)
+    for odd, own_ref, other_ref in ((0, own_even_ref, other_even_ref), (1, own_odd_ref, other_odd_ref)):
+        for which in range(2):
+            x = block_of(core, odd, which, y)[0]
+            out_ref[x] = (own_ref[which] + other_ref[which].astype(F32)).astype(BF16)
 
 
 def add_and_cut(place_ref, parts_ref, out_ref):
@@ -242,35 +249,47 @@
     swap = [(0, 1), (1, 0)]
 
     tokens, columns = output_grads.shape
-    grads = pl.pallas_call(
-        copy_grads,
-        out_shape=jax.ShapeDtypeStruct((ys, columns, tokens), BF16),
-        in_specs=[VMEM],
-        out_specs=VMEM,
-        compiler_params=grant(4),
-    )(output_grads.T)
-    grads = lax.all_to_all(grads, "y", 0, 0, tiled=True)
-    product = (
-        jax.ShapeDtypeStruct((xs * columns, activations.shape[1]), BF16),
-        jax.ShapeDtypeStruct((8, LANES), F32),
-    )
-    value, top = pl.pallas_call(
-        multiply_for_other,
-        out_shape=product,
+    every_second = [list(range(first, ys, 2)) for first in range(2)]
+    even = lax.all_gather(output_grads.T, "y", axis_index_groups=every_second)
+    low = lax.ppermute(even[: ys // 4], "y", [(y, (y - 1) % ys) for y in range(ys)])
+    high = lax.ppermute(even[ys // 4 :], "y", [(y, (y + 1) % ys) for y in range(ys)])
+
+    def product(dtype):
+        return jax.ShapeDtypeStruct((2, columns, activations.shape[1]), dtype)
+
+    top_shape = jax.ShapeDtypeStruct((8, LANES), F32)
+    to_other_even, own_even, top = pl.pallas_call(
+        multiply_even,
+        out_shape=(product(BF16), product(F32), top_shape),
         in_specs=[SMEM, VMEM, VMEM],
-        out_specs=(VMEM, VMEM),
-        compiler_params=grant(12),
-    )(place, grads, activations)
-
-    value = lax.ppermute(value, "core", swap)
-    value, top = pl.pallas_call(
-        multiply_and_add,
-        out_shape=product,
+        out_specs=(VMEM,) * 3,
+        compiler_params=grant(14),
+    )(place, even, activations)
+    to_other_odd, top = pl.pallas_call(
+        functools.partial(multiply_odd, True),
+        out_shape=(product(BF16), top_shape),
         in_specs=[SMEM] + [VMEM] * 4,
         out_specs=(VMEM, VMEM),
-        compiler_params=grant(12),
-    )(place, grads, activations, value, top)
-    value = lax.all_to_all(value.reshape(xs, rows, -1), "x", 0, 0, tiled=True)
+        compiler_params=grant(14),
+    )(place, low, high, activations, top)
+    own_odd, top = pl.pallas_call(
+        functools.partial(multiply_odd, False),
+        out_shape=(product(F32), top_shape),
+        in_specs=[SMEM] + [VMEM] * 4,
+        out_specs=(VMEM, VMEM),
+        compiler_params=grant(14),
+    )(place, low, high, activations, top)
+
+    other_even = lax.ppermute(to_other_even, "core", swap)
+    other_odd = lax.ppermute(to_other_odd, "core", swap)
+    value = pl.pallas_call(
+        add_cores,
+        out_shape=jax.ShapeDtypeStruct((xs, rows, activations.shape[1]), BF16),
+        in_specs=[SMEM] + [VMEM] * 4,
+        out_specs=VMEM,
+        compiler_params=grant(10),
+    )(place, own_even, own_odd, other_even, other_odd)
+    value = lax.all_to_all(value, "x", 0, 0, tiled=True)
     value = pl.pallas_call(
         add_and_cut,
         out_shape=jax.ShapeDtypeStruct((zs, packed, LANES), BF16),
@@ -281,12 +300,14 @@
     value = lax.all_to_all(value, "z", 0, 0, tiled=True)
     value = jnp.sum(value.astype(F32), axis=0)
     route = []
-    for x in range(xs):
-        for half in range(cores):
-            for y in range(ys):
-                for feature in range(zs):
-                    source = ((x * zs + slot_of(feature, y)) * cores + half) * ys + y
-                    route.append((source, (y * zs + feature) * ys + columns_of(half, x, y)))
+    for half in range(cores):
+        for odd in range(2):
+            for which in range(2):
+                for y in range(ys):
+                    x, column = block_of(half, odd, which, y)
+                    for feature in range(zs):
+                        source = ((x * zs + slot_of(feature, y)) * cores + half) * ys + y
+                        route.append((source, (y * zs + feature) * ys + column))
     value = lax.ppermute(value, DEVICE, route)
 
     block = jax.ShapeDtypeStruct((rows, width), F32)

time: 135 us -> 129 us (0.956)
  blocking collectives: 107 us -> 91.9 us
  starting transfers between devices: 14.7 us -> 26.1 us
  waiting for transfers between devices: 5 us -> 2.23 us
    all_to_all x2 -> x1, blocking collectives: 48.7 us -> 14.4 us  [on_device(): value = lax.all_to_all(value, 'x', 0, 0, tiled=True)]
    all_gather x0 -> x1, blocking collectives: none -> 17.7 us  [on_device(): even = lax.all_gather(output_grads.T, 'y', axis_index_groups=every_second)]
    ppermute x1 -> x4, starting transfers between devices: 5.63 us -> 15.2 us  [the longest x1 7.36 us: on_device(): other_even = lax.ppermute(to_other_even, 'core', swap)]
    ppermute x1, waiting for transfers between devices: 3.1 us -> 1.53 us  [on_device(): value = lax.ppermute(value, DEVICE, route)]
    ppermute x1, starting transfers between devices: 5.27 us -> 6.84 us  [on_device(): value = lax.ppermute(value, DEVICE, route)]
  transfers between devices with their start and end apart: 3 -> 6, of which waited for: 2 -> 2; matrix products, arithmetic and copies ran while one was open for 0% -> 0% of each run, Pallas kernels for 0% -> 2%
where the time goes in v7:
time: 129 us
  blocking collectives  91.9 us (71%)
  starting transfers between devices  26.1 us (20%)
  Pallas kernels  5.45 us (4%)
  waiting for transfers between devices  2.23 us (2%)
  local copies, waits for them, and re-layouts  1.93 us (1%)
  between operations  1.42 us (1%)
    all_to_all x1, blocking collectives, on_device(): value = lax.all_to_all(value, 'z', 0, 0, tiled=True)  18.6 us
    all_gather x1, blocking collectives, on_device(): even = lax.all_gather(output_grads.T, 'y', axis_index_groups=every_second)  17.7 us
    all_to_all x1, blocking collectives, on_device(): held = lax.all_to_all(held, 'z', 0, 0, tiled=True)  16.1 us
    all_to_all x1, blocking collectives, on_device(): value = lax.all_to_all(value, 'x', 0, 0, tiled=True)  14.4 us
    all_to_all x1, blocking collectives, on_device(): tops = lax.all_to_all(tops, ('core', 'y'), 0, 0, tiled=True)  13 us
    all_gather x1, blocking collectives, on_device(): held = lax.all_gather(held, 'x')  12.1 us
    ppermute x1, starting transfers between devices, on_device(): other_even = lax.ppermute(to_other_even, 'core', swap)  7.36 us
    ppermute x1, starting transfers between devices, on_device(): value = lax.ppermute(value, DEVICE, route)  6.84 us
  transfers between devices with their start and end apart: 6, of which 2 were waited for; matrix products, arithmetic and copies ran while one was open for 0% of the time, Pallas kernels for 2%

profile of v7, /device:TPU:1, one launch (start us, length us, event | category | flops | bytes accessed | tf_op | source)
XLA Modules:
  0.0 129.0 jit_solution(10684139053492608064)
XLA Ops:
  0.6 17.7 %all-gather = bf16[256,1024]{1,0:T(8,128)(2,1)S(1)} all-gather(bf16[64,1024]{1,0:T(8,128)(2,1)} %bitcast.12), channel_id=2, replica_groups={{0,2,4,6},{1,3,5,7},{8,10,12,14},{9,11,13,15},{16,18,20,22},{17,19,21,2..., dimensions={0}, use_global_device_ids=true | all-gather | bytes 655360 | tf_op jit(solution)/shard_map/all_gather | solution.py:253
  18.4 1.9 %collective-permute-start = (bf16[2,64,1024]{2,1,0:T(8,128)(2,1)S(1)}, bf16[2,64,1024]{2,1,0:T(8,128)(2,1)S(1)}, u32[]{:S(2)}, u32[]{:S(2)}) collective-permute-start(bf16[2,64,1024]{2,1,0:T(8,128)(2,1)S(1)} %bitcast.11), channel_id=1, source_target_pairs={{0,7},{1,0},{2,1},{3,2},{4,3},{5,4},{6,5},{7,6},{8,15},{9,8},{10,9... | collective-permute-start | bytes 786440 | tf_op jit(solution)/shard_map/ppermute | solution.py:254
  20.3 3.4 %collective-permute-start.1 = (bf16[2,64,1024]{2,1,0:T(8,128)(2,1)S(1)}, bf16[2,64,1024]{2,1,0:T(8,128)(2,1)S(1)}, u32[]{:S(2)}, u32[]{:S(2)}) collective-permute-start(bf16[2,64,1024]{2,1,0:T(8,128)(2,1)S(1)} %bitcast.10), channel_id=1, source_target_pairs={{0,1},{1,2},{2,3},{3,4},{4,5},{5,6},{6,7},{7,0},{8,9},{9,10},{10,1... | collective-permute-start | bytes 786440 | tf_op jit(solution)/shard_map/ppermute | solution.py:255
  23.7 0.0 copy-start
  23.7 1.9 %copy-done = bf16[1024,1536]{1,0:T(8,128)(2,1)S(1)} copy-done((bf16[1024,1536]{1,0:T(8,128)(2,1)S(1)}, bf16[1024,1536]{1,0:T(8,128)(2,1)}, u32[]{:S(2)}) %copy-start) | copy-done | bytes 3145752
  25.6 0.0 copy-start.1
  25.6 1.0 shard_map.117
  26.6 7.4 %collective-permute-start.2 = (bf16[2,64,1536]{2,1,0:T(8,128)(2,1)S(1)}, bf16[2,64,1536]{2,1,0:T(8,128)(2,1)S(1)}, u32[]{:S(2)}, u32[]{:S(2)}) collective-permute-start(bf16[2,64,1536]{2,1,0:T(8,128)(2,1)S(1)} %get-tuple-element.31), channel_id=1, source_target_pairs={{0,8},{8,0},{1,9},{9,1},{2,10},{10,2},{3,11},{11,3},{4,12},{12,4},... | collective-permute-start | bytes 1179656 | tf_op jit(solution)/shard_map/ppermute | solution.py:283
  34.0 0.0 collective-permute-done.low_ref
  34.0 0.0 collective-permute-done.1.high_ref
  34.0 0.0 copy-done.1
  34.0 0.6 shard_map.118
  34.6 2.6 %collective-permute-start.3 = (bf16[2,64,1536]{2,1,0:T(8,128)(2,1)S(1)}, bf16[2,64,1536]{2,1,0:T(8,128)(2,1)S(1)}, u32[]{:S(2)}, u32[]{:S(2)}) collective-permute-start(bf16[2,64,1536]{2,1,0:T(8,128)(2,1)S(1)} %get-tuple-element.32), channel_id=1, source_target_pairs={{0,8},{8,0},{1,9},{9,1},{2,10},{10,2},{3,11},{11,3},{4,12},{12,4},... | collective-permute-start | bytes 1179656 | tf_op jit(solution)/shard_map/ppermute | solution.py:284
  37.2 0.6 shard_map.119
  37.8 0.0 collective-permute-done.2.other_even_ref
  37.9 0.7 collective-permute-done.3.other_odd_ref
  38.5 0.0 copy-start.2
  38.5 0.0 copy-start.3
  38.5 0.0 copy-start.4
  38.5 0.1 shard_map.120
  38.7 14.4 %all_to_all.20.parts_ref = bf16[4,64,1536]{2,1,0:T(8,128)(2,1)S(1)} all-to-all(bf16[4,64,1536]{2,1,0:T(8,128)(2,1)S(1)} %shard_map.120), channel_id=1, replica_groups=mesh['x'=4,'z'=8,'core'=2,'y'=8] {'x'}, dimensions={0} | all-to-all | bytes 1572864 | tf_op jit(solution)/shard_map/all_to_all | solution.py:292
  53.1 0.1 shard_map.121
  53.2 18.6 %all_to_all.21 = bf16[8,96,128]{2,1,0:T(8,128)(2,1)S(1)} all-to-all(bf16[8,96,128]{2,1,0:T(8,128)(2,1)S(1)} %shard_map.121), channel_id=1, replica_groups=mesh['x'=4,'z'=8,'core'=2,'y'=8] {'z'}, dimensions={0} | all-to-all | bytes 393216 | tf_op jit(solution)/shard_map/all_to_all | solution.py:300
  71.9 6.8 %collective-permute-start.4 = (f32[96,128]{1,0:T(8,128)S(1)}, f32[96,128]{1,0:T(8,128)S(1)}, u32[]{:S(2)}, u32[]{:S(2)}) collective-permute-start(f32[96,128]{1,0:T(8,128)S(1)} %convert_reduce_fusion), channel_id=1, source_target_pairs={{0,4},{112,12},{16,20},{96,28},{32,36},{80,44},{48,52},{64,60},{65... | collective-permute-start | bytes 147464 | tf_op jit(solution)/shard_map/ppermute | solution.py:311
  79.4 1.5 %collective-permute-done.4.summed_ref = f32[96,128]{1,0:T(8,128)S(1)} collective-permute-done((f32[96,128]{1,0:T(8,128)S(1)}, f32[96,128]{1,0:T(8,128)S(1)}, u32[]{:S(2)}, u32[]{:S(2)}) %collective-permute-start.4) | collective-permute-done | bytes 49184 | tf_op jit(solution)/shard_map/ppermute | solution.py:311
  80.9 0.0 copy-done.2
  80.9 0.0 copy-done.3
  80.9 0.0 copy-done.4
  80.9 0.8 shard_map.122
  81.8 16.1 %all_to_all.22.held_ref = bf16[8,112,128]{2,1,0:T(8,128)(2,1)S(1)} all-to-all(bf16[8,112,128]{2,1,0:T(8,128)(2,1)S(1)} %get-tuple-element.35), channel_id=1, replica_groups=mesh['x'=4,'z'=8,'core'=2,'y'=8] {'z'}, dimensions={0} | all-to-all | bytes 458752 | tf_op jit(solution)/shard_map/all_to_all | solution.py:322
  97.9 12.1 %all-gather.1 = bf16[3136,128]{1,0:T(8,128)(2,1)S(1)} all-gather(bf16[784,128]{1,0:T(8,128)(2,1)S(1)} %shard_map.123), channel_id=3, replica_groups=mesh['x'=4,'z'=8,'core'=2,'y'=8] {'x'}, dimensions={0}, use_global_device_ids=true | all-gather | bytes 1003520 | tf_op jit(solution)/shard_map/all_gather | solution.py:330
  109.9 4.0 %collective-permute-start.5 = (bf16[4,784,128]{2,1,0:T(8,128)(2,1)S(1)}, bf16[4,784,128]{2,1,0:T(8,128)(2,1)S(1)}, u32[]{:S(2)}, u32[]{:S(2)}) collective-permute-start(bf16[4,784,128]{2,1,0:T(8,128)(2,1)S(1)} %bitcast.6), channel_id=1, source_target_pairs={{0,8},{8,0},{1,9},{9,1},{2,10},{10,2},{3,11},{11,3},{4,12},{12,4},... | collective-permute-start | bytes 2408456 | tf_op jit(solution)/shard_map/ppermute | solution.py:331
  114.0 13.0 %all_to_all.23.tops_ref = f32[16,8,128]{2,1,0:T(8,128)S(1)} all-to-all(f32[16,8,128]{2,1,0:T(8,128)S(1)} %shard_map.124), channel_id=1, replica_groups=mesh['x'=4,'z'=8,'core'=2,'y'=8] {'core','y'}, dimensions={0} | all-to-all | bytes 131072 | tf_op jit(solution)/shard_map/all_to_all | solution.py:339
  127.0 0.0 collective-permute-done.5.other_ref
  127.0 2.0 %shard_map.125 = (bf16[64,12288]{1,0:T(8,128)(2,1)}, bf16[64,192]{1,0:T(8,128)(2,1)}, f32[1]{0:T(128)}, f32[1]{0:T(128)}, f32[1]{0:T(128)}) custom-call(s32[1]{0:T(128)} %bitcast.place_ref, f32[16,8,128]{2,1,0:T(8,128)S(1)} %all_to_all.23.tops_ref, bf16[4,784,128]{2,1,0:T(8,128)(2,1)S(1)} %bitcast.8, ...), custom_call_target="tpu_custom_call" | custom-call | tf_op jit(solution)/shard_map/pallas_call | solution.py:342
  (4 shorter events, 0.1 us)
Async XLA Ops:
  18.4 15.6 %collective-permute-start = (bf16[2,64,1024]{2,1,0:T(8,128)(2,1)S(1)}, bf16[2,64,1024]{2,1,0:T(8,128)(2,1)S(1)}, u32[]{:S(2)}, u32[]{:S(2)}) collective-permute-start(bf16[2,64,1024]{2,1,0:T(8,128)(2,1)S(1)} %bitcast.11), channel_id=1, source_target_pairs={{0,7},{1,0},{2,1},{3,2},{4,3},{5,4},{6,5},{7,6},{8,15},{9,8},{10,9... | collective-permute-start | bytes 786440 | tf_op jit(solution)/shard_map/ppermute | solution.py:254
  20.3 13.7 %collective-permute-start.1 = (bf16[2,64,1024]{2,1,0:T(8,128)(2,1)S(1)}, bf16[2,64,1024]{2,1,0:T(8,128)(2,1)S(1)}, u32[]{:S(2)}, u32[]{:S(2)}) collective-permute-start(bf16[2,64,1024]{2,1,0:T(8,128)(2,1)S(1)} %bitcast.10), channel_id=1, source_target_pairs={{0,1},{1,2},{2,3},{3,4},{4,5},{5,6},{6,7},{7,0},{8,9},{9,10},{10,1... | collective-permute-start | bytes 786440 | tf_op jit(solution)/shard_map/ppermute | solution.py:255
  23.7 1.9 %copy-start = (bf16[1024,1536]{1,0:T(8,128)(2,1)S(1)}, bf16[1024,1536]{1,0:T(8,128)(2,1)}, u32[]{:S(2)}) copy-start(bf16[1024,1536]{1,0:T(8,128)(2,1)} %activations_ref.5) | copy-start | bytes 9437188
  25.6 8.4 %copy-start.1 = (bf16[1024,1536]{1,0:T(8,128)(2,1)S(1)}, bf16[1024,1536]{1,0:T(8,128)(2,1)}, u32[]{:S(2)}) copy-start(bf16[1024,1536]{1,0:T(8,128)(2,1)} %activations_ref.5) | copy-start | bytes 9437188
  26.6 11.2 %collective-permute-start.2 = (bf16[2,64,1536]{2,1,0:T(8,128)(2,1)S(1)}, bf16[2,64,1536]{2,1,0:T(8,128)(2,1)S(1)}, u32[]{:S(2)}, u32[]{:S(2)}) collective-permute-start(bf16[2,64,1536]{2,1,0:T(8,128)(2,1)S(1)} %get-tuple-element.31), channel_id=1, source_target_pairs={{0,8},{8,0},{1,9},{9,1},{2,10},{10,2},{3,11},{11,3},{4,12},{12,4},... | collective-permute-start | bytes 1179656 | tf_op jit(solution)/shard_map/ppermute | solution.py:283
  34.6 3.9 %collective-permute-start.3 = (bf16[2,64,1536]{2,1,0:T(8,128)(2,1)S(1)}, bf16[2,64,1536]{2,1,0:T(8,128)(2,1)S(1)}, u32[]{:S(2)}, u32[]{:S(2)}) collective-permute-start(bf16[2,64,1536]{2,1,0:T(8,128)(2,1)S(1)} %get-tuple-element.32), channel_id=1, source_target_pairs={{0,8},{8,0},{1,9},{9,1},{2,10},{10,2},{3,11},{11,3},{4,12},{12,4},... | collective-permute-start | bytes 1179656 | tf_op jit(solution)/shard_map/ppermute | solution.py:284
  38.5 42.4 %copy-start.2 = (f32[64,192]{1,0:T(8,128)S(1)}, f32[64,192]{1,0:T(8,128)}, u32[]{:S(2)}) copy-start(f32[64,192]{1,0:T(8,128)} %master_ref.1) | copy-start | bytes 147460
  38.5 42.4 %copy-start.3 = (f32[64,192]{1,0:T(8,128)S(1)}, f32[64,192]{1,0:T(8,128)}, u32[]{:S(2)}) copy-start(f32[64,192]{1,0:T(8,128)} %second_ref.1) | copy-start | bytes 147460
  38.5 42.4 %copy-start.4 = (bf16[64,192]{1,0:T(8,128)(2,1)S(1)}, bf16[64,192]{1,0:T(8,128)(2,1)}, u32[]{:S(2)}) copy-start(bf16[64,192]{1,0:T(8,128)(2,1)} %moment_ref.1) | copy-start | bytes 73732
  71.9 9.0 %collective-permute-start.4 = (f32[96,128]{1,0:T(8,128)S(1)}, f32[96,128]{1,0:T(8,128)S(1)}, u32[]{:S(2)}, u32[]{:S(2)}) collective-permute-start(f32[96,128]{1,0:T(8,128)S(1)} %convert_reduce_fusion), channel_id=1, source_target_pairs={{0,4},{112,12},{16,20},{96,28},{32,36},{80,44},{48,52},{64,60},{65... | collective-permute-start | bytes 147464 | tf_op jit(solution)/shard_map/ppermute | solution.py:311
  109.9 17.0 %collective-permute-start.5 = (bf16[4,784,128]{2,1,0:T(8,128)(2,1)S(1)}, bf16[4,784,128]{2,1,0:T(8,128)(2,1)S(1)}, u32[]{:S(2)}, u32[]{:S(2)}) collective-permute-start(bf16[4,784,128]{2,1,0:T(8,128)(2,1)S(1)} %bitcast.6), channel_id=1, source_target_pairs={{0,8},{8,0},{1,9},{9,1},{2,10},{10,2},{3,11},{11,3},{4,12},{12,4},... | collective-permute-start | bytes 2408456 | tf_op jit(solution)/shard_map/ppermute | solution.py:331

commit v8 on v7

--- a/solution.py
+++ b/solution.py
@@ -83,8 +83,7 @@
 
 
 def slot_of(feature, y):
-    near = feature // 2 if feature % 2 == 0 else 7 - feature // 2
-    return (near + 4 * (y % 2)) % 8
+    return (feature + 6 + 4 * (y % 2)) % 8
 
 
 def core_and_y(place_ref):
@@ -206,14 +205,31 @@
         out_ref[copy] = best
 
 
+def lay_out(place_ref, own_ref, other_ref, out_ref):
+    rows = out_ref.shape[0]
+    packed = rows + rows // 2
+    is_even = core_and_y(place_ref)[0] == 0
+
+    def fill(even_ref, odd_ref):
+        blocks = (even_ref.shape[1] - TOP_ROWS) // packed
+        for place in range(even_ref.shape[0] * blocks):
+            x, start = place // blocks, place % blocks * packed
+            tails = slice(start + rows, start + packed)
+            middle = unfold(even_ref[x, tails].astype(F32), odd_ref[x, tails].astype(F32))
+            column = 3 * LANES * place
+            out_ref[:, column : column + LANES] = even_ref[x, start : start + rows]
+            out_ref[:, column + LANES : column + 2 * LANES] = middle.astype(BF16)
+            out_ref[:, column + 2 * LANES : column + 3 * LANES] = odd_ref[x, start : start + rows]
+
+    pl.when(is_even)(lambda: fill(own_ref, other_ref))
+    pl.when(jnp.logical_not(is_even))(lambda: fill(other_ref, own_ref))
+
+
 def scale_weights(
-    place_ref, tops_ref, own_ref, other_ref, moment_ref,
+    tops_ref, laid_ref, moment_ref,
     weight_out, moment_out, moment_span_out, weight_span_out, grad_span_out, span_ref,
 ):
-    rows = weight_out.shape[0]
-    packed = rows + rows // 2
     step = pl.program_id(0)
-    is_even = core_and_y(place_ref)[0] == 0
 
     @pl.when(step == 0)
     def _():
@@ -221,22 +237,17 @@
         for place in range(1, tops_ref.shape[0]):
             best = jnp.maximum(best, tops_ref[place])
         spans = best + EPSILON
-        span_ref[...] = spans
+        span_ref[...] = 1.0 / spans
         moment_out[...] = (moment_ref[...] / largest(spans[1:2])).astype(BF16)
         grad_span_out[0] = jnp.max(spans[0:1])
         moment_span_out[0] = jnp.max(spans[1:2])
         weight_span_out[0] = jnp.max(spans[2:3])
 
-    scale = 1.0 / span_ref[2:3]
-    for place in range((own_ref.shape[1] - TOP_ROWS) // packed):
-        where = slice(place * packed, (place + 1) * packed)
-        own = own_ref[step, where].astype(F32) * scale
-        other = other_ref[step, where].astype(F32) * scale
-        even, odd = jnp.where(is_even, own, other), jnp.where(is_even, other, own)
-        start = 3 * LANES * place
-        weight_out[:, start : start + LANES] = even[:rows].astype(BF16)
-        weight_out[:, start + LANES : start + 2 * LANES] = unfold(even[rows:], odd[rows:]).astype(BF16)
-        weight_out[:, start + 2 * LANES : start + 3 * LANES] = odd[:rows].astype(BF16)
+    scale = span_ref[2:3]
+    width = weight_out.shape[1]
+    for start in range(0, width, LANES):
+        where = pl.ds(pl.multiple_of(step * width + start, LANES), LANES)
+        weight_out[:, start : start + LANES] = (laid_ref[:, where].astype(F32) * scale).astype(BF16)
 
 
 def on_device(activations, output_grads, master, moment_q, moment_range, second_moment):
@@ -338,18 +349,21 @@
     )(held)
     tops = lax.all_to_all(tops, ("core", "y"), 0, 0, tiled=True)
 
+    whole = jax.ShapeDtypeStruct((rows, width * xs * zs * cores), BF16)
+    laid = pl.pallas_call(
+        lay_out,
+        out_shape=whole,
+        in_specs=[SMEM, VMEM, VMEM],
+        out_specs=VMEM,
+        compiler_params=grant(8),
+    )(place, held, other)
+
     one = jax.ShapeDtypeStruct((1,), F32)
     weight_q, moment_q_new, moment_span, weight_span, grad_span = pl.pallas_call(
         scale_weights,
         grid=(xs,),
-        out_shape=(
-            jax.ShapeDtypeStruct((rows, width * xs * zs * cores), BF16),
-            jax.ShapeDtypeStruct((rows, width), BF16),
-            one,
-            one,
-            one,
-        ),
-        in_specs=[SMEM, VMEM, VMEM, VMEM, VMEM],
+        out_shape=(whole, jax.ShapeDtypeStruct((rows, width), BF16), one, one, one),
+        in_specs=[VMEM, VMEM, VMEM],
         out_specs=(
             pl.BlockSpec((rows, width * zs * cores), lambda i: (0, i)),
             VMEM,
@@ -359,7 +373,7 @@
         ),
         scratch_shapes=[pltpu.VMEM((8, LANES), F32)],
         compiler_params=grant(8),
-    )(place, tops, held, other, moment)
+    )(tops, laid, moment)
     return master_new, moment_q_new, moment_span, second_new, weight_q, weight_span, grad_span
 
 

time: 129 us -> 132 us (1.023)
  blocking collectives: 91.9 us -> 74.8 us
  starting transfers between devices: 26.1 us -> 38.3 us
  waiting for transfers between devices: 2.23 us -> 9.05 us
    all_to_all x1 -> x0, blocking collectives: 13 us -> none  [on_device(): tops = lax.all_to_all(tops, ('core', 'y'), 0, 0, tiled=True)]
    all_to_all x0 -> x1, waiting for transfers between devices: none -> 6.83 us  [on_device(): tops = lax.all_to_all(tops, ('core', 'y'), 0, 0, tiled=True)]
    all_to_all x0 -> x1, starting transfers between devices: none -> 6.54 us  [on_device(): tops = lax.all_to_all(tops, ('core', 'y'), 0, 0, tiled=True)]
    ppermute x1, starting transfers between devices: 4.04 us -> 9.68 us  [on_device(): other = lax.ppermute(held, 'core', swap)]
    all_to_all x1, blocking collectives: 16.1 us -> 12.4 us  [on_device(): held = lax.all_to_all(held, 'z', 0, 0, tiled=True)]
  transfers between devices with their start and end apart: 6 -> 7, of which waited for: 2 -> 3; matrix products, arithmetic and copies ran while one was open for 0% -> 0% of each run, Pallas kernels for 2% -> 2%
where the time goes in v8:
time: 132 us
  blocking collectives  74.8 us (57%)
  starting transfers between devices  38.3 us (29%)
  waiting for transfers between devices  9.05 us (7%)
  Pallas kernels  6.35 us (5%)
  local copies, waits for them, and re-layouts  1.94 us (1%)
  between operations  1.45 us (1%)
    all_to_all x1, blocking collectives, on_device(): value = lax.all_to_all(value, 'z', 0, 0, tiled=True)  18.6 us
    all_gather x1, blocking collectives, on_device(): even = lax.all_gather(output_grads.T, 'y', axis_index_groups=every_second)  17.7 us
    all_to_all x1, blocking collectives, on_device(): value = lax.all_to_all(value, 'x', 0, 0, tiled=True)  14.5 us
    all_to_all x1, blocking collectives, on_device(): held = lax.all_to_all(held, 'z', 0, 0, tiled=True)  12.4 us
    all_gather x1, blocking collectives, on_device(): held = lax.all_gather(held, 'x')  11.5 us
    ppermute x1, starting transfers between devices, on_device(): other = lax.ppermute(held, 'core', swap)  9.68 us
    ppermute x1, starting transfers between devices, on_device(): other_even = lax.ppermute(to_other_even, 'core', swap)  7.36 us
    ppermute x1, starting transfers between devices, on_device(): value = lax.ppermute(value, DEVICE, route)  6.84 us
  transfers between devices with their start and end apart: 7, of which 3 were waited for; matrix products, arithmetic and copies ran while one was open for 0% of the time, Pallas kernels for 2%

profile of v8, /device:TPU:1, one launch (start us, length us, event | category | flops | bytes accessed | tf_op | source)
XLA Modules:
  0.0 131.9 jit_solution(137184087506214717)
XLA Ops:
  0.6 17.7 %all-gather = bf16[256,1024]{1,0:T(8,128)(2,1)S(1)} all-gather(bf16[64,1024]{1,0:T(8,128)(2,1)} %bitcast.12), channel_id=2, replica_groups={{0,2,4,6},{1,3,5,7},{8,10,12,14},{9,11,13,15},{16,18,20,22},{17,19,21,2..., dimensions={0}, use_global_device_ids=true | all-gather | bytes 655360 | tf_op jit(solution)/shard_map/all_gather | solution.py:264
  18.4 1.9 %collective-permute-start = (bf16[2,64,1024]{2,1,0:T(8,128)(2,1)S(1)}, bf16[2,64,1024]{2,1,0:T(8,128)(2,1)S(1)}, u32[]{:S(2)}, u32[]{:S(2)}) collective-permute-start(bf16[2,64,1024]{2,1,0:T(8,128)(2,1)S(1)} %bitcast.11), channel_id=1, source_target_pairs={{0,7},{1,0},{2,1},{3,2},{4,3},{5,4},{6,5},{7,6},{8,15},{9,8},{10,9... | collective-permute-start | bytes 786440 | tf_op jit(solution)/shard_map/ppermute | solution.py:265
  20.3 3.4 %collective-permute-start.1 = (bf16[2,64,1024]{2,1,0:T(8,128)(2,1)S(1)}, bf16[2,64,1024]{2,1,0:T(8,128)(2,1)S(1)}, u32[]{:S(2)}, u32[]{:S(2)}) collective-permute-start(bf16[2,64,1024]{2,1,0:T(8,128)(2,1)S(1)} %bitcast.10), channel_id=1, source_target_pairs={{0,1},{1,2},{2,3},{3,4},{4,5},{5,6},{6,7},{7,0},{8,9},{9,10},{10,1... | collective-permute-start | bytes 786440 | tf_op jit(solution)/shard_map/ppermute | solution.py:266
  23.7 0.0 copy-start
  23.7 1.9 %copy-done = bf16[1024,1536]{1,0:T(8,128)(2,1)S(1)} copy-done((bf16[1024,1536]{1,0:T(8,128)(2,1)S(1)}, bf16[1024,1536]{1,0:T(8,128)(2,1)}, u32[]{:S(2)}) %copy-start) | copy-done | bytes 3145752
  25.6 0.0 copy-start.1
  25.6 1.0 shard_map.117
  26.6 7.4 %collective-permute-start.2 = (bf16[2,64,1536]{2,1,0:T(8,128)(2,1)S(1)}, bf16[2,64,1536]{2,1,0:T(8,128)(2,1)S(1)}, u32[]{:S(2)}, u32[]{:S(2)}) collective-permute-start(bf16[2,64,1536]{2,1,0:T(8,128)(2,1)S(1)} %get-tuple-element.31), channel_id=1, source_target_pairs={{0,8},{8,0},{1,9},{9,1},{2,10},{10,2},{3,11},{11,3},{4,12},{12,4},... | collective-permute-start | bytes 1179656 | tf_op jit(solution)/shard_map/ppermute | solution.py:294
  34.0 0.0 collective-permute-done.low_ref
  34.0 0.0 collective-permute-done.1.high_ref
  34.0 0.0 copy-done.1
  34.0 0.6 shard_map.118
  34.6 2.6 %collective-permute-start.3 = (bf16[2,64,1536]{2,1,0:T(8,128)(2,1)S(1)}, bf16[2,64,1536]{2,1,0:T(8,128)(2,1)S(1)}, u32[]{:S(2)}, u32[]{:S(2)}) collective-permute-start(bf16[2,64,1536]{2,1,0:T(8,128)(2,1)S(1)} %get-tuple-element.32), channel_id=1, source_target_pairs={{0,8},{8,0},{1,9},{9,1},{2,10},{10,2},{3,11},{11,3},{4,12},{12,4},... | collective-permute-start | bytes 1179656 | tf_op jit(solution)/shard_map/ppermute | solution.py:295
  37.2 0.6 shard_map.119
  37.8 0.0 collective-permute-done.2.other_even_ref
  37.9 0.7 collective-permute-done.3.other_odd_ref
  38.5 0.1 shard_map.120
  38.7 0.0 copy-start.2
  38.7 0.0 copy-start.3
  38.7 0.0 copy-start.4
  38.7 14.5 %all_to_all.20.parts_ref = bf16[4,64,1536]{2,1,0:T(8,128)(2,1)S(1)} all-to-all(bf16[4,64,1536]{2,1,0:T(8,128)(2,1)S(1)} %shard_map.120), channel_id=1, replica_groups=mesh['x'=4,'z'=8,'core'=2,'y'=8] {'x'}, dimensions={0} | all-to-all | bytes 1572864 | tf_op jit(solution)/shard_map/all_to_all | solution.py:303
  53.3 0.1 shard_map.121
  53.4 18.6 %all_to_all.21 = bf16[8,96,128]{2,1,0:T(8,128)(2,1)S(1)} all-to-all(bf16[8,96,128]{2,1,0:T(8,128)(2,1)S(1)} %shard_map.121), channel_id=1, replica_groups=mesh['x'=4,'z'=8,'core'=2,'y'=8] {'z'}, dimensions={0} | all-to-all | bytes 393216 | tf_op jit(solution)/shard_map/all_to_all | solution.py:311
  72.0 6.8 %collective-permute-start.4 = (f32[96,128]{1,0:T(8,128)S(1)}, f32[96,128]{1,0:T(8,128)S(1)}, u32[]{:S(2)}, u32[]{:S(2)}) collective-permute-start(f32[96,128]{1,0:T(8,128)S(1)} %convert_reduce_fusion), channel_id=1, source_target_pairs={{96,4},{112,12},{0,20},{16,28},{32,36},{48,44},{64,52},{80,60},{33... | collective-permute-start | bytes 147464 | tf_op jit(solution)/shard_map/ppermute | solution.py:322
  79.5 1.5 %collective-permute-done.4.summed_ref = f32[96,128]{1,0:T(8,128)S(1)} collective-permute-done((f32[96,128]{1,0:T(8,128)S(1)}, f32[96,128]{1,0:T(8,128)S(1)}, u32[]{:S(2)}, u32[]{:S(2)}) %collective-permute-start.4) | collective-permute-done | bytes 49184 | tf_op jit(solution)/shard_map/ppermute | solution.py:322
  81.1 0.0 copy-done.2
  81.1 0.0 copy-done.3
  81.1 0.0 copy-done.4
  81.1 0.8 shard_map.122
  81.9 12.4 %all_to_all.22.held_ref = bf16[8,112,128]{2,1,0:T(8,128)(2,1)S(1)} all-to-all(bf16[8,112,128]{2,1,0:T(8,128)(2,1)S(1)} %get-tuple-element.35), channel_id=1, replica_groups=mesh['x'=4,'z'=8,'core'=2,'y'=8] {'z'}, dimensions={0} | all-to-all | bytes 458752 | tf_op jit(solution)/shard_map/all_to_all | solution.py:333
  94.4 11.5 %all-gather.1 = bf16[3136,128]{1,0:T(8,128)(2,1)S(1)} all-gather(bf16[784,128]{1,0:T(8,128)(2,1)S(1)} %shard_map.123), channel_id=3, replica_groups=mesh['x'=4,'z'=8,'core'=2,'y'=8] {'x'}, dimensions={0}, use_global_device_ids=true | all-gather | bytes 1003520 | tf_op jit(solution)/shard_map/all_gather | solution.py:341
  105.9 9.7 %collective-permute-start.5 = (bf16[4,784,128]{2,1,0:T(8,128)(2,1)S(1)}, bf16[4,784,128]{2,1,0:T(8,128)(2,1)S(1)}, u32[]{:S(2)}, u32[]{:S(2)}) collective-permute-start(bf16[4,784,128]{2,1,0:T(8,128)(2,1)S(1)} %bitcast.6), channel_id=1, source_target_pairs={{0,8},{8,0},{1,9},{9,1},{2,10},{10,2},{3,11},{11,3},{4,12},{12,4},... | collective-permute-start | bytes 2408456 | tf_op jit(solution)/shard_map/ppermute | solution.py:342
  115.6 0.6 shard_map.124
  116.2 6.5 %all-to-all-start.3 = ((f32[16,8,128]{2,1,0:T(8,128)}), f32[16,8,128]{2,1,0:T(8,128)S(1)}, u32[]{:S(2)}, u32[]{:S(2)}) async-start(f32[16,8,128]{2,1,0:T(8,128)} %shard_map.124), calls=%async_computation.3 | async-start | bytes 131072 | tf_op jit(solution)/shard_map/all_to_all | solution.py:350
  122.8 0.0 collective-permute-done.5.other_ref
  122.8 0.3 shard_map.125.laid_ref
  123.1 6.8 %all-to-all-done.3.tops_ref = f32[16,8,128]{2,1,0:T(8,128)S(1)} async-done(((f32[16,8,128]{2,1,0:T(8,128)}), f32[16,8,128]{2,1,0:T(8,128)S(1)}, u32[]{:S(2)}, u32[]{:S(2)}) %all-to-all-start.3) | async-done | bytes 65568 | tf_op jit(solution)/shard_map/all_to_all | solution.py:350
  129.9 2.0 %shard_map.126 = (bf16[64,12288]{1,0:T(8,128)(2,1)}, bf16[64,192]{1,0:T(8,128)(2,1)}, f32[1]{0:T(128)}, f32[1]{0:T(128)}, f32[1]{0:T(128)}) custom-call(f32[16,8,128]{2,1,0:T(8,128)S(1)} %all-to-all-done.3.tops_ref, bf16[64,12288]{1,0:T(8,128)(2,1)S(1)} %shard_map.125.laid_ref, f32[64,192]{1,0:T(8,128)S(1)} %get-tuple-element.36.moment_ref), custom_call_target="tpu_custom_call" | custom-call | tf_op jit(solution)/shard_map/pallas_call | solution.py:362
  (3 shorter events, 0.1 us)
Async XLA Ops:
  18.4 15.6 %collective-permute-start = (bf16[2,64,1024]{2,1,0:T(8,128)(2,1)S(1)}, bf16[2,64,1024]{2,1,0:T(8,128)(2,1)S(1)}, u32[]{:S(2)}, u32[]{:S(2)}) collective-permute-start(bf16[2,64,1024]{2,1,0:T(8,128)(2,1)S(1)} %bitcast.11), channel_id=1, source_target_pairs={{0,7},{1,0},{2,1},{3,2},{4,3},{5,4},{6,5},{7,6},{8,15},{9,8},{10,9... | collective-permute-start | bytes 786440 | tf_op jit(solution)/shard_map/ppermute | solution.py:265
  20.3 13.7 %collective-permute-start.1 = (bf16[2,64,1024]{2,1,0:T(8,128)(2,1)S(1)}, bf16[2,64,1024]{2,1,0:T(8,128)(2,1)S(1)}, u32[]{:S(2)}, u32[]{:S(2)}) collective-permute-start(bf16[2,64,1024]{2,1,0:T(8,128)(2,1)S(1)} %bitcast.10), channel_id=1, source_target_pairs={{0,1},{1,2},{2,3},{3,4},{4,5},{5,6},{6,7},{7,0},{8,9},{9,10},{10,1... | collective-permute-start | bytes 786440 | tf_op jit(solution)/shard_map/ppermute | solution.py:266
  23.7 1.9 %copy-start = (bf16[1024,1536]{1,0:T(8,128)(2,1)S(1)}, bf16[1024,1536]{1,0:T(8,128)(2,1)}, u32[]{:S(2)}) copy-start(bf16[1024,1536]{1,0:T(8,128)(2,1)} %activations_ref.5) | copy-start | bytes 9437188
  25.6 8.4 %copy-start.1 = (bf16[1024,1536]{1,0:T(8,128)(2,1)S(1)}, bf16[1024,1536]{1,0:T(8,128)(2,1)}, u32[]{:S(2)}) copy-start(bf16[1024,1536]{1,0:T(8,128)(2,1)} %activations_ref.5) | copy-start | bytes 9437188
  26.6 11.2 %collective-permute-start.2 = (bf16[2,64,1536]{2,1,0:T(8,128)(2,1)S(1)}, bf16[2,64,1536]{2,1,0:T(8,128)(2,1)S(1)}, u32[]{:S(2)}, u32[]{:S(2)}) collective-permute-start(bf16[2,64,1536]{2,1,0:T(8,128)(2,1)S(1)} %get-tuple-element.31), channel_id=1, source_target_pairs={{0,8},{8,0},{1,9},{9,1},{2,10},{10,2},{3,11},{11,3},{4,12},{12,4},... | collective-permute-start | bytes 1179656 | tf_op jit(solution)/shard_map/ppermute | solution.py:294
  34.6 3.9 %collective-permute-start.3 = (bf16[2,64,1536]{2,1,0:T(8,128)(2,1)S(1)}, bf16[2,64,1536]{2,1,0:T(8,128)(2,1)S(1)}, u32[]{:S(2)}, u32[]{:S(2)}) collective-permute-start(bf16[2,64,1536]{2,1,0:T(8,128)(2,1)S(1)} %get-tuple-element.32), channel_id=1, source_target_pairs={{0,8},{8,0},{1,9},{9,1},{2,10},{10,2},{3,11},{11,3},{4,12},{12,4},... | collective-permute-start | bytes 1179656 | tf_op jit(solution)/shard_map/ppermute | solution.py:295
  38.7 42.4 %copy-start.2 = (f32[64,192]{1,0:T(8,128)S(1)}, f32[64,192]{1,0:T(8,128)}, u32[]{:S(2)}) copy-start(f32[64,192]{1,0:T(8,128)} %master_ref.1) | copy-start | bytes 147460
  38.7 42.4 %copy-start.3 = (f32[64,192]{1,0:T(8,128)S(1)}, f32[64,192]{1,0:T(8,128)}, u32[]{:S(2)}) copy-start(f32[64,192]{1,0:T(8,128)} %second_ref.1) | copy-start | bytes 147460
  38.7 42.4 %copy-start.4 = (bf16[64,192]{1,0:T(8,128)(2,1)S(1)}, bf16[64,192]{1,0:T(8,128)(2,1)}, u32[]{:S(2)}) copy-start(bf16[64,192]{1,0:T(8,128)(2,1)} %moment_ref.1) | copy-start | bytes 73732
  72.0 9.0 %collective-permute-start.4 = (f32[96,128]{1,0:T(8,128)S(1)}, f32[96,128]{1,0:T(8,128)S(1)}, u32[]{:S(2)}, u32[]{:S(2)}) collective-permute-start(f32[96,128]{1,0:T(8,128)S(1)} %convert_reduce_fusion), channel_id=1, source_target_pairs={{96,4},{112,12},{0,20},{16,28},{32,36},{48,44},{64,52},{80,60},{33... | collective-permute-start | bytes 147464 | tf_op jit(solution)/shard_map/ppermute | solution.py:322
  105.9 16.9 %collective-permute-start.5 = (bf16[4,784,128]{2,1,0:T(8,128)(2,1)S(1)}, bf16[4,784,128]{2,1,0:T(8,128)(2,1)S(1)}, u32[]{:S(2)}, u32[]{:S(2)}) collective-permute-start(bf16[4,784,128]{2,1,0:T(8,128)(2,1)S(1)} %bitcast.6), channel_id=1, source_target_pairs={{0,8},{8,0},{1,9},{9,1},{2,10},{10,2},{3,11},{11,3},{4,12},{12,4},... | collective-permute-start | bytes 2408456 | tf_op jit(solution)/shard_map/ppermute | solution.py:342
  116.2 13.7 %all-to-all-start.3 = ((f32[16,8,128]{2,1,0:T(8,128)}), f32[16,8,128]{2,1,0:T(8,128)S(1)}, u32[]{:S(2)}, u32[]{:S(2)}) async-start(f32[16,8,128]{2,1,0:T(8,128)} %shard_map.124), calls=%async_computation.3 | async-start | bytes 131072 | tf_op jit(solution)/shard_map/all_to_all | solution.py:350

commit v9 on v7

--- a/solution.py
+++ b/solution.py
@@ -83,8 +83,7 @@
 
 
 def slot_of(feature, y):
-    near = feature // 2 if feature % 2 == 0 else 7 - feature // 2
-    return (near + 4 * (y % 2)) % 8
+    return (feature + 6 + 4 * (y % 2)) % 8
 
 
 def core_and_y(place_ref):
@@ -208,35 +207,37 @@
 
 def scale_weights(
     place_ref, tops_ref, own_ref, other_ref, moment_ref,
-    weight_out, moment_out, moment_span_out, weight_span_out, grad_span_out, span_ref,
+    weight_out, moment_out, moment_span_out, weight_span_out, grad_span_out, scaled_ref, written,
 ):
-    rows = weight_out.shape[0]
+    rows = moment_ref.shape[0]
     packed = rows + rows // 2
-    step = pl.program_id(0)
     is_even = core_and_y(place_ref)[0] == 0
-
-    @pl.when(step == 0)
-    def _():
-        best = tops_ref[0]
-        for place in range(1, tops_ref.shape[0]):
-            best = jnp.maximum(best, tops_ref[place])
-        spans = best + EPSILON
-        span_ref[...] = spans
-        moment_out[...] = (moment_ref[...] / largest(spans[1:2])).astype(BF16)
-        grad_span_out[0] = jnp.max(spans[0:1])
-        moment_span_out[0] = jnp.max(spans[1:2])
-        weight_span_out[0] = jnp.max(spans[2:3])
-
-    scale = 1.0 / span_ref[2:3]
-    for place in range((own_ref.shape[1] - TOP_ROWS) // packed):
-        where = slice(place * packed, (place + 1) * packed)
-        own = own_ref[step, where].astype(F32) * scale
-        other = other_ref[step, where].astype(F32) * scale
-        even, odd = jnp.where(is_even, own, other), jnp.where(is_even, other, own)
-        start = 3 * LANES * place
-        weight_out[:, start : start + LANES] = even[:rows].astype(BF16)
-        weight_out[:, start + LANES : start + 2 * LANES] = unfold(even[rows:], odd[rows:]).astype(BF16)
-        weight_out[:, start + 2 * LANES : start + 3 * LANES] = odd[:rows].astype(BF16)
+    best = tops_ref[0]
+    for place in range(1, tops_ref.shape[0]):
+        best = jnp.maximum(best, tops_ref[place])
+    spans = best + EPSILON
+    scale = (1.0 / spans)[2:3]
+    copies = []
+    for x in range(own_ref.shape[0]):
+        blocks = (own_ref.shape[1] - TOP_ROWS) // packed
+        for place in range(blocks):
+            where = slice(place * packed, (place + 1) * packed)
+            own = own_ref[x, where].astype(F32) * scale
+            other = other_ref[x, where].astype(F32) * scale
+            even, odd = jnp.where(is_even, own, other), jnp.where(is_even, other, own)
+            tiles = (even[:rows], unfold(even[rows:], odd[rows:]), odd[:rows])
+            for tile, value in enumerate(tiles):
+                start = LANES * (3 * (x * blocks + place) + tile)
+                scaled_ref[:, start : start + LANES] = value.astype(BF16)
+        where = slice(3 * LANES * blocks * x, 3 * LANES * blocks * (x + 1))
+        copies.append(pltpu.make_async_copy(scaled_ref.at[:, where], weight_out.at[:, where], written.at[x]))
+        copies[-1].start()
+    moment_out[...] = (moment_ref[...] / largest(spans[1:2])).astype(BF16)
+    grad_span_out[0] = jnp.max(spans[0:1])
+    moment_span_out[0] = jnp.max(spans[1:2])
+    weight_span_out[0] = jnp.max(spans[2:3])
+    for copy in copies:
+        copy.wait()
 
 
 def on_device(activations, output_grads, master, moment_q, moment_range, second_moment):
@@ -328,7 +329,6 @@
         compiler_params=grant(4),
     )(held)
     held = lax.all_gather(held, "x")
-    other = lax.ppermute(held, "core", swap)
     tops = pl.pallas_call(
         join_tops,
         out_shape=jax.ShapeDtypeStruct((cores * ys, 8, LANES), F32),
@@ -337,27 +337,16 @@
         compiler_params=grant(4),
     )(held)
     tops = lax.all_to_all(tops, ("core", "y"), 0, 0, tiled=True)
+    other = lax.ppermute(held, "core", swap)
 
     one = jax.ShapeDtypeStruct((1,), F32)
+    whole = jax.ShapeDtypeStruct((rows, width * xs * zs * cores), BF16)
     weight_q, moment_q_new, moment_span, weight_span, grad_span = pl.pallas_call(
         scale_weights,
-        grid=(xs,),
-        out_shape=(
-            jax.ShapeDtypeStruct((rows, width * xs * zs * cores), BF16),
-            jax.ShapeDtypeStruct((rows, width), BF16),
-            one,
-            one,
-            one,
-        ),
-        in_specs=[SMEM, VMEM, VMEM, VMEM, VMEM],
-        out_specs=(
-            pl.BlockSpec((rows, width * zs * cores), lambda i: (0, i)),
-            VMEM,
-            SMEM,
-            SMEM,
-            SMEM,
-        ),
-        scratch_shapes=[pltpu.VMEM((8, LANES), F32)],
+        out_shape=(whole, jax.ShapeDtypeStruct((rows, width), BF16), one, one, one),
+        in_specs=[SMEM] + [VMEM] * 4,
+        out_specs=(pl.BlockSpec(memory_space=pl.ANY), VMEM, SMEM, SMEM, SMEM),
+        scratch_shapes=[pltpu.VMEM(whole.shape, BF16), pltpu.SemaphoreType.DMA((xs,))],
         compiler_params=grant(8),
     )(place, tops, held, other, moment)
     return master_new, moment_q_new, moment_span, second_new, weight_q, weight_span, grad_span

time: 129 us -> 131 us (1.016)
  starting transfers between devices: 26.1 us -> 31.7 us
  blocking collectives: 91.9 us -> 88.2 us
    ppermute x1, starting transfers between devices: 4.04 us -> 9.68 us  [on_device(): other = lax.ppermute(held, 'core', swap)]
    all_to_all x1, blocking collectives: 16.1 us -> 12.4 us  [on_device(): held = lax.all_to_all(held, 'z', 0, 0, tiled=True)]
where the time goes in v9:
time: 131 us
  blocking collectives  88.2 us (67%)
  starting transfers between devices  31.7 us (24%)
  Pallas kernels  5.43 us (4%)
  waiting for transfers between devices  2.23 us (2%)
  local copies, waits for them, and re-layouts  1.93 us (1%)
  between operations  1.42 us (1%)
    all_to_all x1, blocking collectives, on_device(): value = lax.all_to_all(value, 'z', 0, 0, tiled=True)  18.6 us
    all_gather x1, blocking collectives, on_device(): even = lax.all_gather(output_grads.T, 'y', axis_index_groups=every_second)  17.7 us
    all_to_all x1, blocking collectives, on_device(): value = lax.all_to_all(value, 'x', 0, 0, tiled=True)  14.4 us
    all_to_all x1, blocking collectives, on_device(): tops = lax.all_to_all(tops, ('core', 'y'), 0, 0, tiled=True)  13.5 us
    all_to_all x1, blocking collectives, on_device(): held = lax.all_to_all(held, 'z', 0, 0, tiled=True)  12.4 us
    all_gather x1, blocking collectives, on_device(): held = lax.all_gather(held, 'x')  11.5 us
    ppermute x1, starting transfers between devices, on_device(): other = lax.ppermute(held, 'core', swap)  9.68 us
    ppermute x1, starting transfers between devices, on_device(): other_even = lax.ppermute(to_other_even, 'core', swap)  7.36 us
  transfers between devices with their start and end apart: 6, of which 2 were waited for; matrix products, arithmetic and copies ran while one was open for 0% of the time, Pallas kernels for 2%

profile of v9, /device:TPU:1, one launch (start us, length us, event | category | flops | bytes accessed | tf_op | source)
XLA Modules:
  0.0 131.0 jit_solution(6369887684891758259)
XLA Ops:
  0.6 17.7 %all-gather = bf16[256,1024]{1,0:T(8,128)(2,1)S(1)} all-gather(bf16[64,1024]{1,0:T(8,128)(2,1)} %bitcast.12), channel_id=2, replica_groups={{0,2,4,6},{1,3,5,7},{8,10,12,14},{9,11,13,15},{16,18,20,22},{17,19,21,2..., dimensions={0}, use_global_device_ids=true | all-gather | bytes 655360 | tf_op jit(solution)/shard_map/all_gather | solution.py:254
  18.4 1.9 %collective-permute-start = (bf16[2,64,1024]{2,1,0:T(8,128)(2,1)S(1)}, bf16[2,64,1024]{2,1,0:T(8,128)(2,1)S(1)}, u32[]{:S(2)}, u32[]{:S(2)}) collective-permute-start(bf16[2,64,1024]{2,1,0:T(8,128)(2,1)S(1)} %bitcast.11), channel_id=1, source_target_pairs={{0,7},{1,0},{2,1},{3,2},{4,3},{5,4},{6,5},{7,6},{8,15},{9,8},{10,9... | collective-permute-start | bytes 786440 | tf_op jit(solution)/shard_map/ppermute | solution.py:255
  20.3 3.4 %collective-permute-start.1 = (bf16[2,64,1024]{2,1,0:T(8,128)(2,1)S(1)}, bf16[2,64,1024]{2,1,0:T(8,128)(2,1)S(1)}, u32[]{:S(2)}, u32[]{:S(2)}) collective-permute-start(bf16[2,64,1024]{2,1,0:T(8,128)(2,1)S(1)} %bitcast.10), channel_id=1, source_target_pairs={{0,1},{1,2},{2,3},{3,4},{4,5},{5,6},{6,7},{7,0},{8,9},{9,10},{10,1... | collective-permute-start | bytes 786440 | tf_op jit(solution)/shard_map/ppermute | solution.py:256
  23.7 0.0 copy-start
  23.7 1.9 %copy-done = bf16[1024,1536]{1,0:T(8,128)(2,1)S(1)} copy-done((bf16[1024,1536]{1,0:T(8,128)(2,1)S(1)}, bf16[1024,1536]{1,0:T(8,128)(2,1)}, u32[]{:S(2)}) %copy-start) | copy-done | bytes 3145752
  25.6 0.0 copy-start.1
  25.6 1.0 shard_map.117
  26.6 7.4 %collective-permute-start.2 = (bf16[2,64,1536]{2,1,0:T(8,128)(2,1)S(1)}, bf16[2,64,1536]{2,1,0:T(8,128)(2,1)S(1)}, u32[]{:S(2)}, u32[]{:S(2)}) collective-permute-start(bf16[2,64,1536]{2,1,0:T(8,128)(2,1)S(1)} %get-tuple-element.31), channel_id=1, source_target_pairs={{0,8},{8,0},{1,9},{9,1},{2,10},{10,2},{3,11},{11,3},{4,12},{12,4},... | collective-permute-start | bytes 1179656 | tf_op jit(solution)/shard_map/ppermute | solution.py:284
  34.0 0.0 collective-permute-done.low_ref
  34.0 0.0 collective-permute-done.1.high_ref
  34.0 0.0 copy-done.1
  34.0 0.6 shard_map.118
  34.6 2.6 %collective-permute-start.3 = (bf16[2,64,1536]{2,1,0:T(8,128)(2,1)S(1)}, bf16[2,64,1536]{2,1,0:T(8,128)(2,1)S(1)}, u32[]{:S(2)}, u32[]{:S(2)}) collective-permute-start(bf16[2,64,1536]{2,1,0:T(8,128)(2,1)S(1)} %get-tuple-element.32), channel_id=1, source_target_pairs={{0,8},{8,0},{1,9},{9,1},{2,10},{10,2},{3,11},{11,3},{4,12},{12,4},... | collective-permute-start | bytes 1179656 | tf_op jit(solution)/shard_map/ppermute | solution.py:285
  37.2 0.6 shard_map.119
  37.8 0.0 collective-permute-done.2.other_even_ref
  37.9 0.7 collective-permute-done.3.other_odd_ref
  38.5 0.0 copy-start.2
  38.5 0.0 copy-start.3
  38.5 0.0 copy-start.4
  38.5 0.1 shard_map.120
  38.7 14.4 %all_to_all.20.parts_ref = bf16[4,64,1536]{2,1,0:T(8,128)(2,1)S(1)} all-to-all(bf16[4,64,1536]{2,1,0:T(8,128)(2,1)S(1)} %shard_map.120), channel_id=1, replica_groups=mesh['x'=4,'z'=8,'core'=2,'y'=8] {'x'}, dimensions={0} | all-to-all | bytes 1572864 | tf_op jit(solution)/shard_map/all_to_all | solution.py:293
  53.1 0.1 shard_map.121
  53.2 18.6 %all_to_all.21 = bf16[8,96,128]{2,1,0:T(8,128)(2,1)S(1)} all-to-all(bf16[8,96,128]{2,1,0:T(8,128)(2,1)S(1)} %shard_map.121), channel_id=1, replica_groups=mesh['x'=4,'z'=8,'core'=2,'y'=8] {'z'}, dimensions={0} | all-to-all | bytes 393216 | tf_op jit(solution)/shard_map/all_to_all | solution.py:301
  71.9 6.8 %collective-permute-start.4 = (f32[96,128]{1,0:T(8,128)S(1)}, f32[96,128]{1,0:T(8,128)S(1)}, u32[]{:S(2)}, u32[]{:S(2)}) collective-permute-start(f32[96,128]{1,0:T(8,128)S(1)} %convert_reduce_fusion), channel_id=1, source_target_pairs={{96,4},{112,12},{0,20},{16,28},{32,36},{48,44},{64,52},{80,60},{33... | collective-permute-start | bytes 147464 | tf_op jit(solution)/shard_map/ppermute | solution.py:312
  79.4 1.5 %collective-permute-done.4.summed_ref = f32[96,128]{1,0:T(8,128)S(1)} collective-permute-done((f32[96,128]{1,0:T(8,128)S(1)}, f32[96,128]{1,0:T(8,128)S(1)}, u32[]{:S(2)}, u32[]{:S(2)}) %collective-permute-start.4) | collective-permute-done | bytes 49184 | tf_op jit(solution)/shard_map/ppermute | solution.py:312
  80.9 0.0 copy-done.2
  80.9 0.0 copy-done.3
  80.9 0.0 copy-done.4
  80.9 0.8 shard_map.122
  81.8 12.4 %all_to_all.22.held_ref = bf16[8,112,128]{2,1,0:T(8,128)(2,1)S(1)} all-to-all(bf16[8,112,128]{2,1,0:T(8,128)(2,1)S(1)} %get-tuple-element.35), channel_id=1, replica_groups=mesh['x'=4,'z'=8,'core'=2,'y'=8] {'z'}, dimensions={0} | all-to-all | bytes 458752 | tf_op jit(solution)/shard_map/all_to_all | solution.py:323
  94.2 11.5 %all-gather.1 = bf16[3136,128]{1,0:T(8,128)(2,1)S(1)} all-gather(bf16[784,128]{1,0:T(8,128)(2,1)S(1)} %shard_map.123), channel_id=3, replica_groups=mesh['x'=4,'z'=8,'core'=2,'y'=8] {'x'}, dimensions={0}, use_global_device_ids=true | all-gather | bytes 1003520 | tf_op jit(solution)/shard_map/all_gather | solution.py:331
  105.7 9.7 %collective-permute-start.5 = (bf16[4,784,128]{2,1,0:T(8,128)(2,1)S(1)}, bf16[4,784,128]{2,1,0:T(8,128)(2,1)S(1)}, u32[]{:S(2)}, u32[]{:S(2)}) collective-permute-start(bf16[4,784,128]{2,1,0:T(8,128)(2,1)S(1)} %bitcast.6), channel_id=1, source_target_pairs={{0,8},{8,0},{1,9},{9,1},{2,10},{10,2},{3,11},{11,3},{4,12},{12,4},... | collective-permute-start | bytes 2408456 | tf_op jit(solution)/shard_map/ppermute | solution.py:340
  115.4 13.5 %all_to_all.23.tops_ref = f32[16,8,128]{2,1,0:T(8,128)S(1)} all-to-all(f32[16,8,128]{2,1,0:T(8,128)S(1)} %shard_map.124), channel_id=1, replica_groups=mesh['x'=4,'z'=8,'core'=2,'y'=8] {'core','y'}, dimensions={0} | all-to-all | bytes 131072 | tf_op jit(solution)/shard_map/all_to_all | solution.py:339
  128.9 0.0 collective-permute-done.5.other_ref
  128.9 2.0 %shard_map.125 = (bf16[64,12288]{1,0:T(8,128)(2,1)}, bf16[64,192]{1,0:T(8,128)(2,1)}, f32[1]{0:T(128)}, f32[1]{0:T(128)}, f32[1]{0:T(128)}) custom-call(s32[1]{0:T(128)} %bitcast.place_ref, f32[16,8,128]{2,1,0:T(8,128)S(1)} %all_to_all.23.tops_ref, bf16[4,784,128]{2,1,0:T(8,128)(2,1)S(1)} %bitcast.8, ...), custom_call_target="tpu_custom_call" | custom-call | tf_op jit(solution)/shard_map/pallas_call | solution.py:344
  (4 shorter events, 0.1 us)
Async XLA Ops:
  18.4 15.6 %collective-permute-start = (bf16[2,64,1024]{2,1,0:T(8,128)(2,1)S(1)}, bf16[2,64,1024]{2,1,0:T(8,128)(2,1)S(1)}, u32[]{:S(2)}, u32[]{:S(2)}) collective-permute-start(bf16[2,64,1024]{2,1,0:T(8,128)(2,1)S(1)} %bitcast.11), channel_id=1, source_target_pairs={{0,7},{1,0},{2,1},{3,2},{4,3},{5,4},{6,5},{7,6},{8,15},{9,8},{10,9... | collective-permute-start | bytes 786440 | tf_op jit(solution)/shard_map/ppermute | solution.py:255
  20.3 13.7 %collective-permute-start.1 = (bf16[2,64,1024]{2,1,0:T(8,128)(2,1)S(1)}, bf16[2,64,1024]{2,1,0:T(8,128)(2,1)S(1)}, u32[]{:S(2)}, u32[]{:S(2)}) collective-permute-start(bf16[2,64,1024]{2,1,0:T(8,128)(2,1)S(1)} %bitcast.10), channel_id=1, source_target_pairs={{0,1},{1,2},{2,3},{3,4},{4,5},{5,6},{6,7},{7,0},{8,9},{9,10},{10,1... | collective-permute-start | bytes 786440 | tf_op jit(solution)/shard_map/ppermute | solution.py:256
  23.7 1.9 %copy-start = (bf16[1024,1536]{1,0:T(8,128)(2,1)S(1)}, bf16[1024,1536]{1,0:T(8,128)(2,1)}, u32[]{:S(2)}) copy-start(bf16[1024,1536]{1,0:T(8,128)(2,1)} %activations_ref.5) | copy-start | bytes 9437188
  25.6 8.4 %copy-start.1 = (bf16[1024,1536]{1,0:T(8,128)(2,1)S(1)}, bf16[1024,1536]{1,0:T(8,128)(2,1)}, u32[]{:S(2)}) copy-start(bf16[1024,1536]{1,0:T(8,128)(2,1)} %activations_ref.5) | copy-start | bytes 9437188
  26.6 11.2 %collective-permute-start.2 = (bf16[2,64,1536]{2,1,0:T(8,128)(2,1)S(1)}, bf16[2,64,1536]{2,1,0:T(8,128)(2,1)S(1)}, u32[]{:S(2)}, u32[]{:S(2)}) collective-permute-start(bf16[2,64,1536]{2,1,0:T(8,128)(2,1)S(1)} %get-tuple-element.31), channel_id=1, source_target_pairs={{0,8},{8,0},{1,9},{9,1},{2,10},{10,2},{3,11},{11,3},{4,12},{12,4},... | collective-permute-start | bytes 1179656 | tf_op jit(solution)/shard_map/ppermute | solution.py:284
  34.6 3.9 %collective-permute-start.3 = (bf16[2,64,1536]{2,1,0:T(8,128)(2,1)S(1)}, bf16[2,64,1536]{2,1,0:T(8,128)(2,1)S(1)}, u32[]{:S(2)}, u32[]{:S(2)}) collective-permute-start(bf16[2,64,1536]{2,1,0:T(8,128)(2,1)S(1)} %get-tuple-element.32), channel_id=1, source_target_pairs={{0,8},{8,0},{1,9},{9,1},{2,10},{10,2},{3,11},{11,3},{4,12},{12,4},... | collective-permute-start | bytes 1179656 | tf_op jit(solution)/shard_map/ppermute | solution.py:285
  38.5 42.4 %copy-start.2 = (f32[64,192]{1,0:T(8,128)S(1)}, f32[64,192]{1,0:T(8,128)}, u32[]{:S(2)}) copy-start(f32[64,192]{1,0:T(8,128)} %master_ref.1) | copy-start | bytes 147460
  38.5 42.4 %copy-start.3 = (f32[64,192]{1,0:T(8,128)S(1)}, f32[64,192]{1,0:T(8,128)}, u32[]{:S(2)}) copy-start(f32[64,192]{1,0:T(8,128)} %second_ref.1) | copy-start | bytes 147460
  38.5 42.4 %copy-start.4 = (bf16[64,192]{1,0:T(8,128)(2,1)S(1)}, bf16[64,192]{1,0:T(8,128)(2,1)}, u32[]{:S(2)}) copy-start(bf16[64,192]{1,0:T(8,128)(2,1)} %moment_ref.1) | copy-start | bytes 73732
  71.9 9.0 %collective-permute-start.4 = (f32[96,128]{1,0:T(8,128)S(1)}, f32[96,128]{1,0:T(8,128)S(1)}, u32[]{:S(2)}, u32[]{:S(2)}) collective-permute-start(f32[96,128]{1,0:T(8,128)S(1)} %convert_reduce_fusion), channel_id=1, source_target_pairs={{96,4},{112,12},{0,20},{16,28},{32,36},{48,44},{64,52},{80,60},{33... | collective-permute-start | bytes 147464 | tf_op jit(solution)/shard_map/ppermute | solution.py:312
  105.7 23.2 %collective-permute-start.5 = (bf16[4,784,128]{2,1,0:T(8,128)(2,1)S(1)}, bf16[4,784,128]{2,1,0:T(8,128)(2,1)S(1)}, u32[]{:S(2)}, u32[]{:S(2)}) collective-permute-start(bf16[4,784,128]{2,1,0:T(8,128)(2,1)S(1)} %bitcast.6), channel_id=1, source_target_pairs={{0,8},{8,0},{1,9},{9,1},{2,10},{10,2},{3,11},{11,3},{4,12},{12,4},... | collective-permute-start | bytes 2408456 | tf_op jit(solution)/shard_map/ppermute | solution.py:340

commit v10 on v7

--- a/solution.py
+++ b/solution.py
@@ -115,12 +115,12 @@
     top_out[...] = multiply(grads, activations_ref, None, other_out, own_out)
 
 
-def multiply_odd(of_other, place_ref, low_ref, high_ref, activations_ref, top_ref, out_ref, top_out):
+def multiply_odd(of_other, place_ref, first_ref, second_ref, activations_ref, top_ref, out_ref, top_out):
     core, y = core_and_y(place_ref)
     grads = []
     for which in range(2):
         block = block_of(1 - core if of_other else core, 1, which, y)[1] // 2
-        grads.append(jnp.where(block < 2, low_ref[block % 2], high_ref[block % 2]))
+        grads.append(jnp.where(block // 2 == core, first_ref[block % 2], second_ref[block % 2]))
     top_out[...] = multiply(grads, activations_ref, top_ref[...], out_ref)
 
 
@@ -251,8 +251,18 @@
     tokens, columns = output_grads.shape
     every_second = [list(range(first, ys, 2)) for first in range(2)]
     even = lax.all_gather(output_grads.T, "y", axis_index_groups=every_second)
-    low = lax.ppermute(even[: ys // 4], "y", [(y, (y - 1) % ys) for y in range(ys)])
-    high = lax.ppermute(even[ys // 4 :], "y", [(y, (y + 1) % ys) for y in range(ys)])
+    half = ys // 4
+    down = [(y, (y - 1) % ys) for y in range(ys)]
+    up = [(y, (y + 1) % ys) for y in range(ys)]
+
+    def both(first, second):
+        return [(own, to) for own, to in first] + [(ys + own, ys + to) for own, to in second]
+
+    core = lax.axis_index("core")
+    first = lax.dynamic_slice_in_dim(even, core * half, half, 0)
+    second = lax.dynamic_slice_in_dim(even, (1 - core) * half, half, 0)
+    first = lax.ppermute(first, ("core", "y"), both(down, up))
+    second = lax.ppermute(second, ("core", "y"), both(up, down))
 
     def product(dtype):
         return jax.ShapeDtypeStruct((2, columns, activations.shape[1]), dtype)
@@ -263,22 +273,22 @@
         out_shape=(product(BF16), product(F32), top_shape),
         in_specs=[SMEM, VMEM, VMEM],
         out_specs=(VMEM,) * 3,
-        compiler_params=grant(14),
+        compiler_params=grant(8),
     )(place, even, activations)
     to_other_odd, top = pl.pallas_call(
         functools.partial(multiply_odd, True),
         out_shape=(product(BF16), top_shape),
         in_specs=[SMEM] + [VMEM] * 4,
         out_specs=(VMEM, VMEM),
-        compiler_params=grant(14),
-    )(place, low, high, activations, top)
+        compiler_params=grant(8),
+    )(place, first, second, activations, top)
     own_odd, top = pl.pallas_call(
         functools.partial(multiply_odd, False),
         out_shape=(product(F32), top_shape),
         in_specs=[SMEM] + [VMEM] * 4,
         out_specs=(VMEM, VMEM),
-        compiler_params=grant(14),
-    )(place, low, high, activations, top)
+        compiler_params=grant(8),
+    )(place, first, second, activations, top)
 
     other_even = lax.ppermute(to_other_even, "core", swap)
     other_odd = lax.ppermute(to_other_odd, "core", swap)

time: 129 us -> 132 us (1.023)
  blocking collectives: 91.9 us -> 93.6 us
  waiting for transfers between devices: 2.23 us -> 3.85 us
    all_to_all x1, blocking collectives: 13 us -> 14.7 us  [on_device(): tops = lax.all_to_all(tops, ('core', 'y'), 0, 0, tiled=True)]
where the time goes in v10:
time: 132 us
  blocking collectives  93.6 us (71%)
  starting transfers between devices  25.4 us (19%)
  Pallas kernels  5.42 us (4%)
  waiting for transfers between devices  3.85 us (3%)
  local copies, waits for them, and re-layouts  1.93 us (1%)
  between operations  1.43 us (1%)
    all_to_all x1, blocking collectives, on_device(): value = lax.all_to_all(value, 'z', 0, 0, tiled=True)  18.4 us
    all_gather x1, blocking collectives, on_device(): even = lax.all_gather(output_grads.T, 'y', axis_index_groups=every_second)  17.7 us
    all_to_all x1, blocking collectives, on_device(): held = lax.all_to_all(held, 'z', 0, 0, tiled=True)  15.3 us
    all_to_all x1, blocking collectives, on_device(): value = lax.all_to_all(value, 'x', 0, 0, tiled=True)  15 us
    all_to_all x1, blocking collectives, on_device(): tops = lax.all_to_all(tops, ('core', 'y'), 0, 0, tiled=True)  14.7 us
    all_gather x1, blocking collectives, on_device(): held = lax.all_gather(held, 'x')  12.4 us
    ppermute x1, starting transfers between devices, on_device(): other_even = lax.ppermute(to_other_even, 'core', swap)  8.56 us
    ppermute x1, starting transfers between devices, on_device(): value = lax.ppermute(value, DEVICE, route)  5.59 us
  transfers between devices with their start and end apart: 6, of which 2 were waited for; matrix products, arithmetic and copies ran while one was open for 0% of the time, Pallas kernels for 2%

profile of v10, /device:TPU:1, one launch (start us, length us, event | category | flops | bytes accessed | tf_op | source)
XLA Modules:
  0.0 131.7 jit_solution(17918632715239207328)
XLA Ops:
  0.6 17.7 %all-gather = bf16[256,1024]{1,0:T(8,128)(2,1)S(1)} all-gather(bf16[64,1024]{1,0:T(8,128)(2,1)} %bitcast.9), channel_id=2, replica_groups={{0,2,4,6},{1,3,5,7},{8,10,12,14},{9,11,13,15},{16,18,20,22},{17,19,21,2..., dimensions={0}, use_global_device_ids=true | all-gather | bytes 655360 | tf_op jit(solution)/shard_map/all_gather | solution.py:253
  18.4 1.9 %collective-permute-start.1 = (bf16[2,64,1024]{2,1,0:T(8,128)(2,1)S(1)}, bf16[2,64,1024]{2,1,0:T(8,128)(2,1)S(1)}, u32[]{:S(2)}, u32[]{:S(2)}) collective-permute-start(bf16[2,64,1024]{2,1,0:T(8,128)(2,1)S(1)} %get-tuple-element.43), channel_id=1, source_target_pairs={{0,1},{1,2},{2,3},{3,4},{4,5},{5,6},{6,7},{7,0},{8,15},{9,8},{10,9... | collective-permute-start | bytes 786440 | tf_op jit(solution)/shard_map/ppermute | solution.py:265
  20.3 3.4 %collective-permute-start = (bf16[2,64,1024]{2,1,0:T(8,128)(2,1)S(1)}, bf16[2,64,1024]{2,1,0:T(8,128)(2,1)S(1)}, u32[]{:S(2)}, u32[]{:S(2)}) collective-permute-start(bf16[2,64,1024]{2,1,0:T(8,128)(2,1)S(1)} %get-tuple-element.44), channel_id=1, source_target_pairs={{0,7},{1,0},{2,1},{3,2},{4,3},{5,4},{6,5},{7,6},{8,9},{9,10},{10,1... | collective-permute-start | bytes 786440 | tf_op jit(solution)/shard_map/ppermute | solution.py:264
  23.7 0.0 copy-start
  23.7 1.9 %copy-done = bf16[1024,1536]{1,0:T(8,128)(2,1)S(1)} copy-done((bf16[1024,1536]{1,0:T(8,128)(2,1)S(1)}, bf16[1024,1536]{1,0:T(8,128)(2,1)}, u32[]{:S(2)}) %copy-start) | copy-done | bytes 3145752
  25.6 0.0 copy-start.1
  25.6 1.0 shard_map.117
  26.6 8.6 %collective-permute-start.2 = (bf16[2,64,1536]{2,1,0:T(8,128)(2,1)S(1)}, bf16[2,64,1536]{2,1,0:T(8,128)(2,1)S(1)}, u32[]{:S(2)}, u32[]{:S(2)}) collective-permute-start(bf16[2,64,1536]{2,1,0:T(8,128)(2,1)S(1)} %get-tuple-element.31), channel_id=1, source_target_pairs={{0,8},{8,0},{1,9},{9,1},{2,10},{10,2},{3,11},{11,3},{4,12},{12,4},... | collective-permute-start | bytes 1179656 | tf_op jit(solution)/shard_map/ppermute | solution.py:293
  35.2 0.0 collective-permute-done.1.second_ref
  35.2 0.0 collective-permute-done.first_ref
  35.2 0.0 copy-done.1
  35.2 0.6 shard_map.118
  35.8 1.9 %collective-permute-start.3 = (bf16[2,64,1536]{2,1,0:T(8,128)(2,1)S(1)}, bf16[2,64,1536]{2,1,0:T(8,128)(2,1)S(1)}, u32[]{:S(2)}, u32[]{:S(2)}) collective-permute-start(bf16[2,64,1536]{2,1,0:T(8,128)(2,1)S(1)} %get-tuple-element.32), channel_id=1, source_target_pairs={{0,8},{8,0},{1,9},{9,1},{2,10},{10,2},{3,11},{11,3},{4,12},{12,4},... | collective-permute-start | bytes 1179656 | tf_op jit(solution)/shard_map/ppermute | solution.py:294
  37.8 0.6 shard_map.119
  38.4 0.0 collective-permute-done.2.other_even_ref
  38.4 1.1 collective-permute-done.3.other_odd_ref
  39.4 0.0 copy-start.2
  39.4 0.0 copy-start.3
  39.4 0.0 copy-start.4
  39.4 0.1 shard_map.120
  39.6 15.0 %all_to_all.20.parts_ref = bf16[4,64,1536]{2,1,0:T(8,128)(2,1)S(1)} all-to-all(bf16[4,64,1536]{2,1,0:T(8,128)(2,1)S(1)} %shard_map.120), channel_id=1, replica_groups=mesh['x'=4,'z'=8,'core'=2,'y'=8] {'x'}, dimensions={0} | all-to-all | bytes 1572864 | tf_op jit(solution)/shard_map/all_to_all | solution.py:302
  54.6 0.1 shard_map.121
  54.7 18.4 %all_to_all.21 = bf16[8,96,128]{2,1,0:T(8,128)(2,1)S(1)} all-to-all(bf16[8,96,128]{2,1,0:T(8,128)(2,1)S(1)} %shard_map.121), channel_id=1, replica_groups=mesh['x'=4,'z'=8,'core'=2,'y'=8] {'z'}, dimensions={0} | all-to-all | bytes 393216 | tf_op jit(solution)/shard_map/all_to_all | solution.py:310
  73.2 5.6 %collective-permute-start.4 = (f32[96,128]{1,0:T(8,128)S(1)}, f32[96,128]{1,0:T(8,128)S(1)}, u32[]{:S(2)}, u32[]{:S(2)}) collective-permute-start(f32[96,128]{1,0:T(8,128)S(1)} %convert_reduce_fusion), channel_id=1, source_target_pairs={{0,4},{112,12},{16,20},{96,28},{32,36},{80,44},{48,52},{64,60},{65... | collective-permute-start | bytes 147464 | tf_op jit(solution)/shard_map/ppermute | solution.py:321
  79.4 2.8 %collective-permute-done.4.summed_ref = f32[96,128]{1,0:T(8,128)S(1)} collective-permute-done((f32[96,128]{1,0:T(8,128)S(1)}, f32[96,128]{1,0:T(8,128)S(1)}, u32[]{:S(2)}, u32[]{:S(2)}) %collective-permute-start.4) | collective-permute-done | bytes 49184 | tf_op jit(solution)/shard_map/ppermute | solution.py:321
  82.2 0.0 copy-done.2
  82.2 0.0 copy-done.3
  82.2 0.0 copy-done.4
  82.2 0.8 shard_map.122
  83.0 15.3 %all_to_all.22.held_ref = bf16[8,112,128]{2,1,0:T(8,128)(2,1)S(1)} all-to-all(bf16[8,112,128]{2,1,0:T(8,128)(2,1)S(1)} %get-tuple-element.35), channel_id=1, replica_groups=mesh['x'=4,'z'=8,'core'=2,'y'=8] {'z'}, dimensions={0} | all-to-all | bytes 458752 | tf_op jit(solution)/shard_map/all_to_all | solution.py:332
  98.4 12.4 %all-gather.1 = bf16[3136,128]{1,0:T(8,128)(2,1)S(1)} all-gather(bf16[784,128]{1,0:T(8,128)(2,1)S(1)} %shard_map.123), channel_id=3, replica_groups=mesh['x'=4,'z'=8,'core'=2,'y'=8] {'x'}, dimensions={0}, use_global_device_ids=true | all-gather | bytes 1003520 | tf_op jit(solution)/shard_map/all_gather | solution.py:340
  110.8 4.0 %collective-permute-start.5 = (bf16[4,784,128]{2,1,0:T(8,128)(2,1)S(1)}, bf16[4,784,128]{2,1,0:T(8,128)(2,1)S(1)}, u32[]{:S(2)}, u32[]{:S(2)}) collective-permute-start(bf16[4,784,128]{2,1,0:T(8,128)(2,1)S(1)} %bitcast.4), channel_id=1, source_target_pairs={{0,8},{8,0},{1,9},{9,1},{2,10},{10,2},{3,11},{11,3},{4,12},{12,4},... | collective-permute-start | bytes 2408456 | tf_op jit(solution)/shard_map/ppermute | solution.py:341
  114.9 14.7 %all_to_all.23.tops_ref = f32[16,8,128]{2,1,0:T(8,128)S(1)} all-to-all(f32[16,8,128]{2,1,0:T(8,128)S(1)} %shard_map.124), channel_id=1, replica_groups=mesh['x'=4,'z'=8,'core'=2,'y'=8] {'core','y'}, dimensions={0} | all-to-all | bytes 131072 | tf_op jit(solution)/shard_map/all_to_all | solution.py:349
  129.6 0.0 collective-permute-done.5.other_ref
  129.6 2.0 %shard_map.125 = (bf16[64,12288]{1,0:T(8,128)(2,1)}, bf16[64,192]{1,0:T(8,128)(2,1)}, f32[1]{0:T(128)}, f32[1]{0:T(128)}, f32[1]{0:T(128)}) custom-call(s32[1]{0:T(128)} %bitcast.place_ref, f32[16,8,128]{2,1,0:T(8,128)S(1)} %all_to_all.23.tops_ref, bf16[4,784,128]{2,1,0:T(8,128)(2,1)S(1)} %bitcast.6, ...), custom_call_target="tpu_custom_call" | custom-call | tf_op jit(solution)/shard_map/pallas_call | solution.py:352
  (4 shorter events, 0.1 us)
Async XLA Ops:
  18.4 16.8 %collective-permute-start.1 = (bf16[2,64,1024]{2,1,0:T(8,128)(2,1)S(1)}, bf16[2,64,1024]{2,1,0:T(8,128)(2,1)S(1)}, u32[]{:S(2)}, u32[]{:S(2)}) collective-permute-start(bf16[2,64,1024]{2,1,0:T(8,128)(2,1)S(1)} %get-tuple-element.43), channel_id=1, source_target_pairs={{0,1},{1,2},{2,3},{3,4},{4,5},{5,6},{6,7},{7,0},{8,15},{9,8},{10,9... | collective-permute-start | bytes 786440 | tf_op jit(solution)/shard_map/ppermute | solution.py:265
  20.3 14.9 %collective-permute-start = (bf16[2,64,1024]{2,1,0:T(8,128)(2,1)S(1)}, bf16[2,64,1024]{2,1,0:T(8,128)(2,1)S(1)}, u32[]{:S(2)}, u32[]{:S(2)}) collective-permute-start(bf16[2,64,1024]{2,1,0:T(8,128)(2,1)S(1)} %get-tuple-element.44), channel_id=1, source_target_pairs={{0,7},{1,0},{2,1},{3,2},{4,3},{5,4},{6,5},{7,6},{8,9},{9,10},{10,1... | collective-permute-start | bytes 786440 | tf_op jit(solution)/shard_map/ppermute | solution.py:264
  23.7 1.9 %copy-start = (bf16[1024,1536]{1,0:T(8,128)(2,1)S(1)}, bf16[1024,1536]{1,0:T(8,128)(2,1)}, u32[]{:S(2)}) copy-start(bf16[1024,1536]{1,0:T(8,128)(2,1)} %activations_ref.5) | copy-start | bytes 9437188
  25.6 9.6 %copy-start.1 = (bf16[1024,1536]{1,0:T(8,128)(2,1)S(1)}, bf16[1024,1536]{1,0:T(8,128)(2,1)}, u32[]{:S(2)}) copy-start(bf16[1024,1536]{1,0:T(8,128)(2,1)} %activations_ref.5) | copy-start | bytes 9437188
  26.6 11.8 %collective-permute-start.2 = (bf16[2,64,1536]{2,1,0:T(8,128)(2,1)S(1)}, bf16[2,64,1536]{2,1,0:T(8,128)(2,1)S(1)}, u32[]{:S(2)}, u32[]{:S(2)}) collective-permute-start(bf16[2,64,1536]{2,1,0:T(8,128)(2,1)S(1)} %get-tuple-element.31), channel_id=1, source_target_pairs={{0,8},{8,0},{1,9},{9,1},{2,10},{10,2},{3,11},{11,3},{4,12},{12,4},... | collective-permute-start | bytes 1179656 | tf_op jit(solution)/shard_map/ppermute | solution.py:293
  35.8 3.6 %collective-permute-start.3 = (bf16[2,64,1536]{2,1,0:T(8,128)(2,1)S(1)}, bf16[2,64,1536]{2,1,0:T(8,128)(2,1)S(1)}, u32[]{:S(2)}, u32[]{:S(2)}) collective-permute-start(bf16[2,64,1536]{2,1,0:T(8,128)(2,1)S(1)} %get-tuple-element.32), channel_id=1, source_target_pairs={{0,8},{8,0},{1,9},{9,1},{2,10},{10,2},{3,11},{11,3},{4,12},{12,4},... | collective-permute-start | bytes 1179656 | tf_op jit(solution)/shard_map/ppermute | solution.py:294
  39.4 42.7 %copy-start.2 = (f32[64,192]{1,0:T(8,128)S(1)}, f32[64,192]{1,0:T(8,128)}, u32[]{:S(2)}) copy-start(f32[64,192]{1,0:T(8,128)} %master_ref.1) | copy-start | bytes 147460
  39.4 42.7 %copy-start.3 = (f32[64,192]{1,0:T(8,128)S(1)}, f32[64,192]{1,0:T(8,128)}, u32[]{:S(2)}) copy-start(f32[64,192]{1,0:T(8,128)} %second_ref.1) | copy-start | bytes 147460
  39.4 42.7 %copy-start.4 = (bf16[64,192]{1,0:T(8,128)(2,1)S(1)}, bf16[64,192]{1,0:T(8,128)(2,1)}, u32[]{:S(2)}) copy-start(bf16[64,192]{1,0:T(8,128)(2,1)} %moment_ref.1) | copy-start | bytes 73732
  73.2 9.0 %collective-permute-start.4 = (f32[96,128]{1,0:T(8,128)S(1)}, f32[96,128]{1,0:T(8,128)S(1)}, u32[]{:S(2)}, u32[]{:S(2)}) collective-permute-start(f32[96,128]{1,0:T(8,128)S(1)} %convert_reduce_fusion), channel_id=1, source_target_pairs={{0,4},{112,12},{16,20},{96,28},{32,36},{80,44},{48,52},{64,60},{65... | collective-permute-start | bytes 147464 | tf_op jit(solution)/shard_map/ppermute | solution.py:321
  110.8 18.8 %collective-permute-start.5 = (bf16[4,784,128]{2,1,0:T(8,128)(2,1)S(1)}, bf16[4,784,128]{2,1,0:T(8,128)(2,1)S(1)}, u32[]{:S(2)}, u32[]{:S(2)}) collective-permute-start(bf16[4,784,128]{2,1,0:T(8,128)(2,1)S(1)} %bitcast.4), channel_id=1, source_target_pairs={{0,8},{8,0},{1,9},{9,1},{2,10},{10,2},{3,11},{11,3},{4,12},{12,4},... | collective-permute-start | bytes 2408456 | tf_op jit(solution)/shard_map/ppermute | solution.py:341

commit v11 on v7

--- a/solution.py
+++ b/solution.py
@@ -129,7 +129,7 @@
     for odd, own_ref, other_ref in ((0, own_even_ref, other_even_ref), (1, own_odd_ref, other_odd_ref)):
         for which in range(2):
             x = block_of(core, odd, which, y)[0]
-            out_ref[x] = (own_ref[which] + other_ref[which].astype(F32)).astype(BF16)
+            out_ref[x] = (own_ref[which] + other_ref[which]).astype(BF16)
 
 
 def add_and_cut(place_ref, parts_ref, out_ref):
@@ -147,8 +147,8 @@
         middle = total(3 * pair + 1)
         for odd in range(2):
             slot = slot_of(2 * pair + odd, y)
-            out_ref[slot, :rows] = total(3 * pair + 2 * odd).astype(BF16)
-            out_ref[slot, rows:] = fold(middle, odd).astype(BF16)
+            out_ref[slot, :rows] = total(3 * pair + 2 * odd)
+            out_ref[slot, rows:] = fold(middle, odd)
 
 
 def adam_step(
@@ -260,14 +260,14 @@
     top_shape = jax.ShapeDtypeStruct((8, LANES), F32)
     to_other_even, own_even, top = pl.pallas_call(
         multiply_even,
-        out_shape=(product(BF16), product(F32), top_shape),
+        out_shape=(product(F32), product(F32), top_shape),
         in_specs=[SMEM, VMEM, VMEM],
         out_specs=(VMEM,) * 3,
         compiler_params=grant(14),
     )(place, even, activations)
     to_other_odd, top = pl.pallas_call(
         functools.partial(multiply_odd, True),
-        out_shape=(product(BF16), top_shape),
+        out_shape=(product(F32), top_shape),
         in_specs=[SMEM] + [VMEM] * 4,
         out_specs=(VMEM, VMEM),
         compiler_params=grant(14),
@@ -292,13 +292,13 @@
     value = lax.all_to_all(value, "x", 0, 0, tiled=True)
     value = pl.pallas_call(
         add_and_cut,
-        out_shape=jax.ShapeDtypeStruct((zs, packed, LANES), BF16),
+        out_shape=jax.ShapeDtypeStruct((zs, packed, LANES), F32),
         in_specs=[SMEM, VMEM],
         out_specs=VMEM,
         compiler_params=grant(4),
     )(place, value)
     value = lax.all_to_all(value, "z", 0, 0, tiled=True)
-    value = jnp.sum(value.astype(F32), axis=0)
+    value = jnp.sum(value, axis=0)
     route = []
     for half in range(cores):
         for odd in range(2):

time: 129 us -> 135 us (1.047)
  blocking collectives: 91.9 us -> 96.2 us
    all_to_all x1, blocking collectives: 18.6 us -> 21.6 us  [on_device(): value = lax.all_to_all(value, 'z', 0, 0, tiled=True)]
where the time goes in v11:
time: 135 us; the launch traced here: 134 us
  blocking collectives  96.2 us (71%)
  starting transfers between devices  27.3 us (20%)
  Pallas kernels  5.42 us (4%)
  local copies, waits for them, and re-layouts  1.93 us (1%)
  waiting for transfers between devices  1.79 us (1%)
  between operations  1.42 us (1%)
    all_to_all x1, blocking collectives, on_device(): value = lax.all_to_all(value, 'z', 0, 0, tiled=True)  21.6 us
    all_gather x1, blocking collectives, on_device(): even = lax.all_gather(output_grads.T, 'y', axis_index_groups=every_second)  17.7 us
    all_to_all x1, blocking collectives, on_device(): held = lax.all_to_all(held, 'z', 0, 0, tiled=True)  16.7 us
    all_to_all x1, blocking collectives, on_device(): value = lax.all_to_all(value, 'x', 0, 0, tiled=True)  14.4 us
    all_to_all x1, blocking collectives, on_device(): tops = lax.all_to_all(tops, ('core', 'y'), 0, 0, tiled=True)  13.3 us
    all_gather x1, blocking collectives, on_device(): held = lax.all_gather(held, 'x')  12.4 us
    ppermute x1, starting transfers between devices, on_device(): value = lax.ppermute(value, DEVICE, route)  8.09 us
    ppermute x1, starting transfers between devices, on_device(): other_even = lax.ppermute(to_other_even, 'core', swap)  7.36 us
  transfers between devices with their start and end apart: 6, of which 2 were waited for; matrix products, arithmetic and copies ran while one was open for 0% of the time, Pallas kernels for 2%

profile of v11, /device:TPU:1, one launch (start us, length us, event | category | flops | bytes accessed | tf_op | source)
XLA Modules:
  0.0 134.0 jit_solution(9882458540728138567)
XLA Ops:
  0.6 17.7 %all-gather = bf16[256,1024]{1,0:T(8,128)(2,1)S(1)} all-gather(bf16[64,1024]{1,0:T(8,128)(2,1)} %bitcast.12), channel_id=2, replica_groups={{0,2,4,6},{1,3,5,7},{8,10,12,14},{9,11,13,15},{16,18,20,22},{17,19,21,2..., dimensions={0}, use_global_device_ids=true | all-gather | bytes 655360 | tf_op jit(solution)/shard_map/all_gather | solution.py:253
  18.4 1.9 %collective-permute-start = (bf16[2,64,1024]{2,1,0:T(8,128)(2,1)S(1)}, bf16[2,64,1024]{2,1,0:T(8,128)(2,1)S(1)}, u32[]{:S(2)}, u32[]{:S(2)}) collective-permute-start(bf16[2,64,1024]{2,1,0:T(8,128)(2,1)S(1)} %bitcast.11), channel_id=1, source_target_pairs={{0,7},{1,0},{2,1},{3,2},{4,3},{5,4},{6,5},{7,6},{8,15},{9,8},{10,9... | collective-permute-start | bytes 786440 | tf_op jit(solution)/shard_map/ppermute | solution.py:254
  20.3 3.4 %collective-permute-start.1 = (bf16[2,64,1024]{2,1,0:T(8,128)(2,1)S(1)}, bf16[2,64,1024]{2,1,0:T(8,128)(2,1)S(1)}, u32[]{:S(2)}, u32[]{:S(2)}) collective-permute-start(bf16[2,64,1024]{2,1,0:T(8,128)(2,1)S(1)} %bitcast.10), channel_id=1, source_target_pairs={{0,1},{1,2},{2,3},{3,4},{4,5},{5,6},{6,7},{7,0},{8,9},{9,10},{10,1... | collective-permute-start | bytes 786440 | tf_op jit(solution)/shard_map/ppermute | solution.py:255
  23.7 0.0 copy-start
  23.7 1.9 %copy-done = bf16[1024,1536]{1,0:T(8,128)(2,1)S(1)} copy-done((bf16[1024,1536]{1,0:T(8,128)(2,1)S(1)}, bf16[1024,1536]{1,0:T(8,128)(2,1)}, u32[]{:S(2)}) %copy-start) | copy-done | bytes 3145752
  25.6 0.0 copy-start.1
  25.6 1.0 shard_map.117
  26.6 7.4 %collective-permute-start.2 = (f32[2,64,1536]{2,1,0:T(8,128)S(1)}, f32[2,64,1536]{2,1,0:T(8,128)S(1)}, u32[]{:S(2)}, u32[]{:S(2)}) collective-permute-start(f32[2,64,1536]{2,1,0:T(8,128)S(1)} %get-tuple-element.31), channel_id=1, source_target_pairs={{0,8},{8,0},{1,9},{9,1},{2,10},{10,2},{3,11},{11,3},{4,12},{12,4},... | collective-permute-start | bytes 2359304 | tf_op jit(solution)/shard_map/ppermute | solution.py:283
  34.0 0.0 collective-permute-done.low_ref
  34.0 0.0 collective-permute-done.1.high_ref
  34.0 0.0 copy-done.1
  34.0 0.6 shard_map.118
  34.6 2.6 %collective-permute-start.3 = (f32[2,64,1536]{2,1,0:T(8,128)S(1)}, f32[2,64,1536]{2,1,0:T(8,128)S(1)}, u32[]{:S(2)}, u32[]{:S(2)}) collective-permute-start(f32[2,64,1536]{2,1,0:T(8,128)S(1)} %get-tuple-element.32), channel_id=1, source_target_pairs={{0,8},{8,0},{1,9},{9,1},{2,10},{10,2},{3,11},{11,3},{4,12},{12,4},... | collective-permute-start | bytes 2359304 | tf_op jit(solution)/shard_map/ppermute | solution.py:284
  37.2 0.6 shard_map.119
  37.8 0.0 collective-permute-done.2.other_even_ref
  37.8 1.3 collective-permute-done.3.other_odd_ref
  39.1 0.0 copy-start.2
  39.1 0.0 copy-start.3
  39.1 0.0 copy-start.4
  39.1 0.1 shard_map.120
  39.3 14.4 %all_to_all.20.parts_ref = bf16[4,64,1536]{2,1,0:T(8,128)(2,1)S(1)} all-to-all(bf16[4,64,1536]{2,1,0:T(8,128)(2,1)S(1)} %shard_map.120), channel_id=1, replica_groups=mesh['x'=4,'z'=8,'core'=2,'y'=8] {'x'}, dimensions={0} | all-to-all | bytes 1572864 | tf_op jit(solution)/shard_map/all_to_all | solution.py:292
  53.7 0.1 shard_map.121
  53.8 21.6 %all_to_all.21 = f32[8,96,128]{2,1,0:T(8,128)S(1)} all-to-all(f32[8,96,128]{2,1,0:T(8,128)S(1)} %shard_map.121), channel_id=1, replica_groups=mesh['x'=4,'z'=8,'core'=2,'y'=8] {'z'}, dimensions={0} | all-to-all | bytes 786432 | tf_op jit(solution)/shard_map/all_to_all | solution.py:300
  75.4 8.1 %collective-permute-start.4 = (f32[96,128]{1,0:T(8,128)S(1)}, f32[96,128]{1,0:T(8,128)S(1)}, u32[]{:S(2)}, u32[]{:S(2)}) collective-permute-start(f32[96,128]{1,0:T(8,128)S(1)} %reduce_sum.9), channel_id=1, source_target_pairs={{0,4},{112,12},{16,20},{96,28},{32,36},{80,44},{48,52},{64,60},{65... | collective-permute-start | bytes 147464 | tf_op jit(solution)/shard_map/ppermute | solution.py:311
  84.2 0.5 collective-permute-done.4.summed_ref
  84.7 0.0 copy-done.2
  84.7 0.0 copy-done.3
  84.7 0.0 copy-done.4
  84.7 0.8 shard_map.122
  85.5 16.7 %all_to_all.22.held_ref = bf16[8,112,128]{2,1,0:T(8,128)(2,1)S(1)} all-to-all(bf16[8,112,128]{2,1,0:T(8,128)(2,1)S(1)} %get-tuple-element.35), channel_id=1, replica_groups=mesh['x'=4,'z'=8,'core'=2,'y'=8] {'z'}, dimensions={0} | all-to-all | bytes 458752 | tf_op jit(solution)/shard_map/all_to_all | solution.py:322
  102.3 12.4 %all-gather.1 = bf16[3136,128]{1,0:T(8,128)(2,1)S(1)} all-gather(bf16[784,128]{1,0:T(8,128)(2,1)S(1)} %shard_map.123), channel_id=3, replica_groups=mesh['x'=4,'z'=8,'core'=2,'y'=8] {'x'}, dimensions={0}, use_global_device_ids=true | all-gather | bytes 1003520 | tf_op jit(solution)/shard_map/all_gather | solution.py:330
  114.7 4.0 %collective-permute-start.5 = (bf16[4,784,128]{2,1,0:T(8,128)(2,1)S(1)}, bf16[4,784,128]{2,1,0:T(8,128)(2,1)S(1)}, u32[]{:S(2)}, u32[]{:S(2)}) collective-permute-start(bf16[4,784,128]{2,1,0:T(8,128)(2,1)S(1)} %bitcast.6), channel_id=1, source_target_pairs={{0,8},{8,0},{1,9},{9,1},{2,10},{10,2},{3,11},{11,3},{4,12},{12,4},... | collective-permute-start | bytes 2408456 | tf_op jit(solution)/shard_map/ppermute | solution.py:331
  118.7 13.3 %all_to_all.23.tops_ref = f32[16,8,128]{2,1,0:T(8,128)S(1)} all-to-all(f32[16,8,128]{2,1,0:T(8,128)S(1)} %shard_map.124), channel_id=1, replica_groups=mesh['x'=4,'z'=8,'core'=2,'y'=8] {'core','y'}, dimensions={0} | all-to-all | bytes 131072 | tf_op jit(solution)/shard_map/all_to_all | solution.py:339
  132.0 0.0 collective-permute-done.5.other_ref
  132.0 2.0 %shard_map.125 = (bf16[64,12288]{1,0:T(8,128)(2,1)}, bf16[64,192]{1,0:T(8,128)(2,1)}, f32[1]{0:T(128)}, f32[1]{0:T(128)}, f32[1]{0:T(128)}) custom-call(s32[1]{0:T(128)} %bitcast.place_ref, f32[16,8,128]{2,1,0:T(8,128)S(1)} %all_to_all.23.tops_ref, bf16[4,784,128]{2,1,0:T(8,128)(2,1)S(1)} %bitcast.8, ...), custom_call_target="tpu_custom_call" | custom-call | tf_op jit(solution)/shard_map/pallas_call | solution.py:342
  (4 shorter events, 0.1 us)
Async XLA Ops:
  18.4 15.6 %collective-permute-start = (bf16[2,64,1024]{2,1,0:T(8,128)(2,1)S(1)}, bf16[2,64,1024]{2,1,0:T(8,128)(2,1)S(1)}, u32[]{:S(2)}, u32[]{:S(2)}) collective-permute-start(bf16[2,64,1024]{2,1,0:T(8,128)(2,1)S(1)} %bitcast.11), channel_id=1, source_target_pairs={{0,7},{1,0},{2,1},{3,2},{4,3},{5,4},{6,5},{7,6},{8,15},{9,8},{10,9... | collective-permute-start | bytes 786440 | tf_op jit(solution)/shard_map/ppermute | solution.py:254
  20.3 13.7 %collective-permute-start.1 = (bf16[2,64,1024]{2,1,0:T(8,128)(2,1)S(1)}, bf16[2,64,1024]{2,1,0:T(8,128)(2,1)S(1)}, u32[]{:S(2)}, u32[]{:S(2)}) collective-permute-start(bf16[2,64,1024]{2,1,0:T(8,128)(2,1)S(1)} %bitcast.10), channel_id=1, source_target_pairs={{0,1},{1,2},{2,3},{3,4},{4,5},{5,6},{6,7},{7,0},{8,9},{9,10},{10,1... | collective-permute-start | bytes 786440 | tf_op jit(solution)/shard_map/ppermute | solution.py:255
  23.7 1.9 %copy-start = (bf16[1024,1536]{1,0:T(8,128)(2,1)S(1)}, bf16[1024,1536]{1,0:T(8,128)(2,1)}, u32[]{:S(2)}) copy-start(bf16[1024,1536]{1,0:T(8,128)(2,1)} %activations_ref.5) | copy-start | bytes 9437188
  25.6 8.4 %copy-start.1 = (bf16[1024,1536]{1,0:T(8,128)(2,1)S(1)}, bf16[1024,1536]{1,0:T(8,128)(2,1)}, u32[]{:S(2)}) copy-start(bf16[1024,1536]{1,0:T(8,128)(2,1)} %activations_ref.5) | copy-start | bytes 9437188
  26.6 11.2 %collective-permute-start.2 = (f32[2,64,1536]{2,1,0:T(8,128)S(1)}, f32[2,64,1536]{2,1,0:T(8,128)S(1)}, u32[]{:S(2)}, u32[]{:S(2)}) collective-permute-start(f32[2,64,1536]{2,1,0:T(8,128)S(1)} %get-tuple-element.31), channel_id=1, source_target_pairs={{0,8},{8,0},{1,9},{9,1},{2,10},{10,2},{3,11},{11,3},{4,12},{12,4},... | collective-permute-start | bytes 2359304 | tf_op jit(solution)/shard_map/ppermute | solution.py:283
  34.6 4.5 %collective-permute-start.3 = (f32[2,64,1536]{2,1,0:T(8,128)S(1)}, f32[2,64,1536]{2,1,0:T(8,128)S(1)}, u32[]{:S(2)}, u32[]{:S(2)}) collective-permute-start(f32[2,64,1536]{2,1,0:T(8,128)S(1)} %get-tuple-element.32), channel_id=1, source_target_pairs={{0,8},{8,0},{1,9},{9,1},{2,10},{10,2},{3,11},{11,3},{4,12},{12,4},... | collective-permute-start | bytes 2359304 | tf_op jit(solution)/shard_map/ppermute | solution.py:284
  39.1 45.6 %copy-start.2 = (f32[64,192]{1,0:T(8,128)S(1)}, f32[64,192]{1,0:T(8,128)}, u32[]{:S(2)}) copy-start(f32[64,192]{1,0:T(8,128)} %master_ref.1) | copy-start | bytes 147460
  39.1 45.6 %copy-start.3 = (f32[64,192]{1,0:T(8,128)S(1)}, f32[64,192]{1,0:T(8,128)}, u32[]{:S(2)}) copy-start(f32[64,192]{1,0:T(8,128)} %second_ref.1) | copy-start | bytes 147460
  39.1 45.6 %copy-start.4 = (bf16[64,192]{1,0:T(8,128)(2,1)S(1)}, bf16[64,192]{1,0:T(8,128)(2,1)}, u32[]{:S(2)}) copy-start(bf16[64,192]{1,0:T(8,128)(2,1)} %moment_ref.1) | copy-start | bytes 73732
  75.4 9.2 %collective-permute-start.4 = (f32[96,128]{1,0:T(8,128)S(1)}, f32[96,128]{1,0:T(8,128)S(1)}, u32[]{:S(2)}, u32[]{:S(2)}) collective-permute-start(f32[96,128]{1,0:T(8,128)S(1)} %reduce_sum.9), channel_id=1, source_target_pairs={{0,4},{112,12},{16,20},{96,28},{32,36},{80,44},{48,52},{64,60},{65... | collective-permute-start | bytes 147464 | tf_op jit(solution)/shard_map/ppermute | solution.py:311
  114.7 17.3 %collective-permute-start.5 = (bf16[4,784,128]{2,1,0:T(8,128)(2,1)S(1)}, bf16[4,784,128]{2,1,0:T(8,128)(2,1)S(1)}, u32[]{:S(2)}, u32[]{:S(2)}) collective-permute-start(bf16[4,784,128]{2,1,0:T(8,128)(2,1)S(1)} %bitcast.6), channel_id=1, source_target_pairs={{0,8},{8,0},{1,9},{9,1},{2,10},{10,2},{3,11},{11,3},{4,12},{12,4},... | collective-permute-start | bytes 2408456 | tf_op jit(solution)/shard_map/ppermute | solution.py:331

commit v12 on v11

--- a/solution.py
+++ b/solution.py
@@ -83,7 +83,7 @@
 
 
 def slot_of(feature, y):
-    near = feature // 2 if feature % 2 == 0 else 7 - feature // 2
+    near = feature // 2 if feature % 2 == 0 else 4 + (feature // 2 + 2) % 4
     return (near + 4 * (y % 2)) % 8
 
 

time: 135 us -> 135 us (level)
  no operation moved by 1% of the time
where the time goes in v12:
time: 135 us
  blocking collectives  96.5 us (71%)
  starting transfers between devices  27.2 us (20%)
  Pallas kernels  5.43 us (4%)
  waiting for transfers between devices  2.46 us (2%)
  local copies, waits for them, and re-layouts  1.93 us (1%)
  between operations  1.43 us (1%)
    all_to_all x1, blocking collectives, on_device(): value = lax.all_to_all(value, 'z', 0, 0, tiled=True)  21.6 us
    all_gather x1, blocking collectives, on_device(): even = lax.all_gather(output_grads.T, 'y', axis_index_groups=every_second)  17.7 us
    all_to_all x1, blocking collectives, on_device(): held = lax.all_to_all(held, 'z', 0, 0, tiled=True)  16.1 us
    all_to_all x1, blocking collectives, on_device(): tops = lax.all_to_all(tops, ('core', 'y'), 0, 0, tiled=True)  14.4 us
    all_to_all x1, blocking collectives, on_device(): value = lax.all_to_all(value, 'x', 0, 0, tiled=True)  14.4 us
    all_gather x1, blocking collectives, on_device(): held = lax.all_gather(held, 'x')  12.2 us
    ppermute x1, starting transfers between devices, on_device(): value = lax.ppermute(value, DEVICE, route)  8.09 us
    ppermute x1, starting transfers between devices, on_device(): other_even = lax.ppermute(to_other_even, 'core', swap)  7.36 us
  transfers between devices with their start and end apart: 6, of which 2 were waited for; matrix products, arithmetic and copies ran while one was open for 0% of the time, Pallas kernels for 2%

profile of v12, /device:TPU:1, one launch (start us, length us, event | category | flops | bytes accessed | tf_op | source)
XLA Modules:
  0.0 135.0 jit_solution(12447199399848083668)
XLA Ops:
  0.6 17.7 %all-gather = bf16[256,1024]{1,0:T(8,128)(2,1)S(1)} all-gather(bf16[64,1024]{1,0:T(8,128)(2,1)} %bitcast.12), channel_id=2, replica_groups={{0,2,4,6},{1,3,5,7},{8,10,12,14},{9,11,13,15},{16,18,20,22},{17,19,21,2..., dimensions={0}, use_global_device_ids=true | all-gather | bytes 655360 | tf_op jit(solution)/shard_map/all_gather | solution.py:253
  18.4 1.9 %collective-permute-start = (bf16[2,64,1024]{2,1,0:T(8,128)(2,1)S(1)}, bf16[2,64,1024]{2,1,0:T(8,128)(2,1)S(1)}, u32[]{:S(2)}, u32[]{:S(2)}) collective-permute-start(bf16[2,64,1024]{2,1,0:T(8,128)(2,1)S(1)} %bitcast.11), channel_id=1, source_target_pairs={{0,7},{1,0},{2,1},{3,2},{4,3},{5,4},{6,5},{7,6},{8,15},{9,8},{10,9... | collective-permute-start | bytes 786440 | tf_op jit(solution)/shard_map/ppermute | solution.py:254
  20.3 3.4 %collective-permute-start.1 = (bf16[2,64,1024]{2,1,0:T(8,128)(2,1)S(1)}, bf16[2,64,1024]{2,1,0:T(8,128)(2,1)S(1)}, u32[]{:S(2)}, u32[]{:S(2)}) collective-permute-start(bf16[2,64,1024]{2,1,0:T(8,128)(2,1)S(1)} %bitcast.10), channel_id=1, source_target_pairs={{0,1},{1,2},{2,3},{3,4},{4,5},{5,6},{6,7},{7,0},{8,9},{9,10},{10,1... | collective-permute-start | bytes 786440 | tf_op jit(solution)/shard_map/ppermute | solution.py:255
  23.7 0.0 copy-start
  23.7 1.9 %copy-done = bf16[1024,1536]{1,0:T(8,128)(2,1)S(1)} copy-done((bf16[1024,1536]{1,0:T(8,128)(2,1)S(1)}, bf16[1024,1536]{1,0:T(8,128)(2,1)}, u32[]{:S(2)}) %copy-start) | copy-done | bytes 3145752
  25.6 0.0 copy-start.1
  25.6 1.0 shard_map.117
  26.6 7.4 %collective-permute-start.2 = (f32[2,64,1536]{2,1,0:T(8,128)S(1)}, f32[2,64,1536]{2,1,0:T(8,128)S(1)}, u32[]{:S(2)}, u32[]{:S(2)}) collective-permute-start(f32[2,64,1536]{2,1,0:T(8,128)S(1)} %get-tuple-element.31), channel_id=1, source_target_pairs={{0,8},{8,0},{1,9},{9,1},{2,10},{10,2},{3,11},{11,3},{4,12},{12,4},... | collective-permute-start | bytes 2359304 | tf_op jit(solution)/shard_map/ppermute | solution.py:283
  34.0 0.0 collective-permute-done.low_ref
  34.0 0.0 collective-permute-done.1.high_ref
  34.0 0.0 copy-done.1
  34.0 0.6 shard_map.118
  34.6 2.6 %collective-permute-start.3 = (f32[2,64,1536]{2,1,0:T(8,128)S(1)}, f32[2,64,1536]{2,1,0:T(8,128)S(1)}, u32[]{:S(2)}, u32[]{:S(2)}) collective-permute-start(f32[2,64,1536]{2,1,0:T(8,128)S(1)} %get-tuple-element.32), channel_id=1, source_target_pairs={{0,8},{8,0},{1,9},{9,1},{2,10},{10,2},{3,11},{11,3},{4,12},{12,4},... | collective-permute-start | bytes 2359304 | tf_op jit(solution)/shard_map/ppermute | solution.py:284
  37.2 0.6 shard_map.119
  37.8 0.0 collective-permute-done.2.other_even_ref
  37.8 1.3 collective-permute-done.3.other_odd_ref
  39.1 0.0 copy-start.2
  39.1 0.0 copy-start.3
  39.1 0.0 copy-start.4
  39.1 0.1 shard_map.120
  39.3 14.4 %all_to_all.20.parts_ref = bf16[4,64,1536]{2,1,0:T(8,128)(2,1)S(1)} all-to-all(bf16[4,64,1536]{2,1,0:T(8,128)(2,1)S(1)} %shard_map.120), channel_id=1, replica_groups=mesh['x'=4,'z'=8,'core'=2,'y'=8] {'x'}, dimensions={0} | all-to-all | bytes 1572864 | tf_op jit(solution)/shard_map/all_to_all | solution.py:292
  53.7 0.1 shard_map.121
  53.8 21.6 %all_to_all.21 = f32[8,96,128]{2,1,0:T(8,128)S(1)} all-to-all(f32[8,96,128]{2,1,0:T(8,128)S(1)} %shard_map.121), channel_id=1, replica_groups=mesh['x'=4,'z'=8,'core'=2,'y'=8] {'z'}, dimensions={0} | all-to-all | bytes 786432 | tf_op jit(solution)/shard_map/all_to_all | solution.py:300
  75.4 8.1 %collective-permute-start.4 = (f32[96,128]{1,0:T(8,128)S(1)}, f32[96,128]{1,0:T(8,128)S(1)}, u32[]{:S(2)}, u32[]{:S(2)}) collective-permute-start(f32[96,128]{1,0:T(8,128)S(1)} %reduce_sum.9), channel_id=1, source_target_pairs={{0,4},{96,12},{16,20},{112,28},{32,36},{64,44},{48,52},{80,60},{65... | collective-permute-start | bytes 147464 | tf_op jit(solution)/shard_map/ppermute | solution.py:311
  84.2 1.2 collective-permute-done.4.summed_ref
  85.3 0.0 copy-done.2
  85.3 0.0 copy-done.3
  85.3 0.0 copy-done.4
  85.3 0.8 shard_map.122
  86.2 16.1 %all_to_all.22.held_ref = bf16[8,112,128]{2,1,0:T(8,128)(2,1)S(1)} all-to-all(bf16[8,112,128]{2,1,0:T(8,128)(2,1)S(1)} %get-tuple-element.35), channel_id=1, replica_groups=mesh['x'=4,'z'=8,'core'=2,'y'=8] {'z'}, dimensions={0} | all-to-all | bytes 458752 | tf_op jit(solution)/shard_map/all_to_all | solution.py:322
  102.4 12.2 %all-gather.1 = bf16[3136,128]{1,0:T(8,128)(2,1)S(1)} all-gather(bf16[784,128]{1,0:T(8,128)(2,1)S(1)} %shard_map.123), channel_id=3, replica_groups=mesh['x'=4,'z'=8,'core'=2,'y'=8] {'x'}, dimensions={0}, use_global_device_ids=true | all-gather | bytes 1003520 | tf_op jit(solution)/shard_map/all_gather | solution.py:330
  114.6 3.9 %collective-permute-start.5 = (bf16[4,784,128]{2,1,0:T(8,128)(2,1)S(1)}, bf16[4,784,128]{2,1,0:T(8,128)(2,1)S(1)}, u32[]{:S(2)}, u32[]{:S(2)}) collective-permute-start(bf16[4,784,128]{2,1,0:T(8,128)(2,1)S(1)} %bitcast.6), channel_id=1, source_target_pairs={{0,8},{8,0},{1,9},{9,1},{2,10},{10,2},{3,11},{11,3},{4,12},{12,4},... | collective-permute-start | bytes 2408456 | tf_op jit(solution)/shard_map/ppermute | solution.py:331
  118.5 14.4 %all_to_all.23.tops_ref = f32[16,8,128]{2,1,0:T(8,128)S(1)} all-to-all(f32[16,8,128]{2,1,0:T(8,128)S(1)} %shard_map.124), channel_id=1, replica_groups=mesh['x'=4,'z'=8,'core'=2,'y'=8] {'core','y'}, dimensions={0} | all-to-all | bytes 131072 | tf_op jit(solution)/shard_map/all_to_all | solution.py:339
  132.9 0.0 collective-permute-done.5.other_ref
  133.0 2.0 %shard_map.125 = (bf16[64,12288]{1,0:T(8,128)(2,1)}, bf16[64,192]{1,0:T(8,128)(2,1)}, f32[1]{0:T(128)}, f32[1]{0:T(128)}, f32[1]{0:T(128)}) custom-call(s32[1]{0:T(128)} %bitcast.place_ref, f32[16,8,128]{2,1,0:T(8,128)S(1)} %all_to_all.23.tops_ref, bf16[4,784,128]{2,1,0:T(8,128)(2,1)S(1)} %bitcast.8, ...), custom_call_target="tpu_custom_call" | custom-call | tf_op jit(solution)/shard_map/pallas_call | solution.py:342
  (4 shorter events, 0.1 us)
Async XLA Ops:
  18.4 15.6 %collective-permute-start = (bf16[2,64,1024]{2,1,0:T(8,128)(2,1)S(1)}, bf16[2,64,1024]{2,1,0:T(8,128)(2,1)S(1)}, u32[]{:S(2)}, u32[]{:S(2)}) collective-permute-start(bf16[2,64,1024]{2,1,0:T(8,128)(2,1)S(1)} %bitcast.11), channel_id=1, source_target_pairs={{0,7},{1,0},{2,1},{3,2},{4,3},{5,4},{6,5},{7,6},{8,15},{9,8},{10,9... | collective-permute-start | bytes 786440 | tf_op jit(solution)/shard_map/ppermute | solution.py:254
  20.3 13.7 %collective-permute-start.1 = (bf16[2,64,1024]{2,1,0:T(8,128)(2,1)S(1)}, bf16[2,64,1024]{2,1,0:T(8,128)(2,1)S(1)}, u32[]{:S(2)}, u32[]{:S(2)}) collective-permute-start(bf16[2,64,1024]{2,1,0:T(8,128)(2,1)S(1)} %bitcast.10), channel_id=1, source_target_pairs={{0,1},{1,2},{2,3},{3,4},{4,5},{5,6},{6,7},{7,0},{8,9},{9,10},{10,1... | collective-permute-start | bytes 786440 | tf_op jit(solution)/shard_map/ppermute | solution.py:255
  23.7 1.9 %copy-start = (bf16[1024,1536]{1,0:T(8,128)(2,1)S(1)}, bf16[1024,1536]{1,0:T(8,128)(2,1)}, u32[]{:S(2)}) copy-start(bf16[1024,1536]{1,0:T(8,128)(2,1)} %activations_ref.5) | copy-start | bytes 9437188
  25.6 8.4 %copy-start.1 = (bf16[1024,1536]{1,0:T(8,128)(2,1)S(1)}, bf16[1024,1536]{1,0:T(8,128)(2,1)}, u32[]{:S(2)}) copy-start(bf16[1024,1536]{1,0:T(8,128)(2,1)} %activations_ref.5) | copy-start | bytes 9437188
  26.6 11.2 %collective-permute-start.2 = (f32[2,64,1536]{2,1,0:T(8,128)S(1)}, f32[2,64,1536]{2,1,0:T(8,128)S(1)}, u32[]{:S(2)}, u32[]{:S(2)}) collective-permute-start(f32[2,64,1536]{2,1,0:T(8,128)S(1)} %get-tuple-element.31), channel_id=1, source_target_pairs={{0,8},{8,0},{1,9},{9,1},{2,10},{10,2},{3,11},{11,3},{4,12},{12,4},... | collective-permute-start | bytes 2359304 | tf_op jit(solution)/shard_map/ppermute | solution.py:283
  34.6 4.5 %collective-permute-start.3 = (f32[2,64,1536]{2,1,0:T(8,128)S(1)}, f32[2,64,1536]{2,1,0:T(8,128)S(1)}, u32[]{:S(2)}, u32[]{:S(2)}) collective-permute-start(f32[2,64,1536]{2,1,0:T(8,128)S(1)} %get-tuple-element.32), channel_id=1, source_target_pairs={{0,8},{8,0},{1,9},{9,1},{2,10},{10,2},{3,11},{11,3},{4,12},{12,4},... | collective-permute-start | bytes 2359304 | tf_op jit(solution)/shard_map/ppermute | solution.py:284
  39.1 46.2 %copy-start.2 = (f32[64,192]{1,0:T(8,128)S(1)}, f32[64,192]{1,0:T(8,128)}, u32[]{:S(2)}) copy-start(f32[64,192]{1,0:T(8,128)} %master_ref.1) | copy-start | bytes 147460
  39.1 46.2 %copy-start.3 = (f32[64,192]{1,0:T(8,128)S(1)}, f32[64,192]{1,0:T(8,128)}, u32[]{:S(2)}) copy-start(f32[64,192]{1,0:T(8,128)} %second_ref.1) | copy-start | bytes 147460
  39.1 46.2 %copy-start.4 = (bf16[64,192]{1,0:T(8,128)(2,1)S(1)}, bf16[64,192]{1,0:T(8,128)(2,1)}, u32[]{:S(2)}) copy-start(bf16[64,192]{1,0:T(8,128)(2,1)} %moment_ref.1) | copy-start | bytes 73732
  75.4 9.9 %collective-permute-start.4 = (f32[96,128]{1,0:T(8,128)S(1)}, f32[96,128]{1,0:T(8,128)S(1)}, u32[]{:S(2)}, u32[]{:S(2)}) collective-permute-start(f32[96,128]{1,0:T(8,128)S(1)} %reduce_sum.9), channel_id=1, source_target_pairs={{0,4},{96,12},{16,20},{112,28},{32,36},{64,44},{48,52},{80,60},{65... | collective-permute-start | bytes 147464 | tf_op jit(solution)/shard_map/ppermute | solution.py:311
  114.6 18.4 %collective-permute-start.5 = (bf16[4,784,128]{2,1,0:T(8,128)(2,1)S(1)}, bf16[4,784,128]{2,1,0:T(8,128)(2,1)S(1)}, u32[]{:S(2)}, u32[]{:S(2)}) collective-permute-start(bf16[4,784,128]{2,1,0:T(8,128)(2,1)S(1)} %bitcast.6), channel_id=1, source_target_pairs={{0,8},{8,0},{1,9},{9,1},{2,10},{10,2},{3,11},{11,3},{4,12},{12,4},... | collective-permute-start | bytes 2408456 | tf_op jit(solution)/shard_map/ppermute | solution.py:331
